TPU v7x, 32 devices: a whole 2x2x4 slice. The times are simulated.
32 devices in a mesh: rep: 4 (over y, x), fsdp: 8 (over z, core).
Axes of the slice: x: 2, y: 2, z: 4, core: 2. Of those that a mesh axis runs over, the one named last changes fastest.
Arguments:
- tokens: bfloat16 [10240, 2048], P(('rep', 'fsdp')), may hold values from -6 to 6
- lengths: int32 [4, 2], P('rep'), may hold values from 1024 to 1536, as said below
- dealing: int32 [10240], P('rep'), may hold values from 0 to 2559, as said below
- routes: int32 [10240, 4], P('rep'), may hold values from 0 to 7, all different within a row; in each aligned block of 320 rows (0 to 319, 320 to 639, ...) at most 192 rows name the same one
- cotangent: bfloat16 [10240, 2048], P(('rep', 'fsdp')), may hold values from -6 to 6
- first_gain: bfloat16 [2048], P('fsdp'), may hold values from 0.5 to 1.5
- projection: bfloat16 [2048, 6144], P('fsdp'), may hold values from -0.125 to 0.125
- projection_bias: bfloat16 [6144], P('fsdp'), may hold values from -0.59765625 to 0.59765625
- output_weight: bfloat16 [2048, 2048], P('fsdp'), may hold values from -1.25 to 1.25
- second_gain: bfloat16 [2048], P('fsdp'), may hold values from 0.5 to 1.5
- router_weight: bfloat16 [2048, 8], P('fsdp'), may hold values from -0.0625 to 0.0625
- shared_gate: bfloat16 [2048], P('fsdp'), may hold values from -0.125 to 0.125
- shared_in: bfloat16 [2, 2048, 5632], P(None, None, 'fsdp'), may hold values from -0.125 to 0.125
- shared_out: bfloat16 [5632, 2048], P('fsdp'), may hold values from -0.15625 to 0.15625
- expert_in: bfloat16 [8, 2, 2048, 1408], P(None, None, None, 'fsdp'), may hold values from -0.125 to 0.125
- expert_out: bfloat16 [8, 1408, 2048], P(None, 'fsdp'), may hold values from -0.4375 to 0.4375
Outputs:
- mixed: bfloat16 [10240, 2048], P(('rep', 'fsdp'))
- tokens_grad: float32 [10240, 2048], P(('rep', 'fsdp'))
- first_gain_grad: float32 [2048], P('fsdp')
- projection_grad: float32 [2048, 6144], P('fsdp')
- projection_bias_grad: float32 [6144], P('fsdp')
- output_weight_grad: float32 [2048, 2048], P('fsdp')
- second_gain_grad: float32 [2048], P('fsdp')
- router_weight_grad: float32 [2048, 8], P('fsdp')
- shared_gate_grad: float32 [2048], P('fsdp')
- shared_in_grad: float32 [2, 2048, 5632], P(None, None, 'fsdp')
- shared_out_grad: float32 [5632, 2048], P('fsdp')
- expert_in_grad: float32 [8, 2, 2048, 1408], P(None, None, None, 'fsdp')
- expert_out_grad: float32 [8, 1408, 2048], P(None, 'fsdp')
Inputs may be any that keep to these rules, and one draw needn't show every extreme that they name: A group's two lengths add up to 2560; the first group's first sequence has exactly 1024 tokens. `dealing`: within a group's 2560 rows every value stands once; the k-th of a device's 320 rows holds a value from 8 * k to 8 * k + 7. `routes`: A row names 4 different experts; in each aligned block of 320 rows (one device's rows) no expert is named by more than 192 rows, and in some blocks one is named by exactly 192.
All inputs are finite; a program needn't handle non-finite values.
Results may differ from a plain program's by a relative error of at most 0.018.
Values may be sent and summed in bfloat16 or wider, within the bound.
A program may use at most 576 MiB of HBM per device.

v0:
```python
from functools import partial

import jax
import jax.numpy as jnp
from jax import lax
from jax.sharding import PartitionSpec as P

HEAD_DIM = 128


EPS = 1e-06
THETA = 1000000.0
NEG = -1e30
HIGHEST_PRECISION = lax.Precision.HIGHEST


def rms(values, gain):
    return values * lax.rsqrt(jnp.mean(values * values, axis=-1, keepdims=True) + EPS) * gain


def rope_tables(position, size):
    half = size // 2
    freq = THETA ** (-(jnp.arange(half, dtype=jnp.float32) * (2.0 / size)))
    angle = position.astype(jnp.float32)[:, None] * freq[None, :]
    return (jnp.cos(angle), jnp.sin(angle))


def rotate(values, cosine, sine):
    half = values.shape[-1] // 2
    first = values[..., :half]
    second = values[..., half:]
    cos_part = cosine[:, None, :]
    sin_part = sine[:, None, :]
    return jnp.concatenate(
        [first * cos_part - second * sin_part, second * cos_part + first * sin_part], axis=-1
    )


def gated(gate_values, up_values):
    return jax.nn.silu(gate_values) * up_values


def expert_slots(routes, experts, capacity):
    pairs = routes.reshape(-1)
    total = pairs.shape[0]
    member = (pairs[:, None] == jnp.arange(experts, dtype=jnp.int32)[None, :]).astype(jnp.int32)
    before = jnp.cumsum(member, axis=0) - member
    within = jnp.sum(before * member, axis=1)
    slot = pairs * capacity + within
    source = (
        jnp.full((experts * capacity,), total, jnp.int32)
        .at[slot]
        .set(jnp.arange(total, dtype=jnp.int32))
    )
    return (slot, source)


def take_rows(block, index):
    return jnp.take(block, index, axis=0)


def contract_rows(left, right):
    return lax.dot_general(
        left, right, (((0,), (0,)), ((), ())), preferred_element_type=jnp.float32
    )


def contract_columns(left, right):
    return lax.dot_general(
        left, right, (((1,), (1,)), ((), ())), preferred_element_type=jnp.float32
    )


def shards(
    tokens,
    lengths,
    dealing,
    routes,
    cotangent,
    first_gain,
    projection,
    projection_bias,
    output_weight,
    second_gain,
    router_weight,
    shared_gate,
    shared_in,
    shared_out,
    expert_in,
    expert_out,
):
    width = tokens.shape[1]
    local_rows = tokens.shape[0]
    group_rows = dealing.shape[0]
    devices = group_rows // local_rows
    heads = width // HEAD_DIM
    picks = routes.shape[1]
    experts = expert_in.shape[0]
    capacity = local_rows * picks * 6 // (5 * experts)
    scale = HEAD_DIM ** (-0.5)
    place = lax.axis_index("fsdp")
    offset = place * local_rows
    stream_mine = lax.dynamic_slice_in_dim(dealing, offset, local_rows)
    routes_mine = lax.dynamic_slice_in_dim(routes, offset, local_rows, 0)
    first_length = lengths[0, 0]
    second_all = (dealing >= first_length).astype(jnp.int32)
    second_mine = (stream_mine >= first_length).astype(jnp.int32)
    visible = (second_mine[:, None] == second_all[None, :]) & (
        dealing[None, :] <= stream_mine[:, None]
    )
    cosine, sine = rope_tables(stream_mine - second_mine * first_length, HEAD_DIM)
    weight_projection, weight_output, weight_router, gain_one, bias_full, gain_two, weight_gate = (
        lax.all_gather(projection, "fsdp", axis=0, tiled=True),
        lax.all_gather(output_weight, "fsdp", axis=0, tiled=True),
        lax.all_gather(router_weight, "fsdp", axis=0, tiled=True),
        lax.all_gather(first_gain, "fsdp", axis=0, tiled=True),
        lax.all_gather(projection_bias, "fsdp", axis=0, tiled=True),
        lax.all_gather(second_gain, "fsdp", axis=0, tiled=True),
        lax.all_gather(shared_gate, "fsdp", axis=0, tiled=True),
    )
    gain_one = gain_one.astype(jnp.float32)
    gain_two = gain_two.astype(jnp.float32)
    router_float = weight_router.astype(jnp.float32)
    gate_float = weight_gate.astype(jnp.float32)
    inputs = tokens.astype(jnp.float32)
    normed_one, norm_one_back = jax.vjp(rms, inputs, gain_one)
    hidden_one = normed_one.astype(jnp.bfloat16)
    projected = jnp.dot(
        hidden_one, weight_projection, preferred_element_type=jnp.float32
    ) + bias_full.astype(jnp.float32)
    query = projected[:, :width].reshape(local_rows, heads, HEAD_DIM)
    keyed = projected[:, width : 2 * width].reshape(local_rows, heads, HEAD_DIM)

    def turn(first, second):
        return (rotate(first, cosine, sine), rotate(second, cosine, sine))

    (query_turned, key_turned), turn_back = jax.vjp(turn, query, keyed)
    query_low = query_turned.astype(jnp.bfloat16)
    key_low = key_turned.reshape(local_rows, width).astype(jnp.bfloat16)
    value_low = projected[:, 2 * width :].astype(jnp.bfloat16)
    key_all, value_all = (
        lax.all_gather(key_low, "fsdp", axis=0, tiled=True),
        lax.all_gather(value_low, "fsdp", axis=0, tiled=True),
    )
    key_all = key_all.reshape(group_rows, heads, HEAD_DIM)
    value_all = value_all.reshape(group_rows, heads, HEAD_DIM)

    def scores_now():
        raw = (
            jnp.einsum("qhd,khd->hqk", query_low, key_all, preferred_element_type=jnp.float32)
            * scale
        )
        return jnp.where(visible[None], raw, NEG)

    scores = scores_now()
    peak = jnp.max(scores, axis=-1, keepdims=True)
    shifted = jnp.exp(scores - peak)
    total = jnp.sum(shifted, axis=-1, keepdims=True)
    log_total = peak + jnp.log(total)
    attended = jnp.einsum(
        "hqk,khd->qhd",
        (shifted / total).astype(jnp.bfloat16),
        value_all,
        preferred_element_type=jnp.float32,
    )
    attended_low = attended.reshape(local_rows, width).astype(jnp.bfloat16)
    residual = inputs + jnp.dot(attended_low, weight_output, preferred_element_type=jnp.float32)
    normed_two, norm_two_back = jax.vjp(rms, residual, gain_two)
    hidden_two = normed_two.astype(jnp.bfloat16)

    def route(hidden, chosen_routes):
        chosen = (
            chosen_routes[:, :, None] == jnp.arange(experts, dtype=jnp.int32)[None, None, :]
        ).astype(jnp.float32)

        def gating(logits):
            lifted = jnp.exp(logits - jnp.max(logits, axis=-1, keepdims=True))
            normal = lifted / jnp.sum(lifted, axis=-1, keepdims=True)
            return jnp.sum(normal[:, None, :] * chosen, axis=-1)

        return jax.vjp(gating, jnp.dot(hidden, weight_router, preferred_element_type=jnp.float32))

    gates_mine, gate_back = route(hidden_two, routes_mine)
    hidden_all = lax.all_gather(hidden_two, "fsdp", axis=0, tiled=True)
    gate_input = jnp.dot(hidden_all, weight_gate, preferred_element_type=jnp.float32)
    sigma_all = jax.nn.sigmoid(gate_input)
    sigma_mine, sigma_back = jax.vjp(
        jax.nn.sigmoid, lax.dynamic_slice_in_dim(gate_input, offset, local_rows)
    )
    shared_mix = jnp.einsum(
        "nd,cdf->ncf", hidden_all, shared_in, preferred_element_type=jnp.float32
    )
    shared_act = gated(shared_mix[:, 0], shared_mix[:, 1]).astype(jnp.bfloat16)
    slot_all, source_all = jax.vmap(partial(expert_slots, experts=experts, capacity=capacity))(
        routes.reshape(devices, local_rows, picks)
    )
    gates_all, _ = route(hidden_all, routes)
    valid = source_all < local_rows * picks
    token_block = source_all // picks
    padded = jnp.concatenate(
        [
            hidden_all.reshape(devices, local_rows, width),
            jnp.zeros((devices, 1, width), jnp.bfloat16),
        ],
        axis=1,
    )
    expert_rows = jax.vmap(take_rows)(padded, token_block)
    expert_rows = (
        expert_rows.reshape(devices, experts, capacity, width)
        .transpose(1, 0, 2, 3)
        .reshape(experts, devices * capacity, width)
    )
    gate_pairs = jnp.concatenate(
        [gates_all.reshape(devices, local_rows * picks), jnp.zeros((devices, 1), jnp.float32)],
        axis=1,
    )
    slot_gate = jax.vmap(take_rows)(gate_pairs, source_all)
    slot_gate = (
        slot_gate.reshape(devices, experts, capacity)
        .transpose(1, 0, 2)
        .reshape(experts, devices * capacity)
    )
    slot_token = jnp.where(
        valid, token_block + local_rows * jnp.arange(devices, dtype=jnp.int32)[:, None], 0
    )
    slot_token = (
        slot_token.reshape(devices, experts, capacity)
        .transpose(1, 0, 2)
        .reshape(experts, devices * capacity)
    )

    def expert_part(accumulated, inputs_now):
        weight_in, weight_down, rows_in, gate_of, token_at = inputs_now
        mixture = jnp.einsum("rd,cdf->rcf", rows_in, weight_in, preferred_element_type=jnp.float32)
        activation = gated(mixture[:, 0], mixture[:, 1]).astype(jnp.bfloat16)
        output = jnp.dot(activation, weight_down, preferred_element_type=jnp.float32)
        return (accumulated.at[token_at].add(gate_of[:, None] * output), None)

    routed_all, _ = lax.scan(
        expert_part,
        jnp.zeros((group_rows, width), jnp.float32),
        (expert_in, expert_out, expert_rows, slot_gate, slot_token),
    )
    summed = lax.psum_scatter(
        sigma_all[:, None] * jnp.dot(shared_act, shared_out, preferred_element_type=jnp.float32)
        + routed_all,
        "fsdp",
        scatter_dimension=0,
        tiled=True,
    )
    mixed = (residual + summed).astype(jnp.bfloat16)
    grad_mine = cotangent.astype(jnp.float32)
    grad_all = lax.all_gather(cotangent, "fsdp", axis=0, tiled=True).astype(jnp.float32)
    shared_grad_low = (sigma_all[:, None] * grad_all).astype(jnp.bfloat16)
    _, shared_act_back = jax.vjp(gated, shared_mix[:, 0], shared_mix[:, 1])
    shared_gate_grad, shared_up_grad = shared_act_back(
        contract_columns(shared_grad_low, shared_out)
    )
    shared_mix_grad = jnp.stack([shared_gate_grad, shared_up_grad], axis=1).astype(jnp.bfloat16)
    shared_in_grad = jnp.einsum(
        "nd,ncf->cdf", hidden_all, shared_mix_grad, preferred_element_type=jnp.float32
    )
    shared_out_grad = contract_rows(shared_act, shared_grad_low)

    def expert_back_part(accumulated, inputs_now):
        weight_in, weight_down, rows_in, gate_of, token_at = inputs_now
        mixture = jnp.einsum("rd,cdf->rcf", rows_in, weight_in, preferred_element_type=jnp.float32)
        act_float, act_back = jax.vjp(gated, mixture[:, 0], mixture[:, 1])
        activation = act_float.astype(jnp.bfloat16)
        output = jnp.dot(activation, weight_down, preferred_element_type=jnp.float32)
        upstream = jnp.take(grad_all, token_at, axis=0)
        slot_grad = (gate_of[:, None] * upstream).astype(jnp.bfloat16)
        gate_part = jnp.sum(upstream * output, axis=-1)
        gate_grad, up_grad = act_back(contract_columns(slot_grad, weight_down))
        mixture_grad = jnp.stack([gate_grad, up_grad], axis=1).astype(jnp.bfloat16)
        row_grad = jnp.einsum(
            "rcf,cdf->rd", mixture_grad, weight_in, preferred_element_type=jnp.float32
        )
        in_grad = jnp.einsum(
            "rd,rcf->cdf", rows_in, mixture_grad, preferred_element_type=jnp.float32
        )
        down_grad = contract_rows(activation, slot_grad)
        return (accumulated.at[token_at].add(row_grad), (gate_part, in_grad, down_grad))

    hidden_sum, (gate_parts, expert_in_grad, expert_out_grad) = lax.scan(
        expert_back_part,
        jnp.zeros((group_rows, width), jnp.float32),
        (expert_in, expert_out, expert_rows, slot_gate, slot_token),
    )
    gate_slots = (
        gate_parts.reshape(experts, devices, capacity)
        .transpose(1, 0, 2)
        .reshape(devices, experts * capacity)
    )
    gate_pair_grad = jax.vmap(take_rows)(gate_slots, slot_all).reshape(group_rows, picks)
    sigma_part = jnp.sum(
        grad_all * jnp.dot(shared_act, shared_out, preferred_element_type=jnp.float32), axis=-1
    )
    gates_grad, sigma_grad = (
        lax.psum_scatter(gate_pair_grad, "fsdp", scatter_dimension=0, tiled=True),
        lax.psum_scatter(sigma_part, "fsdp", scatter_dimension=0, tiled=True),
    )
    summed_back = lax.psum_scatter(
        jnp.einsum("ncf,cdf->nd", shared_mix_grad, shared_in, preferred_element_type=jnp.float32)
        + hidden_sum,
        "fsdp",
        scatter_dimension=0,
        tiled=True,
    )
    hidden_grad = summed_back
    (logit_grad,) = gate_back(gates_grad)
    (gate_input_grad,) = sigma_back(sigma_grad)
    hidden_grad = (
        hidden_grad
        + jnp.dot(logit_grad, router_float.T, precision=HIGHEST_PRECISION)
        + gate_input_grad[:, None] * gate_float[None, :]
    )
    hidden_float = hidden_two.astype(jnp.float32)
    router_grad = jnp.dot(hidden_float.T, logit_grad, precision=HIGHEST_PRECISION)
    gate_weight_grad = jnp.dot(gate_input_grad, hidden_float, precision=HIGHEST_PRECISION)
    residual_norm_grad, gain_two_grad = norm_two_back(hidden_grad)
    residual_grad = grad_mine + residual_norm_grad
    output_low = residual_grad.astype(jnp.bfloat16)
    output_grad = contract_rows(attended_low, output_low)
    attended_grad = (
        contract_columns(output_low, weight_output)
        .astype(jnp.bfloat16)
        .reshape(local_rows, heads, HEAD_DIM)
    )
    probs = jnp.exp(scores_now() - log_total)
    prob_grad = jnp.einsum(
        "qhd,khd->hqk", attended_grad, value_all, preferred_element_type=jnp.float32
    )
    row_dot = jnp.sum(probs * prob_grad, axis=-1, keepdims=True)
    score_grad = (probs * (prob_grad - row_dot)).astype(jnp.bfloat16)
    query_grad = (
        jnp.einsum("hqk,khd->qhd", score_grad, key_all, preferred_element_type=jnp.float32) * scale
    )
    key_part = (
        jnp.einsum("hqk,qhd->khd", score_grad, query_low, preferred_element_type=jnp.float32)
        * scale
    )
    value_part = jnp.einsum(
        "hqk,qhd->khd",
        probs.astype(jnp.bfloat16),
        attended_grad,
        preferred_element_type=jnp.float32,
    )
    key_grad, value_grad = (
        lax.psum_scatter(
            key_part.reshape(group_rows, width), "fsdp", scatter_dimension=0, tiled=True
        ),
        lax.psum_scatter(
            value_part.reshape(group_rows, width), "fsdp", scatter_dimension=0, tiled=True
        ),
    )
    query_raw_grad, key_raw_grad = turn_back(
        (query_grad, key_grad.reshape(local_rows, heads, HEAD_DIM))
    )
    projected_grad = jnp.concatenate(
        [
            query_raw_grad.reshape(local_rows, width),
            key_raw_grad.reshape(local_rows, width),
            value_grad,
        ],
        axis=1,
    ).astype(jnp.bfloat16)
    bias_grad = jnp.sum(projected_grad.astype(jnp.float32), axis=0)
    projection_grad = contract_rows(hidden_one, projected_grad)
    hidden_one_grad = contract_columns(projected_grad, weight_projection)
    input_norm_grad, gain_one_grad = norm_one_back(hidden_one_grad)
    tokens_grad = residual_grad + input_norm_grad
    sharded = (
        lax.psum_scatter(gain_one_grad, "fsdp", scatter_dimension=0, tiled=True),
        lax.psum_scatter(projection_grad, "fsdp", scatter_dimension=0, tiled=True),
        lax.psum_scatter(bias_grad, "fsdp", scatter_dimension=0, tiled=True),
        lax.psum_scatter(output_grad, "fsdp", scatter_dimension=0, tiled=True),
        lax.psum_scatter(gain_two_grad, "fsdp", scatter_dimension=0, tiled=True),
        lax.psum_scatter(router_grad, "fsdp", scatter_dimension=0, tiled=True),
        lax.psum_scatter(gate_weight_grad, "fsdp", scatter_dimension=0, tiled=True),
    )
    totals = lax.psum(
        (
            sharded[0],
            sharded[1],
            sharded[2],
            sharded[3],
            sharded[4],
            sharded[5],
            sharded[6],
            shared_in_grad,
            shared_out_grad,
            expert_in_grad,
            expert_out_grad,
        ),
        "rep",
    )
    return (
        mixed,
        tokens_grad,
        totals[0],
        totals[1],
        totals[2],
        totals[3],
        totals[4],
        totals[5],
        totals[6],
        totals[7],
        totals[8],
        totals[9],
        totals[10],
    )


def solution(mesh):
    in_specs = (
        P(("rep", "fsdp"), None),
        P("rep", None),
        P("rep"),
        P("rep", None),
        P(("rep", "fsdp"), None),
        P("fsdp"),
        P("fsdp", None),
        P("fsdp"),
        P("fsdp", None),
        P("fsdp"),
        P("fsdp", None),
        P("fsdp"),
        P(None, None, "fsdp"),
        P("fsdp", None),
        P(None, None, None, "fsdp"),
        P(None, "fsdp", None),
    )
    out_specs = (
        P(("rep", "fsdp"), None),
        P(("rep", "fsdp"), None),
        P("fsdp"),
        P("fsdp", None),
        P("fsdp"),
        P("fsdp", None),
        P("fsdp"),
        P("fsdp", None),
        P("fsdp"),
        P(None, None, "fsdp"),
        P("fsdp", None),
        P(None, None, None, "fsdp"),
        P(None, "fsdp", None),
    )
    return jax.shard_map(shards, mesh=mesh, in_specs=in_specs, out_specs=out_specs, check_vma=False)
```

profile of v0, /device:TPU:0, one launch (start us, length us, event | category | flops | bytes accessed | tf_op | source)
XLA Modules:
  0.0 5197.6 jit_solution(10399476123924008918)
XLA Ops:
  21.7 23.8 all-gather.1
  48.6 183.9 %all-gather.11.cloned.1.call-done = bf16[2048,6144]{1,0:T(8,128)(2,1)} async-done(((bf16[256,6144]{1,0:T(8,128)(2,1)}), bf16[2048,6144]{1,0:T(8,128)(2,1)}) %all-gather.11.cloned.1.call-update) | async-done | bytes 25165840 | tf_op jit(solution)/shard_map/all_gather | solution.py:113
  277.0 82.6 %all-gather.15.cloned.1.call-done = bf16[2560,2048]{1,0:T(8,128)(2,1)} async-done(((bf16[320,2048]{1,0:T(8,128)(2,1)}), bf16[2560,2048]{1,0:T(8,128)(2,1)}) %all-gather.15.cloned.1.call-update) | async-done | bytes 10485776 | tf_op jit(solution)/shard_map/all_gather | solution.py:142
  373.8 25.2 fusion.146
  399.0 17.2 fusion.58
  416.3 43.4 all-gather.13.cloned.1.call-done
  459.7 24.5 fusion.97
  484.2 57.4 %all-gather.17.cloned.1.call-done = bf16[2048,2048]{1,0:T(8,128)(2,1)} async-done(((bf16[256,2048]{1,0:T(8,128)(2,1)}), bf16[2048,2048]{1,0:T(8,128)(2,1)}) %all-gather.17.cloned.1.call-update) | async-done | bytes 8388624 | tf_op jit(solution)/shard_map/all_gather | solution.py:114
  558.9 31.5 reduce-window.6
  602.7 37.9 scatter_custom_fusion.2
  683.5 57.1 %all-gather.19.cloned.1.call-done = bf16[2560,2048]{1,0:T(8,128)(2,1)} async-done(((bf16[320,2048]{1,0:T(8,128)(2,1)}), bf16[2560,2048]{1,0:T(8,128)(2,1)}) %all-gather.19.cloned.1.call-update) | async-done | bytes 10485776 | tf_op jit(solution)/shard_map/all_gather | solution.py:184
  764.5 351.3 %gather_fusion.2 = bf16[12288,2048]{1,0:T(8,128)(2,1)} fusion(bf16[8,321,2048]{2,0,1:T(8,128)(2,1)} %concatenate.21, s32[12288]{0:T(1024)S(1)} %reshape.450), kind=kCustom, calls=%fused_computation.2 | custom fusion | bytes 100761600 | tf_op jit(solution)/shard_map/vmap(jit(_take))/gather | solution.py:59
  1115.7 33.5 select_bitcast_fusion
  1149.2 33.4 copy.156
  1193.3 74.8 %gather_fusion.1 = f32[12288]{0:T(1024)S(1)} fusion(f32[8,1281]{1,0:T(8,128)S(1)} %concatenate.20, s32[12288]{0:T(1024)S(1)} %copy-done.1), kind=kCustom, calls=%fused_computation.1 | custom fusion | bytes 196608 | tf_op jit(solution)/shard_map/vmap(jit(_take))/gather | solution.py:59
  1278.7 806.5 %while.27 = (s32[]{:T(128)}, f32[2560,2048]{1,0:T(8,128)}, f32[8,1536]{1,0:T(8,128)S(1)}, f32[8,2,2048,176]{2,3,1,0:T(8,128)}, f32[8,176,2048]{2,1,0:T(8,128)}, ...) while((s32[]{:T(128)}, f32[2560,2048]{1,0:T(8,128)}, ...), condition=%wide.region_18.19_spmd, body=%wide.region_15.18_spmd.sunk | while | flops 9995810816 | bytes 193930992 | solution.py:285
  1280.0 19.5 gather_fusion
  1331.9 35.6 scatter_custom_fusion.13
  1380.7 19.5 gather_fusion
  1432.7 35.6 scatter_custom_fusion.13
  1481.5 19.5 gather_fusion
  1533.4 35.6 scatter_custom_fusion.13
  1582.2 19.5 gather_fusion
  1634.1 35.6 scatter_custom_fusion.13
  1682.9 19.5 gather_fusion
  1734.9 35.6 scatter_custom_fusion.13
  1783.7 19.5 gather_fusion
  1835.6 35.6 scatter_custom_fusion.13
  1884.4 19.5 gather_fusion
  1936.4 35.6 scatter_custom_fusion.13
  1985.2 19.5 gather_fusion
  2037.1 35.6 scatter_custom_fusion.13
  2086.0 62.4 %gather_fusion.3 = f32[10240]{0:T(1024)S(1)} fusion(f32[8,1536]{1,0:T(8,128)S(1)} %reshape.425, s32[10240]{0:T(1024)S(1)} %copy-done.2), kind=kCustom, calls=%fused_computation.3 | custom fusion | bytes 163840 | tf_op jit(solution)/shard_map/vmap(jit(_take))/gather | solution.py:59
  2162.1 19.3 fusion.69
  2181.4 17.4 fusion.83
  2198.8 28.4 bitcast_add_fusion
  2237.8 417.4 %while.26 = (s32[]{:T(128)}, f32[2560,2048]{1,0:T(8,128)}, s32[8,1536]{1,0:T(8,128)}, f32[8,1536]{1,0:T(8,128)}, bf16[8,1536,2048]{2,1,0:T(8,128)(2,1)}, /*index...) while((s32[]{:T(128)}, f32[2560,2048]{1,0:T(8,128)}, s32[8,1536]{1,0:T(8,128)}, ...), condition=%wide.region_13.14_spmd, body=%wide.region_11.13_spmd.sunk | while | flops 3329806848 | bytes 61834336 | solution.py:239
  2254.0 36.5 scatter_custom_fusion.11
  2306.4 36.5 scatter_custom_fusion.11
  2359.0 36.5 scatter_custom_fusion.11
  2411.5 36.2 scatter_custom_fusion.11
  2463.6 36.0 scatter_custom_fusion.11
  2515.4 36.0 scatter_custom_fusion.11
  2567.3 36.0 scatter_custom_fusion.11
  2619.2 36.0 scatter_custom_fusion.11
  2655.2 20.9 multiply_reduce_fusion.2
  2680.8 27.4 all-reduce.6
  2716.9 166.5 %reduce-scatter.9.cloned.1.call-done = f32[320,2048]{1,0:T(8,128)} async-done(((f32[2560,2048]{1,0:T(8,128)}), f32[320,2048]{1,0:T(8,128)}) %reduce-scatter.9.cloned.1.call-update) | async-done | bytes 2621456 | tf_op jit(solution)/shard_map/reduce_scatter | solution.py:244
  2898.0 42.7 multiply_reduce_fusion.1
  2940.7 41.4 multiply_convert_fusion.4
  2982.1 16.6 broadcast_multiply_fusion
  2998.7 21.3 copy.164
  3020.1 27.0 fusion.60
  3047.1 21.3 copy.169
  3081.1 17.3 multiply_bitcast_fusion
  3098.4 127.9 %reduce-scatter.15.cloned.1.call-done = f32[320,2048]{1,0:T(8,128)} async-done(((f32[2560,2048]{1,0:T(8,128)}), f32[320,2048]{1,0:T(8,128)}) %reduce-scatter.15.cloned.1.call-update) | async-done | bytes 2621456 | tf_op jit(solution)/shard_map/reduce_scatter | solution.py:350
  3230.0 204.7 %reduce-scatter.17.cloned.1.call-done = f32[320,2048]{1,0:T(8,128)} async-done(((f32[2560,2048]{1,0:T(8,128)}), f32[320,2048]{1,0:T(8,128)}) %reduce-scatter.17.cloned.1.call-update) | async-done | bytes 2621456 | tf_op jit(solution)/shard_map/reduce_scatter | solution.py:353
  3451.0 21.5 fusion.114
  3472.7 21.3 fusion.77
  3508.8 94.8 %reduce-scatter.21.cloned.1.call-done = f32[256,2048]{1,0:T(8,128)} async-done(((f32[2048,2048]{1,0:T(8,128)}), f32[256,2048]{1,0:T(8,128)}) %reduce-scatter.21.cloned.1.call-update) | async-done | bytes 2097168 | tf_op jit(solution)/shard_map/reduce_scatter | solution.py:377
  3603.5 483.9 %reduce-scatter.19.cloned.1.call-done = f32[256,6144]{1,0:T(8,128)} async-done(((f32[2048,6144]{1,0:T(8,128)}), f32[256,6144]{1,0:T(8,128)}) %reduce-scatter.19.cloned.1.call-update) | async-done | bytes 6291472 | tf_op jit(solution)/shard_map/reduce_scatter | solution.py:375
  4109.3 26.4 all-reduce.11
  4136.0 17.0 all-reduce.12
  4158.1 984.4 %all-reduce.16.cloned.1.call-done = (f32[256,6144]{1,0:T(8,128)}, f32[256,2048]{1,0:T(8,128)}, f32[2,2048,704]{1,2,0:T(8,128)}, f32[704,2048]{1,0:T(8,128)}, f32...) async-done(((f32[256,6144]{1,0:T(8,128)}, f32[256,2048]{1,0:T(8,128)}, f32[2,2048,704]{1,2,0:T(8,128)}, f32[704,2048]{1,0:T(8,128)}, f32[8,2,2048,176]{2,3,1,0:T(8,128)}, ...) | async-done | bytes 60293136 | tf_op jit(solution)/shard_map/psum | solution.py:382
  (518 shorter events, 858.3 us)
Async XLA Ops:
  7.2 2174.2 %copy-start = (bf16[704,2048]{1,0:T(8,128)(2,1)S(1)}, bf16[704,2048]{1,0:T(8,128)(2,1)}, u32[]{:S(2)}) copy-start(bf16[704,2048]{1,0:T(8,128)(2,1)} %param.33) | copy-start | bytes 8650756
  7.2 14.4 copy-start.62
  7.2 38.3 copy-start.60
  7.2 38.3 copy-start.43
  7.2 225.3 %all-gather.11.cloned.1.call-start = ((), (), s32[]{:S(2)}) async-start(), calls=%async_computation.8 | async-start | bytes 28311552 | tf_op jit(solution)/shard_map/all_gather | solution.py:113
  8.0 351.7 %all-gather.15.cloned.1.call-start = ((), (), s32[]{:S(2)}) async-start(), calls=%async_computation.10 | async-start | bytes 11796480 | tf_op jit(solution)/shard_map/all_gather | solution.py:142
  21.6 223.8 %copy-start.24 = (f32[8,1,256]{2,1,0:T(1,128)}, f32[8,1,256]{2,1,0:T(1,128)S(1)}, u32[]{:S(2)}) copy-start(f32[8,1,256]{2,1,0:T(1,128)S(1)} %convert_element_type.140) | copy-start | bytes 24580
  48.0 197.5 %copy-start.26 = (f32[320]{0:T(512)}, f32[320]{0:T(512)S(1)}, u32[]{:S(2)}) copy-start(f32[320]{0:T(512)S(1)} %fusion.132) | copy-start | bytes 3844
  48.6 205.2 %copy-start.18 = (f32[320,64]{1,0:T(8,128)}, f32[320,64]{1,0:T(8,128)S(1)}, u32[]{:S(2)}) copy-start(f32[320,64]{1,0:T(8,128)S(1)} %get-tuple-element.210) | copy-start | bytes 245764
  48.6 205.2 %copy-start.20 = (f32[320,64]{1,0:T(8,128)}, f32[320,64]{1,0:T(8,128)S(1)}, u32[]{:S(2)}) copy-start(f32[320,64]{1,0:T(8,128)S(1)} %get-tuple-element.211) | copy-start | bytes 245764
  261.9 197.8 %all-gather.13.cloned.1.call-start = ((), (), s32[]{:S(2)}) async-start(), calls=%async_computation.9 | async-start | bytes 11796480 | tf_op jit(solution)/shard_map/all_gather | solution.py:143
  265.0 276.6 %all-gather.17.cloned.1.call-start = ((), (), s32[]{:S(2)}) async-start(), calls=%async_computation.11 | async-start | bytes 9437184 | tf_op jit(solution)/shard_map/all_gather | solution.py:114
  265.6 404.0 %all-gather.21.cloned.1.call-start = ((), (), s32[]{:S(2)}) async-start(), calls=%async_computation.14 | async-start | bytes 11796480 | tf_op jit(solution)/shard_map/all_gather | solution.py:253
  266.2 474.4 %all-gather.19.cloned.1.call-start = ((), (), s32[]{:S(2)}) async-start(), calls=%async_computation.12 | async-start | bytes 11796480 | tf_op jit(solution)/shard_map/all_gather | solution.py:184
  275.3 274.1 %copy-start.34 = (f32[8,1,256]{2,1,0:T(1,128)}, f32[8,1,256]{2,1,0:T(1,128)S(1)}, u32[]{:S(2)}) copy-start(f32[8,1,256]{2,1,0:T(1,128)S(1)} %convert_element_type.142) | copy-start | bytes 24580
  399.0 60.6 %copy-start.30 = (f32[16,320]{1,0:T(8,128)}, f32[16,320]{1,0:T(8,128)S(1)}, u32[]{:S(2)}) copy-start(f32[16,320]{1,0:T(8,128)S(1)} %get-tuple-element.212) | copy-start | bytes 61444
  416.3 67.9 %copy-start.38 = (f32[16,320]{1,0:T(8,128)}, f32[16,320]{1,0:T(8,128)S(1)}, u32[]{:S(2)}) copy-start(f32[16,320]{1,0:T(8,128)S(1)} %fusion.58) | copy-start | bytes 61444
  551.7 2157.3 %reduce-scatter.13.cloned.1.call-start = ((), (), s32[]{:S(2)}) async-start(), calls=%async_computation.16 | async-start | bytes 1474560 | tf_op jit(solution)/shard_map/reduce_scatter | solution.py:300
  595.1 7.3 copy-start.64
  595.1 7.4 copy-start.63
  597.6 45.4 copy-start.67
  597.6 55.3 %copy-start.61 = (bf16[256,8]{0,1:T(8,128)(2,1)S(1)}, bf16[256,8]{0,1:T(8,128)(2,1)}, u32[]{:S(2)}) copy-start(bf16[256,8]{0,1:T(8,128)(2,1)} %param.30) | copy-start | bytes 12292
  640.7 42.8 copy-start.22
  1149.2 33.4 copy-start.28
  1182.6 6.9 copy-start.33
  1193.3 74.8 %copy-start.23 = (s32[8,1536]{1,0:T(8,128)S(1)}, s32[8,1536]{1,0:T(8,128)}, u32[]{:S(2)}) copy-start(s32[8,1536]{1,0:T(8,128)} %copy-done.22) | copy-start | bytes 147460
  1269.0 9.7 copy-start.44
  1306.8 7.9 copy-start.3
  1407.6 7.9 copy-start.3
  1508.3 7.9 copy-start.3
  1609.1 7.9 copy-start.3
  1669.7 6.0 copy-start.69
  1709.8 7.9 copy-start.3
  1810.5 7.9 copy-start.3
  1911.3 7.9 copy-start.3
  2012.0 7.9 copy-start.3
  2154.4 555.7 %reduce-scatter.11.cloned.1.call-start = ((), (), s32[]{:S(2)}) async-start(), calls=%async_computation.15 | async-start | bytes 23592960 | tf_op jit(solution)/shard_map/reduce_scatter | solution.py:303
  2154.5 7.6 copy-start.4
  2162.1 493.1 %copy-start.56 = (f32[2560]{0:T(1024)}, f32[2560]{0:T(1024)S(1)}, u32[]{:S(2)}) copy-start(f32[2560]{0:T(1024)S(1)} %add_divide_fusion.1) | copy-start | bytes 30724
  2227.2 656.2 %reduce-scatter.9.cloned.1.call-start = ((), (), s32[]{:S(2)}) async-start(), calls=%async_computation.13 | async-start | bytes 23592960 | tf_op jit(solution)/shard_map/reduce_scatter | solution.py:244
  2676.1 34.0 copy-start.35
  2676.2 34.0 copy-start.47
  2676.2 550.1 %reduce-scatter.15.cloned.1.call-start = ((), (), s32[]{:S(2)}) async-start(), calls=%async_computation.17 | async-start | bytes 23592960 | tf_op jit(solution)/shard_map/reduce_scatter | solution.py:350
  2708.9 7.9 copy-start.52
  2710.0 6.8 copy-start.48
  2710.1 6.8 copy-start.36
  2710.1 6.8 copy-start.50
  2710.2 6.7 copy-start.59
  3020.0 414.7 %reduce-scatter.17.cloned.1.call-start = ((), (), s32[]{:S(2)}) async-start(), calls=%async_computation.18 | async-start | bytes 23592960 | tf_op jit(solution)/shard_map/reduce_scatter | solution.py:353
  3068.4 535.1 %reduce-scatter.21.cloned.1.call-start = ((), (), s32[]{:S(2)}) async-start(), calls=%async_computation.20 | async-start | bytes 18874368 | tf_op jit(solution)/shard_map/reduce_scatter | solution.py:377
  3081.0 1006.4 %reduce-scatter.19.cloned.1.call-start = ((), (), s32[]{:S(2)}) async-start(), calls=%async_computation.19 | async-start | bytes 56623104 | tf_op jit(solution)/shard_map/reduce_scatter | solution.py:375
  3436.8 13.2 copy-start.10
  3472.6 21.4 copy-start.37
  3472.6 21.4 copy-start.49
  3472.6 21.4 copy-start.51
  3472.6 22.7 copy-start.57
  3472.6 663.4 %reduce-scatter.23.cloned.1.call-start = ((), (), s32[]{:S(2)}) async-start(), calls=%async_computation.21 | async-start | bytes 73728 | tf_op jit(solution)/shard_map/reduce_scatter | solution.py:379
  3472.6 21.3 copy-start.5
  3495.2 1647.2 %all-reduce.16.cloned.1.call-start = ((), (), s32[]{:S(2)}) async-start(), calls=%async_computation.22 | async-start | bytes 120586240 | tf_op jit(solution)/shard_map/psum | solution.py:382
  4093.1 16.2 copy-start.45
  4093.1 59.9 %copy-start.55 = (f32[320]{0:T(512)S(1)}, f32[320]{0:T(512)}, u32[]{:S(2)}) copy-start(f32[320]{0:T(512)} %copy-done.54) | copy-start | bytes 3844
  5142.5 6.3 copy-start.17
  5148.8 12.6 slice-start
  5150.1 11.3 slice-start.1
  (45 other events, 139.1 us)
Sparse Core Ops, SparseCore 0:
  9.7 222.7 all-gather.10
  262.0 97.5 all-gather.14
  361.9 97.7 all-gather.12
  461.1 80.4 all-gather.16
  543.1 97.9 all-gather.20
  642.5 97.9 all-gather.18
  2154.6 32.2 reduce-scatter.12
  2227.3 206.7 reduce-scatter.10
  2676.3 207.0 reduce-scatter.8
  3020.1 206.0 reduce-scatter.14
  3228.6 206.0 reduce-scatter.16
  3436.9 166.5 reduce-scatter.20
  3605.9 481.4 reduce-scatter.18
  4089.6 28.4 reduce-scatter.22
  4123.0 1019.4 all-reduce.15
where the time goes:
time: 5220 us; the launch traced here: 5200 us
  waiting for transfers between devices  2490 us (48%)
  local copies, waits for them, and re-layouts  968 us (19%)
  other arithmetic  821 us (16%)
  matrix products  757 us (15%)
  blocking collectives  144 us (3%)
    psum x1, waiting for transfers between devices, shards(): lax.psum((sharded[0], sharded[1], sharded[2], sharded[3], sharded[4], sha...  984 us
    gather x7, local copies, waits for them, and re-layouts, take_rows(): return jnp.take(block, index, axis=0)  492 us
    reduce_scatter x1, waiting for transfers between devices, shards(): lax.psum_scatter(projection_grad, 'fsdp', scatter_dimension=0, tiled=True)  484 us
    scatter-add x8, other arithmetic, expert_part(): return (accumulated.at[token_at].add(gate_of[:, None] * output), None)  290 us
    scatter-add x8, other arithmetic, expert_back_part(): accumulated.at[token_at].add(row_grad)  285 us
    reduce_scatter x1, waiting for transfers between devices, shards(): lax.psum_scatter(value_part.reshape(group_rows, width), 'fsdp', scatter_d...  205 us
    all_gather x1, waiting for transfers between devices, shards(): lax.all_gather(projection, 'fsdp', axis=0, tiled=True)  184 us
    reduce_scatter x1, waiting for transfers between devices, shards(): lax.psum_scatter(sigma_all[:, None] * jnp.dot(shared_act, shared_out, pre...  167 us
  transfers between devices with their start and end apart: 15, of which 11 were waited for; matrix products, arithmetic and copies ran while one was open for 18% of the time, Pallas kernels for 0%

commit v1 on v0

v1 whole, which is shorter than its diff:
```python
import functools

import jax
import jax.numpy as jnp
from jax import lax
from jax.experimental import pallas as pl
from jax.experimental.pallas import tpu as pltpu
from jax.sharding import PartitionSpec as P

HEAD_DIM = 128
EPS = 1e-06
THETA = 1000000.0
NEG = -1e30
LOW = jnp.bfloat16
WIDE = jnp.float32


def dot(left, right, dims, kind=WIDE):
    return lax.dot_general(left, right, ((dims[0], dims[1]), ((), ())), preferred_element_type=kind)


def mm(left, right, kind=WIDE):
    return dot(left, right, ((1,), (0,)), kind)


def mm_nt(left, right, kind=WIDE):
    return dot(left, right, ((1,), (1,)), kind)


def mm_tn(left, right, kind=WIDE):
    return dot(left, right, ((0,), (0,)), kind)


def scale_of(values):
    return lax.rsqrt(jnp.mean(values * values, axis=-1, keepdims=True) + EPS)


def rope_tables(position):
    half = HEAD_DIM // 2
    freq = THETA ** (-(jnp.arange(half, dtype=WIDE) * (2.0 / HEAD_DIM)))
    angle = position.astype(WIDE)[:, None] * freq[None, :]
    return (jnp.cos(angle), jnp.sin(angle))


def pair_block(ref, index, size):
    block = ref[:, pl.ds(pl.multiple_of(index * size, size), size), :]
    return block.reshape(block.shape[0] * size, block.shape[2])


def put_block(ref, index, size, block):
    ref[:, pl.ds(pl.multiple_of(index * size, size), size), :] = block.reshape(
        ref.shape[0], size, block.shape[1]
    )


def first_block(first_length, index, width):
    return jnp.where(index * width >= first_length, first_length // width, 0)


def span_mask(at_col, at_row, first_length):
    lowest = jnp.where(at_col >= first_length, first_length, 0)
    return (at_row <= at_col) & (at_row >= lowest)


def attend_kernel(
    size,
    lengths,
    query_in,
    key_in,
    value_in,
    cosine,
    sine,
    at_col,
    at_row,
    query,
    keyed,
    value,
    out,
    log_total,
):
    devices, rows, _ = query_in.shape
    width = size * devices
    first_length = lengths[0]
    factor = HEAD_DIM ** (-0.5)

    def prepare(index, carry):
        wave, ripple = pair_block(cosine, index, size), pair_block(sine, index, size)
        for source, target in ((query_in, query), (key_in, keyed)):
            block = pair_block(source, index, size)
            block = block * wave + pltpu.roll(block, HEAD_DIM // 2, 1) * ripple
            put_block(target, index, size, block.astype(LOW))
        put_block(value, index, size, pair_block(value_in, index, size).astype(LOW))
        return carry

    lax.fori_loop(0, rows // size, prepare, 0)

    def for_queries(index, carry):
        block = pair_block(query, index, size)
        places = pair_block(at_col, index, size)[:, :1]

        def for_keys(other, state):
            peak, total, summed = state
            raw = mm_nt(block, pair_block(keyed, other, size)) * factor
            raw = jnp.where(span_mask(places, at_row[other], first_length), raw, NEG)
            higher = jnp.maximum(peak, jnp.max(raw, axis=1, keepdims=True))
            lifted = jnp.exp(raw - higher)
            fade = jnp.exp(peak - higher)
            total = total * fade + jnp.sum(lifted, axis=1, keepdims=True)
            summed = summed * fade + mm(lifted.astype(LOW), pair_block(value, other, size))
            return higher, total, summed

        start = (
            jnp.full((width, 1), 2 * NEG, WIDE),
            jnp.zeros((width, 1), WIDE),
            jnp.zeros((width, HEAD_DIM), WIDE),
        )
        lowest = first_block(first_length, index, width)
        peak, total, summed = lax.fori_loop(lowest, index + 1, for_keys, start)
        put_block(out, index, size, (summed / total).astype(LOW))
        put_block(
            log_total, index, size, jnp.broadcast_to(peak + jnp.log(total), (width, HEAD_DIM))
        )
        return carry

    lax.fori_loop(0, rows // size, for_queries, 0)


def attend_back_kernel(
    size,
    lengths,
    query,
    keyed,
    value,
    attended,
    attended_back,
    log_total,
    cosine,
    sine,
    scale_row,
    at_col,
    at_row,
    query_back,
    key_back,
    value_back,
    query_scaled,
    key_scaled,
    value_scaled,
    query_sum,
    key_sum,
    value_sum,
):
    devices, rows, _ = query.shape
    width = size * devices
    first_length = lengths[0]
    factor = HEAD_DIM ** (-0.5)
    key_sum[...] = jnp.zeros_like(key_sum)
    value_sum[...] = jnp.zeros_like(value_sum)

    def for_queries(index, carry):
        block = pair_block(query, index, size)
        places = pair_block(at_col, index, size)[:, :1]
        logs = pair_block(log_total, index, size)[:, :1]
        pushed = pair_block(attended_back, index, size)
        row_dot = jnp.sum(
            pushed.astype(WIDE) * pair_block(attended, index, size).astype(WIDE),
            axis=1,
            keepdims=True,
        )

        def for_keys(other, summed):
            key_block = pair_block(keyed, other, size)
            raw = mm_nt(block, key_block) * factor
            raw = jnp.where(span_mask(places, at_row[other], first_length), raw, NEG)
            probs = jnp.exp(raw - logs)
            prob_back = mm_nt(pushed, pair_block(value, other, size))
            score_back = (probs * (prob_back - row_dot)).astype(LOW)
            here = pl.ds(pl.multiple_of(other * width, width), width)
            value_sum[here, :] += mm_tn(probs.astype(LOW), pushed)
            key_sum[here, :] += mm_tn(score_back, block)
            return summed + mm(score_back, key_block)

        lowest = first_block(first_length, index, width)
        query_sum[pl.ds(pl.multiple_of(index * width, width), width), :] = lax.fori_loop(
            lowest, index + 1, for_keys, jnp.zeros((width, HEAD_DIM), WIDE)
        )
        return carry

    lax.fori_loop(0, rows // size, for_queries, 0)

    def finish(index, carry):
        wave, ripple = pair_block(cosine, index, size), pair_block(sine, index, size)
        scale = pair_block(scale_row, index, size)[:, :1]
        here = pl.ds(pl.multiple_of(index * width, width), width)
        for source, target, scaled in (
            (query_sum, query_back, query_scaled),
            (key_sum, key_back, key_scaled),
        ):
            block = source[here, :] * factor
            block = block * wave - pltpu.roll(block, HEAD_DIM // 2, 1) * ripple
            block = block.astype(LOW)
            put_block(target, index, size, block)
            put_block(scaled, index, size, (block.astype(WIDE) * scale).astype(LOW))
        block = value_sum[here, :].astype(LOW)
        put_block(value_back, index, size, block)
        put_block(value_scaled, index, size, (block.astype(WIDE) * scale).astype(LOW))
        return carry

    lax.fori_loop(0, rows // size, finish, 0)


def work(micros):
    return pl.CostEstimate(
        flops=int(micros * 1e9), bytes_accessed=int(micros * 3e6), transcendentals=0
    )


def head_spec(devices, rows, first):
    return pl.BlockSpec((devices, rows, HEAD_DIM), lambda head: (0, 0, first + head))


def attend(lengths, projected, cosine, sine, at_col, at_row, held, size):
    devices, rows, _ = projected.shape
    whole = pl.BlockSpec((devices, rows, HEAD_DIM), lambda head: (0, 0, 0))
    low = jax.ShapeDtypeStruct((devices, rows, held * HEAD_DIM), LOW)
    return pl.pallas_call(
        functools.partial(attend_kernel, size),
        grid=(held,),
        in_specs=[
            pl.BlockSpec(memory_space=pltpu.SMEM),
            head_spec(devices, rows, 0),
            head_spec(devices, rows, held),
            head_spec(devices, rows, 2 * held),
            whole,
            whole,
            whole,
            pl.BlockSpec(at_row.shape, lambda head: (0, 0, 0)),
        ],
        out_specs=[head_spec(devices, rows, 0)] * 5,
        out_shape=[low] * 4 + [jax.ShapeDtypeStruct(low.shape, WIDE)],
        cost_estimate=work(30),
        compiler_params=pltpu.CompilerParams(vmem_limit_bytes=48 * 2**20),
    )(lengths, projected, projected, projected, cosine, sine, at_col, at_row)


def attend_back(
    lengths, query, keyed, value, attended, pushed, log_total, cosine, sine, scale_row,
    at_col, at_row, held, size,
):
    devices, rows, _ = query.shape
    whole = pl.BlockSpec((devices, rows, HEAD_DIM), lambda head: (0, 0, 0))
    own = head_spec(devices, rows, 0)
    low = jax.ShapeDtypeStruct((devices, rows, held * HEAD_DIM), LOW)
    return pl.pallas_call(
        functools.partial(attend_back_kernel, size),
        grid=(held,),
        in_specs=[
            pl.BlockSpec(memory_space=pltpu.SMEM),
            own,
            own,
            own,
            own,
            own,
            own,
            whole,
            whole,
            whole,
            whole,
            pl.BlockSpec(at_row.shape, lambda head: (0, 0, 0)),
        ],
        out_specs=[own] * 6,
        out_shape=[low] * 6,
        scratch_shapes=[pltpu.VMEM((devices * rows, HEAD_DIM), WIDE)] * 3,
        compiler_params=pltpu.CompilerParams(vmem_limit_bytes=48 * 2**20),
    )(
        lengths, query, keyed, value, attended, pushed, log_total, cosine, sine, scale_row,
        at_col, at_row,
    )


def chunks_of(total):
    return [(start, min(256, total - start)) for start in range(0, total, 256)]


def middle_kernel(
    experts, hidden, weights, chosen, spread, back, act_out, grad_out, strengths
):
    total = act_out.shape[1]
    rows = hidden[...]
    lane = lax.broadcasted_iota(jnp.int32, (rows.shape[0], 128), 1)
    logits = mm_nt(rows, weights[2 * total :, :])
    sigma = jax.nn.sigmoid(logits)
    masked = jnp.where((lane >= 1) & (lane <= experts), logits, NEG)
    lifted = jnp.exp(masked - jnp.max(masked, axis=1, keepdims=True))
    normal = lifted / jnp.sum(lifted, axis=1, keepdims=True)
    named = chosen[...].astype(WIDE)
    strength = jnp.where(lane == 0, sigma, normal * named)
    high = strength.astype(LOW)
    rest = (strength - high.astype(WIDE)).astype(LOW)
    strengths[...] = jnp.zeros_like(strengths)
    for start, size in chunks_of(total):
        here = pl.ds(start, size)
        gate = mm_nt(rows, weights[start : start + size, :])
        up = mm_nt(rows, weights[total + start : total + start + size, :])
        wide = mm(high, spread[:, here]) + mm(rest, spread[:, here])
        pushed = back[:, here].astype(WIDE)
        curve = jax.nn.sigmoid(gate)
        silu = gate * curve
        act = silu * up
        act_out[:, here] = (wide * act).astype(LOW)
        strengths[...] += mm_nt((act * pushed).astype(LOW), spread[:, here])
        pushed = wide * pushed
        grad_out[:, here] = (pushed * up * (curve + silu * (1.0 - curve))).astype(LOW)
        grad_out[:, pl.ds(total + start, size)] = (pushed * silu).astype(LOW)
    backs = strengths[...]
    gates_back = jnp.where(lane >= 1, backs * named, 0.0)
    logit_grad = normal * (gates_back - jnp.sum(normal * gates_back, axis=1, keepdims=True))
    logit_grad = jnp.where(lane == 0, backs * sigma * (1.0 - sigma), logit_grad)
    grad_out[:, 2 * total :] = logit_grad.astype(LOW)


def middle(hidden, weights, chosen, spread, back, experts):
    group, width = hidden.shape
    total = back.shape[1]
    rows = group // 5
    by_rows = lambda columns: pl.BlockSpec((rows, columns), lambda i: (i, 0))
    held = lambda shape: pl.BlockSpec(shape, lambda i: (0, 0), pipeline_mode=pl.Buffered(1))
    return pl.pallas_call(
        functools.partial(middle_kernel, experts),
        grid=(group // rows,),
        in_specs=[
            by_rows(width),
            held(weights.shape),
            by_rows(128),
            held(spread.shape),
            by_rows(total),
        ],
        out_specs=[by_rows(total), by_rows(weights.shape[0])],
        out_shape=[
            jax.ShapeDtypeStruct((group, total), LOW),
            jax.ShapeDtypeStruct((group, weights.shape[0]), LOW),
        ],
        scratch_shapes=[pltpu.VMEM((rows, 128), WIDE)],
        cost_estimate=work(55),
        compiler_params=pltpu.CompilerParams(vmem_limit_bytes=58 * 2**20),
    )(hidden, weights, chosen, spread, back)


def ring_blocks(block, devices, first, last):
    ring = [(i, (i + 2) % devices) for i in range(devices)]
    blocks = [block]
    for _ in range(first, last):
        blocks.append(lax.ppermute(blocks[-1], "fsdp", ring))
    return blocks


def ring_place(blocks, devices):
    mine = lax.axis_index("fsdp")
    twin = [(i, i ^ 1) for i in range(devices)]
    whole = jnp.zeros((devices,) + blocks[0].shape, blocks[0].dtype)
    for step, block in enumerate(blocks):
        owner = lax.rem(mine + devices - 2 * step, devices)
        whole = lax.dynamic_update_index_in_dim(whole, block, owner, 0)
        other = lax.ppermute(block, "fsdp", twin)
        whole = lax.dynamic_update_index_in_dim(whole, other, owner ^ 1, 0)
    return whole


def remote(source, target, sent, arrived, where):
    return pltpu.make_async_remote_copy(
        src_ref=source,
        dst_ref=target,
        send_sem=sent,
        recv_sem=arrived,
        device_id=where,
        device_id_type=pl.DeviceIdType.MESH,
    )


def open_kernel(peers):
    barrier = pltpu.get_barrier_semaphore()
    for peer in peers:
        pl.semaphore_signal(
            barrier, inc=1, device_id=peer, device_id_type=pl.DeviceIdType.MESH
        )
    pl.semaphore_wait(barrier, len(peers))


def gather_kernel(
    devices,
    reps,
    token,
    strip,
    share,
    small,
    token_all,
    strip_all,
    share_all,
    small_all,
    ring_sent,
    ring_got,
    twin_sent,
    twin_got,
    deal_sent,
    deal_got,
    rep_sent,
    rep_got,
    share_sent,
    share_got,
    pass_sent,
    pass_got,
    local_done,
):
    mine = lax.axis_index("fsdp")
    copy = lax.axis_index("rep")
    steps = devices // 2
    right = lax.rem(mine + 2, devices)
    twin = mine + 1 - 2 * lax.rem(mine, 2)
    around = [{"fsdp": lax.rem(mine + k, devices)} for k in range(1, devices)]
    across = [{"rep": lax.rem(copy + k, reps)} for k in range(1, reps)]
    open_kernel(around + across)

    owners = [lax.rem(mine + devices - 2 * s, devices) for s in range(steps)]
    inputs = (token, share, small)
    whole = (token_all, share_all.at[:, copy], small_all)
    everything = []

    def begin(one):
        one.start()
        everything.append(one)
        return one

    locals_ = [
        pltpu.make_async_copy(token, token_all.at[mine], local_done.at[0]),
        pltpu.make_async_copy(share, share_all.at[mine, copy], local_done.at[1]),
        pltpu.make_async_copy(small, small_all.at[mine], local_done.at[2]),
        pltpu.make_async_copy(strip.at[mine], strip_all.at[mine, copy], local_done.at[3]),
    ]
    def ring_step(j, s):
        source = inputs[j] if s == 0 else whole[j].at[owners[s]]
        if s + 1 < steps:
            begin(
                remote(
                    source,
                    whole[j].at[owners[s]],
                    ring_sent.at[j, s],
                    ring_got.at[j, s],
                    {"fsdp": right},
                )
            )
        begin(
            remote(
                source,
                whole[j].at[owners[s]],
                twin_sent.at[j, s],
                twin_got.at[j, s],
                {"fsdp": twin},
            )
        )

    def ring_wait(j, s):
        remote(
            inputs[j],
            whole[j].at[owners[s + 1]],
            ring_sent.at[j, s],
            ring_got.at[j, s],
            {"fsdp": right},
        ).wait_recv()

    deals = []
    for k in range(1, devices):
        peer = lax.rem(mine + k, devices)
        deals.append(
            begin(
                remote(
                    strip.at[peer],
                    strip_all.at[mine, copy],
                    deal_sent.at[k - 1],
                    deal_got.at[k - 1],
                    {"fsdp": peer},
                )
            )
        )
    ring_step(1, 0)
    ring_step(2, 0)
    ring_step(0, 0)
    for one in locals_:
        one.start()
    for s in range(1, steps):
        for j in (1, 2):
            ring_wait(j, s - 1)
            ring_step(j, s)

    if steps > 1:
        ring_wait(0, 0)
        ring_step(0, 1)
    locals_[3].wait()
    for one in deals:
        one.wait_recv()
    crossed = []
    for k in range(1, reps):
        crossed.append(
            begin(
                remote(
                    strip_all.at[:, copy],
                    strip_all.at[:, copy],
                    rep_sent.at[k - 1],
                    rep_got.at[k - 1],
                    {"rep": lax.rem(copy + k, reps)},
                )
            )
        )
    shared = []
    for k in range(1, reps):
        for s in range(steps):
            source = share if s == 0 else share_all.at[owners[s], copy]
            shared.append(
                begin(
                    remote(
                        source,
                        share_all.at[owners[s], copy],
                        share_sent.at[k - 1, s],
                        share_got.at[k - 1, s],
                        {"rep": lax.rem(copy + k, reps)},
                    )
                )
            )
    if steps > 2:
        ring_wait(0, 1)
        ring_step(0, 2)
    for k in range(1, reps):
        origin = lax.rem(copy + reps - k, reps)
        for s in range(steps):
            shared[(k - 1) * steps + s].wait_recv()
            begin(
                remote(
                    share_all.at[owners[s], origin],
                    share_all.at[owners[s], origin],
                    pass_sent.at[k - 1, s],
                    pass_got.at[k - 1, s],
                    {"fsdp": twin},
                )
            )
    for s in range(3, steps):
        ring_wait(0, s - 1)
        ring_step(0, s)
    for one in everything:
        one.wait_send()
    for j in range(3):
        for s in range(steps):
            remote(
                inputs[j],
                whole[j].at[owners[s]],
                twin_sent.at[j, s],
                twin_got.at[j, s],
                {"fsdp": twin},
            ).wait_recv()
    for one in crossed:
        one.wait_recv()
    for k in range(1, reps):
        for s in range(steps):
            remote(
                share,
                share_all.at[owners[s], copy],
                pass_sent.at[k - 1, s],
                pass_got.at[k - 1, s],
                {"fsdp": twin},
            ).wait_recv()
    for one in locals_[:3]:
        one.wait()


def gather_all(token, strip, share, small, reps):
    devices, piece, columns = strip.shape
    steps = devices // 2
    dma = pltpu.SemaphoreType.DMA
    anywhere = pl.BlockSpec(memory_space=pl.ANY)
    return pl.pallas_call(
        functools.partial(gather_kernel, devices, reps),
        in_specs=[pl.BlockSpec(memory_space=pltpu.VMEM)] * 4,
        out_specs=[anywhere] * 4,
        out_shape=[
            jax.ShapeDtypeStruct((devices,) + token.shape, LOW),
            jax.ShapeDtypeStruct((devices, reps, piece, columns), LOW),
            jax.ShapeDtypeStruct((devices, reps) + share.shape, LOW),
            jax.ShapeDtypeStruct((devices,) + small.shape, LOW),
        ],
        scratch_shapes=[
            dma((3, steps)),
            dma((3, steps)),
            dma((3, steps)),
            dma((3, steps)),
            dma((devices - 1,)),
            dma((devices - 1,)),
            dma((reps - 1,)),
            dma((reps - 1,)),
            dma((reps - 1, steps)),
            dma((reps - 1, steps)),
            dma((reps - 1, steps)),
            dma((reps - 1, steps)),
            dma((4,)),
        ],
        cost_estimate=work(100),
        compiler_params=pltpu.CompilerParams(collective_id=0, has_side_effects=True),
    )(token, strip, share, small)


def reduce_rep(values):
    return lax.psum(values, "rep")


def shards(
    tokens,
    lengths,
    dealing,
    routes,
    cotangent,
    first_gain,
    projection,
    projection_bias,
    output_weight,
    second_gain,
    router_weight,
    shared_gate,
    shared_in,
    shared_out,
    expert_in,
    expert_out,
):
    width = tokens.shape[1]
    rows = tokens.shape[0]
    group = dealing.shape[0]
    devices = group // rows
    part = width // devices
    held = part // HEAD_DIM
    experts, _, _, units = expert_in.shape
    hidden = -(-units // 16) * 16
    common = shared_out.shape[0]
    total = common + experts * hidden
    reps = lax.axis_size("rep")
    piece = part // reps
    mine = lax.axis_index("fsdp")
    copy = lax.axis_index("rep")
    scale = HEAD_DIM ** (-0.5)

    gain_one = first_gain.astype(WIDE)
    strip = lax.dynamic_slice_in_dim(projection, copy * piece, piece, 0).astype(WIDE)
    strip = (lax.dynamic_slice_in_dim(gain_one, copy * piece, piece, 0)[:, None] * strip).astype(LOW)
    strip = strip.reshape(piece, 3, devices, part).transpose(2, 0, 1, 3)
    strip = strip.reshape(devices, piece, 3 * part)
    share = lax.dynamic_slice_in_dim(output_weight, copy * piece, piece, 0)
    small = jnp.concatenate(
        [second_gain, shared_gate, projection_bias, router_weight.reshape(-1)]
    )
    length = small.shape[0]
    small = jnp.pad(small, (0, -length % 2048)).reshape(-1, 128)
    token_all, strip, share, small = gather_all(tokens, strip, share, small, reps)
    token_all = token_all.reshape(group, width)
    weight_mine = strip.reshape(width, 3 * part)
    weight_output = share.reshape(width, width)
    small = small.reshape(devices, -1)[:, :length]
    cot_in, _ = lax.optimization_barrier((cotangent, token_all))
    steps = devices // 2
    cot_blocks = ring_blocks(cot_in, devices, 0, steps // 2)

    gain_two = small[:, :part].reshape(width).astype(WIDE)
    gate_weight = small[:, part : 2 * part].reshape(width, 1)
    bias = small[:, 2 * part : 5 * part].reshape(3, devices, part)
    bias_mine = lax.dynamic_slice_in_dim(bias, mine, 1, 1).reshape(3 * part).astype(WIDE)
    router = small[:, 5 * part :].reshape(width, experts)
    choice_weight = jnp.concatenate(
        [gate_weight, router, jnp.zeros((width, 127 - experts), LOW)], axis=1
    )
    full = -(-total // 128) * 128
    expert_rows = expert_in.transpose(0, 1, 3, 2)
    expert_down = expert_out
    if hidden > units:
        expert_rows = jnp.pad(expert_rows, ((0, 0), (0, 0), (0, hidden - units), (0, 0)))
        expert_down = jnp.pad(expert_down, ((0, 0), (0, hidden - units), (0, 0)))
    fill = jnp.zeros((full - total, width), LOW)
    weights = []
    for half in range(2):
        weights.append(shared_in[half].T)
        weights.append(expert_rows[:, half].reshape(experts * hidden, width))
        weights.append(fill)
    weights = jnp.concatenate(weights + [choice_weight.T], axis=0)
    weight_down = jnp.concatenate(
        [shared_out, expert_down.reshape(experts * hidden, width), fill], axis=0
    )

    scale_all = scale_of(token_all.astype(WIDE))
    projected = scale_all * mm(token_all, weight_mine) + bias_mine
    first_length = lengths[0, 0]
    second = (dealing >= first_length).astype(jnp.int32)
    cosine, sine = rope_tables(dealing - second * first_length)
    shape = (devices, rows, HEAD_DIM)
    cosine = jnp.concatenate([cosine, cosine], axis=1).reshape(shape)
    sine = jnp.concatenate([-sine, sine], axis=1).reshape(shape)
    size = 256 // devices
    at_col = jnp.broadcast_to(dealing.reshape(devices, rows, 1), shape)
    at_row = dealing.reshape(devices, rows // size, size).transpose(1, 0, 2)
    at_row = at_row.reshape(rows // size, 1, devices * size)
    scale_row = jnp.broadcast_to(scale_all.reshape(devices, rows, 1), shape)
    query, keyed, value, attended_mine, log_total = attend(
        lengths[0], projected.reshape(devices, rows, 3 * part), cosine, sine, at_col, at_row,
        held, size,
    )
    attended, halfway = lax.optimization_barrier(
        (attended_mine.reshape(group, part), cot_blocks[-1])
    )
    cot_blocks = cot_blocks[:-1] + ring_blocks(halfway, devices, steps // 2, steps - 1)
    cot_all = ring_place(cot_blocks, devices).reshape(group, width)
    attended = lax.all_to_all(attended, "fsdp", split_axis=0, concat_axis=1, tiled=True)

    residual = tokens.astype(WIDE) + mm(attended, weight_output)
    scale_two = scale_of(residual)
    unit = residual * scale_two
    hidden_two = (unit * gain_two).astype(LOW)
    hidden_blocks = ring_blocks(hidden_two, devices, 0, steps - 1)
    hidden_all = ring_place(hidden_blocks, devices).reshape(group, width)

    lane = jnp.arange(128, dtype=jnp.int32)
    chosen = jnp.any(routes[:, :, None] + 1 == lane[None, None, :], axis=1).astype(LOW)
    owner = jnp.concatenate(
        [
            jnp.zeros((common,), jnp.int32),
            1 + jnp.repeat(jnp.arange(experts, dtype=jnp.int32), hidden),
            jnp.full((full - total,), 127, jnp.int32),
        ]
    )
    spread = (owner[None, :] == lane[:, None]).astype(LOW)
    back = mm_nt(cot_all, weight_down, LOW)
    act_low, grads = middle(hidden_all, weights, chosen, spread, back, experts)

    down_grad = mm_tn(act_low, cot_all, LOW)
    in_grad = mm_tn(grads, hidden_all, LOW)
    choice_weight_grad = in_grad[2 * full :].T
    grads, down_grad, in_grad = lax.optimization_barrier((grads, down_grad, in_grad))
    down_grad = reduce_rep(down_grad)
    hidden_back = mm(grads, weights, LOW)
    act_low, in_grad, hidden_back = lax.optimization_barrier((act_low, in_grad, hidden_back))
    in_grad, down_grad = lax.optimization_barrier((in_grad, down_grad))
    in_grad = reduce_rep(in_grad)
    hidden_back = lax.psum_scatter(hidden_back, "fsdp", scatter_dimension=0, tiled=True)
    hidden_back = hidden_back.astype(WIDE)
    layered = mm(act_low, weight_down, LOW)

    gain_two_grad = jnp.sum(hidden_back * unit, axis=0)
    pushed = hidden_back * gain_two
    residual_grad = cotangent.astype(WIDE) + scale_two * (
        pushed - unit * jnp.mean(pushed * unit, axis=-1, keepdims=True)
    )
    output_low = residual_grad.astype(LOW)
    attended_back = mm_nt(output_low, weight_output, LOW)
    attended_back = lax.all_to_all(
        attended_back, "fsdp", split_axis=1, concat_axis=0, tiled=True
    ).reshape(devices, rows, part)
    attended_back, attended_held = lax.optimization_barrier((attended_back, attended))
    lane = jnp.arange(128, dtype=jnp.int32)
    extra = jnp.where(
        lane[None, :] == experts + 1, gain_two_grad[:, None].astype(LOW), choice_weight_grad
    )
    output_grad = jnp.concatenate([mm_tn(attended_held, output_low, LOW), extra], axis=1)
    layered, output_grad = lax.optimization_barrier((layered, output_grad))
    layered = lax.psum_scatter(layered, "fsdp", scatter_dimension=0, tiled=True)
    mixed = (residual + layered.astype(WIDE)).astype(LOW)
    output_grad = lax.psum_scatter(output_grad, "fsdp", scatter_dimension=0, tiled=True)

    parts = attend_back(
        lengths[0], query, keyed, value, attended_mine, attended_back, log_total, cosine, sine,
        scale_row, at_col, at_row, held, size,
    )
    projected_back = jnp.concatenate(parts[:3], axis=2).reshape(group, 3 * part)
    scaled_back = jnp.concatenate(parts[3:], axis=2).reshape(group, 3 * part)
    bias_grad = jnp.sum(projected_back.astype(WIDE), axis=0)
    weight_grad = mm_tn(token_all, scaled_back, LOW)
    bias_rows = jnp.broadcast_to(
        bias_grad.astype(LOW).reshape(1, 1, 3, part), (devices, 16, 3, part)
    )
    weight_grad = jnp.concatenate([weight_grad.reshape(devices, part, 3, part), bias_rows], axis=1)
    weight_grad = lax.all_to_all(
        weight_grad, "fsdp", split_axis=0, concat_axis=2, tiled=False
    ).reshape(part + 16, 3 * width)
    weight_grad, projected_back = lax.optimization_barrier((weight_grad, projected_back))
    token_back = mm_nt(projected_back, weight_mine, LOW)
    weight_grad, _ = lax.optimization_barrier((weight_grad, token_back))
    weight_grad, output_grad, in_grad, down_grad = lax.optimization_barrier(
        (weight_grad, output_grad, in_grad, down_grad)
    )
    weight_grad, output_grad = lax.psum((weight_grad, output_grad), "rep")
    bias_grad = weight_grad[part].astype(WIDE).reshape(devices, 3 * part)
    bias_grad = lax.dynamic_slice_in_dim(bias_grad, mine, 1, 0)[0]
    weight_grad = weight_grad[:part].astype(WIDE)
    small = output_grad[:, width:].astype(WIDE)
    output_grad = output_grad[:, :width].astype(WIDE)
    first_gain_grad = jnp.sum(weight_grad * projection.astype(WIDE), axis=1)
    projection_grad = weight_grad * gain_one[:, None]

    pushed = lax.psum_scatter(token_back, "fsdp", scatter_dimension=0, tiled=True).astype(WIDE)
    inputs = tokens.astype(WIDE)
    scale_one = scale_of(inputs)
    unit_one = inputs * scale_one
    tokens_grad = residual_grad + scale_one * (
        pushed - unit_one * jnp.mean(pushed * unit_one, axis=-1, keepdims=True)
    )

    in_grad = in_grad[: 2 * full].reshape(2, full, width)
    shared_in_grad = in_grad[:, :common].astype(WIDE).transpose(0, 2, 1)
    expert_in_grad = in_grad[:, common:total].reshape(2, experts, hidden, width)
    expert_in_grad = expert_in_grad[:, :, :units].astype(WIDE).transpose(1, 0, 3, 2)
    down_grad = down_grad.astype(WIDE)
    return (
        mixed,
        tokens_grad,
        first_gain_grad,
        projection_grad,
        bias_grad,
        output_grad,
        small[:, experts + 1],
        small[:, 1 : experts + 1],
        small[:, 0],
        shared_in_grad,
        down_grad[:common],
        expert_in_grad,
        down_grad[common:total].reshape(experts, hidden, width)[:, :units],
    )


def solution(mesh):
    in_specs = (
        P(("rep", "fsdp"), None),
        P("rep", None),
        P("rep"),
        P("rep", None),
        P(("rep", "fsdp"), None),
        P("fsdp"),
        P("fsdp", None),
        P("fsdp"),
        P("fsdp", None),
        P("fsdp"),
        P("fsdp", None),
        P("fsdp"),
        P(None, None, "fsdp"),
        P("fsdp", None),
        P(None, None, None, "fsdp"),
        P(None, "fsdp", None),
    )
    out_specs = (
        P(("rep", "fsdp"), None),
        P(("rep", "fsdp"), None),
        P("fsdp"),
        P("fsdp", None),
        P("fsdp"),
        P("fsdp", None),
        P("fsdp"),
        P("fsdp", None),
        P("fsdp"),
        P(None, None, "fsdp"),
        P("fsdp", None),
        P(None, None, None, "fsdp"),
        P(None, "fsdp", None),
    )
    return jax.shard_map(shards, mesh=mesh, in_specs=in_specs, out_specs=out_specs, check_vma=False)
```

time: 5220 us -> 1340 us (0.26)
  waiting for transfers between devices: 2490 us -> 336 us
  local copies, waits for them, and re-layouts: 968 us -> 159 us
  other arithmetic: 821 us -> 72.9 us
  matrix products: 757 us -> 268 us
  Pallas kernels: 0 us -> 325 us
    reduce_scatter x7 -> x3, waiting for transfers between devices: 983 us -> 0.01 us  [the longest x1 0.01 us: shards(): lax.psum_scatter(hidden_back, 'fsdp', scatter_dimension=0, tiled=True)]
    psum x1 -> x3, waiting for transfers between devices: 984 us -> 216 us  [the longest x2 154 us: reduce_rep(): return lax.psum(values, 'rep')]
    gather x15 -> x0, local copies, waits for them, and re-layouts: 648 us -> none  [the longest x7 492 us: take_rows(): return jnp.take(block, index, axis=0)]
    scatter-add x16 -> x0, other arithmetic: 574 us -> none  [the longest x8 290 us: expert_part(): return (accumulated.at[token_at].add(gate_of[:, None] * output), None)]
    all_gather x6 -> x0, waiting for transfers between devices: 424 us -> none  [the longest x1 184 us: shards(): lax.all_gather(projection, 'fsdp', axis=0, tiled=True)]
    dot_general x72 -> x11, matrix products: 673 us -> 268 us  [dot(): lax.dot_general(left, right, ((dims[0], dims[1]), ((), ())), preferred_el...]
    pallas_call x0 -> x4, Pallas kernels: none -> 325 us  [the longest x1 155 us: gather_all(): pl.pallas_call(functools.partial(gather_kernel, devices, reps), in_specs=...]
    all_to_all x0 -> x1, blocking collectives: none -> 133 us  [shards(): lax.all_to_all(weight_grad, 'fsdp', split_axis=0, concat_axis=2, tiled=Fa...]
  transfers between devices with their start and end apart: 15 -> 23, of which waited for: 11 -> 9; matrix products, arithmetic and copies ran while one was open for 18% -> 29% of each run, Pallas kernels for 0% -> 7%
where the time goes in v1:
time: 1340 us; the launch traced here: 1330 us
  waiting for transfers between devices  336 us (25%)
  Pallas kernels  325 us (24%)
  matrix products  268 us (20%)
  local copies, waits for them, and re-layouts  159 us (12%)
  blocking collectives  133 us (10%)
  other arithmetic  72.9 us (5%)
  starting transfers between devices  16.7 us (1%)
  between operations  16.7 us (1%)
    dot_general x11, matrix products, dot(): lax.dot_general(left, right, ((dims[0], dims[1]), ((), ())), preferred_el...  268 us
    pallas_call x1, Pallas kernels, gather_all(): pl.pallas_call(functools.partial(gather_kernel, devices, reps), in_specs=...  155 us
    psum x2, waiting for transfers between devices, reduce_rep(): return lax.psum(values, 'rep')  154 us
    all_to_all x1, blocking collectives, shards(): lax.all_to_all(weight_grad, 'fsdp', split_axis=0, concat_axis=2, tiled=Fa...  133 us
    ppermute x6, waiting for transfers between devices, ring_blocks(): blocks.append(lax.ppermute(blocks[-1], 'fsdp', ring))  113 us
    pallas_call x1, Pallas kernels, middle(): pl.pallas_call(functools.partial(middle_kernel, experts), grid=(group //...  79.6 us
    psum x1, waiting for transfers between devices, shards(): weight_grad, output_grad = lax.psum((weight_grad, output_grad), 'rep')  62.5 us
    unnamed x99, local copies, waits for them, and re-layouts  47.3 us
  transfers between devices with their start and end apart: 23, of which 9 were waited for; matrix products, arithmetic and copies ran while one was open for 29% of the time, Pallas kernels for 7%

profile of v1, /device:TPU:0, one launch (start us, length us, event | category | flops | bytes accessed | tf_op | source)
XLA Modules:
  0.0 1328.0 jit_solution(14083997113622646795)
XLA Ops:
  14.1 155.0 %shard_map.255 = (bf16[8,320,2048]{2,1,0:T(8,128)(2,1)}, bf16[8,4,64,768]{3,2,1,0:T(8,128)(2,1)}, bf16[8,4,64,2048]{3,2,1,0:T(8,128)(2,1)}, bf16[8,32,128]{2,1,0:T(8,128)(2,1)}) custom-call(bf16[320,2048]{1,0:T(8,128)(2,1)} %token_.1, bf16[8,64,768]{2,1,0:T(8,128)(2,1)} %reshape.249.strip, bf16[64,2048]{1,0:T(8,128)(2,1)} %constant_dynamic-slice_fusion.2.share, ...), custom_call_target="tpu_custom_call" | custom-call | flops 99999997952 | bytes 300000000 | tf_op jit(solution)/shard_map/pallas_call | solution.py:577
  171.5 6.1 multiply_reduce_fusion
  178.6 3.8 bitcast_dynamic-update-slice_fusion.1
  182.4 11.2 fusion.38
  193.7 6.2 constant_dynamic-update-slice_fusion.1
  203.0 4.6 fusion.23
  207.6 13.2 multiply_add_fusion
  224.3 43.1 %shard_map.256 = (bf16[8,320,256]{2,1,0:T(8,128)(2,1)S(1)}, bf16[8,320,256]{2,1,0:T(8,128)(2,1)S(1)}, bf16[8,320,256]{2,1,0:T(8,128)(2,1)S(1)}, bf16[8,320,256]{2,1,0:T(8,128)(2,1)}, f32[8,320,256]{2,1,0:T(8,128)}) custom-call(s32[2]{0:T(128)S(1)} %bitcast.144, f32[8,320,768]{2,1,0:T(8,128)} %bitcast.184, f32[8,320,768]{2,1,0:T(8,128)} %bitcast.185, ...), custom_call_target="tpu_custom_call" | custom-call | flops 30000001024 | bytes 90000000 | tf_op jit(solution)/shard_map/pallas_call | solution.py:225
  272.9 3.9 bitcast_dynamic-update-slice_fusion
  276.7 6.1 constant_dynamic-update-slice_fusion
  282.8 2.6 collective-permute-start.1
  285.4 5.4 broadcast.122.clone.1
  293.7 22.4 %collective-permute-done.1 = bf16[320,2048]{1,0:T(8,128)(2,1)} collective-permute-done((bf16[320,2048]{1,0:T(8,128)(2,1)}, bf16[320,2048]{1,0:T(8,128)(2,1)}, u32[]{:S(2)}, u32[]{:S(2)}) %collective-permute-start.1) | collective-permute-done | bytes 1310752 | tf_op jit(solution)/shard_map/ppermute | solution.py:352
  316.1 4.3 all-to-all-start
  321.4 2.5 bitcast_dynamic-update-slice_fusion.8
  325.8 2.6 bitcast_dynamic-update-slice_fusion.7
  328.4 2.6 bitcast_dynamic-update-slice_fusion.6
  331.0 2.6 bitcast_dynamic-update-slice_fusion.5
  333.6 41.1 %collective-permute-done.12 = bf16[320,2048]{1,0:T(8,128)(2,1)} collective-permute-done((bf16[320,2048]{1,0:T(8,128)(2,1)}, bf16[320,2048]{1,0:T(8,128)(2,1)}, u32[]{:S(2)}, u32[]{:S(2)}) %collective-permute-start.12) | collective-permute-done | bytes 1310752 | tf_op jit(solution)/shard_map/ppermute | solution.py:352
  374.7 6.0 all-to-all-done
  382.2 5.9 multiply_reduce_fusion.1
  390.9 4.1 bitcast_dynamic-update-slice_fusion.4
  395.0 2.8 bitcast_dynamic-update-slice_fusion.3
  397.8 2.6 bitcast_dynamic-update-slice_fusion.2
  400.4 23.0 %collective-permute-done.3 = bf16[320,2048]{1,0:T(8,128)(2,1)} collective-permute-done((bf16[320,2048]{1,0:T(8,128)(2,1)}, bf16[320,2048]{1,0:T(8,128)(2,1)}, u32[]{:S(2)}, u32[]{:S(2)}) %collective-permute-start.3) | collective-permute-done | bytes 1310752 | tf_op jit(solution)/shard_map/ppermute | solution.py:352
  423.4 31.5 %fusion.3.back = bf16[2560,2176]{1,0:T(8,128)(2,1)} fusion(bf16[2560,2048]{1,0:T(8,128)(2,1)} %bitcast.37, bf16[64,2048]{1,0:T(8,128)(2,1)S(1)} %broadcast_in_dim.130, bf16[1408,2048]{1,0:T(8,128)(2,1)} %bitcast.180, bf16[704,2048]{1,0:T(8,128)(2,1)} %param.29), kind=kOutput, calls=%fused_computation.16 | convolution fusion | flops 22843752448 | bytes 30539776 | tf_op jit(solution)/shard_map/dot_general | solution.py:19
  456.6 2.5 bitcast_dynamic-update-slice_fusion.16
  459.1 2.5 bitcast_dynamic-update-slice_fusion.15
  464.1 24.6 %collective-permute-done.7 = bf16[320,2048]{1,0:T(8,128)(2,1)S(1)} collective-permute-done((bf16[320,2048]{1,0:T(8,128)(2,1)S(1)}, bf16[320,2048]{1,0:T(8,128)(2,1)S(1)}, u32[]{:S(2)}, u32[]{:S(2)}) %collective-permute-start.7) | collective-permute-done | bytes 1310752 | tf_op jit(solution)/shard_map/ppermute | solution.py:352
  493.6 79.6 %shard_map.257 = (bf16[2560,2176]{1,0:T(8,128)(2,1)}, bf16[2560,4480]{1,0:T(8,128)(2,1)}) custom-call(bf16[2560,2048]{1,0:T(8,128)(2,1)} %bitcast.160, bf16[4480,2048]{1,0:T(8,128)(2,1)} %fusion.22.weights, bf16[2560,128]{1,0:T(8,128)(2,1)} %convert_element_type.118.chosen, bf16[128,2176]{1,0:T(8,128)(2,1)} %fusion.17.spread, bf16[2560,2176]{1,0:T(8,128)(2,1)} %fusion.3.back), custom_call_target="tpu_custom_call" | custom-call | flops 54999998464 | bytes 165000000 | tf_op jit(solution)/shard_map/pallas_call | solution.py:327
  573.2 30.6 %fusion.40 = bf16[2176,2048]{1,0:T(8,128)(2,1)} fusion(bf16[2560,2176]{1,0:T(8,128)(2,1)} %get-tuple-element.64, bf16[2560,2048]{1,0:T(8,128)(2,1)} %bitcast.37), kind=kOutput, calls=%fused_computation.115 | convolution fusion | flops 22817013760 | bytes 30539776 | tf_op jit(solution)/shard_map/dot_general | solution.py:19
  603.8 55.7 %fusion.41 = bf16[4480,2048]{1,0:T(8,128)(2,1)} fusion(bf16[2560,4480]{1,0:T(8,128)(2,1)} %get-tuple-element.63, bf16[2560,2048]{1,0:T(8,128)(2,1)} %bitcast.161), kind=kOutput, calls=%fused_computation.116 | convolution fusion | flops 46976204800 | bytes 51773440 | tf_op jit(solution)/shard_map/dot_general | solution.py:19
  659.6 58.4 %fusion.42 = bf16[2560,2048]{1,0:T(8,128)(2,1)} fusion(bf16[2560,4480]{1,0:T(8,128)(2,1)} %get-tuple-element.63, bf16[4480,2048]{1,0:T(8,128)(2,1)} %fusion.22.weights), kind=kOutput, calls=%fused_computation.117 | convolution fusion | flops 46976204800 | bytes 51773440 | tf_op jit(solution)/shard_map/dot_general | solution.py:19
  718.0 124.5 %all-reduce.6.cloned.1.call-done = bf16[2176,2048]{1,0:T(8,128)(2,1)} async-done(((bf16[2176,2048]{1,0:T(8,128)(2,1)}), bf16[2176,2048]{1,0:T(8,128)(2,1)}) %all-reduce.6.cloned.1.call-update) | async-done | bytes 8912912 | tf_op jit(solution)/shard_map/psum | solution.py:608
  842.5 3.0 fusion.7
  848.0 2.9 fusion.9
  852.4 7.5 fusion.15
  859.8 4.6 all-to-all-start.1
  864.5 32.2 %fusion.2 = bf16[2560,2048]{1,0:T(8,128)(2,1)} fusion(bf16[2560,2176]{1,0:T(8,128)(2,1)} %get-tuple-element.64, bf16[64,2048]{1,0:T(8,128)(2,1)S(1)} %copy-done.21, bf16[1408,2048]{1,0:T(8,128)(2,1)} %bitcast.181, bf16[704,2048]{1,0:T(8,128)(2,1)} %param.29), kind=kOutput, calls=%fused_computation.15 | convolution fusion | flops 22843752448 | bytes 30539776 | tf_op jit(solution)/shard_map/dot_general | solution.py:19
  896.7 7.2 fusion.18
  903.8 4.0 pad_maximum_fusion.1
  908.8 14.1 %copy.72 = bf16[2048,2560]{1,0:T(8,128)(2,1)} copy(bf16[2048,2560]{0,1:T(8,128)(2,1)} %bitcast.150) | data formatting | bytes 20971520 | tf_op jit(solution)/shard_map/dot_general | solution.py:19
  924.3 47.2 %shard_map.258 = (bf16[8,320,256]{2,1,0:T(8,128)(2,1)S(1)}, bf16[8,320,256]{2,1,0:T(8,128)(2,1)S(1)}, bf16[8,320,256]{2,1,0:T(8,128)(2,1)S(1)}, bf16[8,320,256]{...) custom-call(s32[2]{0:T(128)S(1)} %bitcast.145, bf16[8,320,256]{2,1,0:T(8,128)(2,1)} %copy-done.2, ...), custom_call_target="tpu_custom_call" | custom-call | tf_op jit(solution)/shard_map/pallas_call | solution.py:253
  974.9 2.8 reduce_sum.80
  977.8 3.3 pad_maximum_fusion.2
  981.1 6.5 copy.73
  987.6 12.7 fusion.43
  1000.5 132.6 %all_to_all.47 = bf16[8,272,3,1,256]{4,1,2,3,0:T(8,128)(2,1)S(1)} all-to-all(bf16[8,272,3,1,256]{4,1,2,3,0:T(8,128)(2,1)S(1)} %maximum_bitcast_fusion), channel_id=1, replica_groups=mesh['rep'=4,'fsdp'=8] {'fsdp'}, dimensions={0} | all-to-all | bytes 6684672 | tf_op jit(solution)/shard_map/all_to_all | solution.py:780
  1133.1 3.0 copy.75
  1136.0 6.0 reshape_squeeze.11
  1142.1 13.7 %fusion.44 = bf16[2560,2048]{1,0:T(8,128)(2,1)} fusion(bf16[2560,768]{1,0:T(8,128)(2,1)} %bitcast.55, bf16[2048,768]{1,0:T(8,128)(2,1)} %bitcast.187), kind=kOutput, calls=%fused_computation.119 | convolution fusion | flops 8053063680 | bytes 17563648 | tf_op jit(solution)/shard_map/dot_general | solution.py:19
  1155.7 29.2 %all-reduce.8.cloned.1.call-done = bf16[4480,2048]{1,0:T(8,128)(2,1)} async-done(((bf16[4480,2048]{1,0:T(8,128)(2,1)}), bf16[4480,2048]{1,0:T(8,128)(2,1)}) %all-reduce.8.cloned.1.call-update) | async-done | bytes 18350096 | tf_op jit(solution)/shard_map/psum | solution.py:608
  1186.6 5.3 slice.108
  1192.0 10.5 slice.110
  1205.6 5.8 copy-done.9
  1211.4 3.1 convert_bitcast_fusion
  1214.5 8.2 copy.77
  1222.7 8.8 convert_bitcast_fusion.1
  1231.5 3.5 add_convert_fusion
  1235.0 62.5 %all-reduce.10.cloned.1.call-done = (bf16[272,6144]{1,0:T(8,128)(2,1)}, bf16[256,2176]{0,1:T(8,128)(2,1)}) async-done(((bf16[272,6144]{1,0:T(8,128)(2,1)}, bf16[256,2176]{0,1:T(8,128)(2,1)}), (bf16[272,6144]{1,0:T(8,128)(2,1)}, bf16[256,2176]{0,1:T(8,128)(2,1)})) %all-reduce.10.cloned.1.call-update) | async-done | bytes 4456464 | tf_op jit(solution)/shard_map/psum | solution.py:789
  1298.5 2.7 slice_convert_fusion
  1301.2 2.9 copy.76
  1306.7 7.8 convert_multiply_fusion
  1316.7 3.5 fusion.13
  (205 shorter events, 60.8 us)
Async XLA Ops:
  8.0 4.5 copy-start
  8.0 5.2 copy-start.31
  8.0 5.4 copy-start.32
  8.0 5.4 copy-start.33
  8.1 5.4 copy-start.34
  14.1 155.0 %copy-start.16 = (bf16[320,2048]{1,0:T(8,128)(2,1)S(1)}, bf16[320,2048]{1,0:T(8,128)(2,1)}, u32[]{:S(2)}) copy-start(bf16[320,2048]{1,0:T(8,128)(2,1)} %param.20) | copy-start | bytes 3932164
  169.1 8.5 copy-start.26
  169.1 8.6 copy-start.27
  169.2 8.9 copy-start.7
  169.2 113.6 %collective-permute-start = (bf16[320,2048]{1,0:T(8,128)(2,1)S(1)}, bf16[320,2048]{1,0:T(8,128)(2,1)}, u32[]{:S(2)}, u32[]{:S(2)}) collective-permute-start(bf16[320,2048]{1,0:T(8,128)(2,1)S(1)} %copy-done.16), channel_id=1, source_target_pairs={{0,2},{1,3},{2,4},{3,5},{4,6},{5,7},{6,0},{7,1},{8,10},{9,11},{10,... | collective-permute-start | bytes 3932168 | tf_op jit(solution)/shard_map/ppermute | solution.py:352
  171.5 149.9 %collective-permute-start.9 = (bf16[320,2048]{1,0:T(8,128)(2,1)S(1)}, bf16[320,2048]{1,0:T(8,128)(2,1)}, u32[]{:S(2)}, u32[]{:S(2)}) collective-permute-start(bf16[320,2048]{1,0:T(8,128)(2,1)S(1)} %copy-done.16), channel_id=1, source_target_pairs={{0,1},{1,0},{2,3},{3,2},{4,5},{5,4},{6,7},{7,6},{8,9},{9,8},{10,11... | collective-permute-start | bytes 3932168 | tf_op jit(solution)/shard_map/ppermute | solution.py:363
  178.6 45.7 %copy-start.5 = (s32[10,1,256]{2,1,0:T(1,128)}, s32[10,1,256]{2,1,0:T(1,128)S(1)}, u32[]{:S(2)}) copy-start(s32[10,1,256]{2,1,0:T(1,128)S(1)} %reshape.258.at_row) | copy-start | bytes 30724
  193.7 6.9 copy-start.28
  199.8 7.8 copy-start.36
  267.4 1.1 copy-start.2
  268.5 1.1 copy-start.3
  269.6 1.1 copy-start.4
  270.7 118.8 %copy-start.22 = (f32[1,2,8,128]{3,1,2,0:T(2,128)}, f32[1,2,8,128]{3,1,2,0:T(2,128)S(1)}, u32[]{:S(2)}) copy-start(f32[1,2,8,128]{3,1,2,0:T(2,128)S(1)} %copy.82) | copy-start | bytes 24580
  282.8 33.3 %collective-permute-start.1 = (bf16[320,2048]{1,0:T(8,128)(2,1)}, bf16[320,2048]{1,0:T(8,128)(2,1)}, u32[]{:S(2)}, u32[]{:S(2)}) collective-permute-start(bf16[320,2048]{1,0:T(8,128)(2,1)} %collective-permute-done), channel_id=1, source_target_pairs={{0,2},{1,3},{2,4},{3,5},{4,6},{5,7},{6,0},{7,1},{8,10},{9,11},{10,... | collective-permute-start | bytes 3932168 | tf_op jit(solution)/shard_map/ppermute | solution.py:352
  293.5 34.9 %collective-permute-start.10 = (bf16[320,2048]{1,0:T(8,128)(2,1)}, bf16[320,2048]{1,0:T(8,128)(2,1)}, u32[]{:S(2)}, u32[]{:S(2)}) collective-permute-start(bf16[320,2048]{1,0:T(8,128)(2,1)} %collective-permute-done), channel_id=1, source_target_pairs={{0,1},{1,0},{2,3},{3,2},{4,5},{5,4},{6,7},{7,6},{8,9},{9,8},{10,11... | collective-permute-start | bytes 3932168 | tf_op jit(solution)/shard_map/ppermute | solution.py:363
  316.1 64.6 %all-to-all-start = ((bf16[8,320,256]{2,1,0:T(8,128)(2,1)}), bf16[8,320,256]{2,1,0:T(8,128)(2,1)}, u32[]{:S(2)}, u32[]{:S(2)}) async-start(bf16[8,320,256]{2,1,0:T(8,128)(2,1)} %bitcast.9), calls=%async_computation | async-start | bytes 2621440 | tf_op jit(solution)/shard_map/all_to_all | solution.py:712
  320.4 522.1 %all-reduce.6.cloned.1.call-start = ((), (), s32[]{:S(2)}) async-start(), calls=%async_computation.11 | async-start | bytes 17825792 | tf_op jit(solution)/shard_map/psum | solution.py:608
  323.9 50.8 %collective-permute-start.12 = (bf16[320,2048]{1,0:T(8,128)(2,1)}, bf16[320,2048]{1,0:T(8,128)(2,1)}, u32[]{:S(2)}, u32[]{:S(2)}) collective-permute-start(bf16[320,2048]{1,0:T(8,128)(2,1)} %collective-permute-done.1), channel_id=1, source_target_pairs={{0,2},{1,3},{2,4},{3,5},{4,6},{5,7},{6,0},{7,1},{8,10},{9,11},{10,... | collective-permute-start | bytes 3932168 | tf_op jit(solution)/shard_map/ppermute | solution.py:352
  328.4 53.8 %copy-start.11 = (bf16[320,2048]{1,0:T(8,128)(2,1)S(1)}, bf16[320,2048]{1,0:T(8,128)(2,1)}, u32[]{:S(2)}) copy-start(bf16[320,2048]{1,0:T(8,128)(2,1)} %token_.1) | copy-start | bytes 3932164
  328.4 62.5 %collective-permute-start.11 = (bf16[320,2048]{1,0:T(8,128)(2,1)}, bf16[320,2048]{1,0:T(8,128)(2,1)}, u32[]{:S(2)}, u32[]{:S(2)}) collective-permute-start(bf16[320,2048]{1,0:T(8,128)(2,1)} %collective-permute-done.1), channel_id=1, source_target_pairs={{0,1},{1,0},{2,3},{3,2},{4,5},{5,4},{6,7},{7,6},{8,9},{9,8},{10,11... | collective-permute-start | bytes 3932168 | tf_op jit(solution)/shard_map/ppermute | solution.py:363
  374.7 23.1 %collective-permute-start.13 = (bf16[320,2048]{1,0:T(8,128)(2,1)}, bf16[320,2048]{1,0:T(8,128)(2,1)}, u32[]{:S(2)}, u32[]{:S(2)}) collective-permute-start(bf16[320,2048]{1,0:T(8,128)(2,1)} %collective-permute-done.12), channel_id=1, source_target_pairs={{0,1},{1,0},{2,3},{3,2},{4,5},{5,4},{6,7},{7,6},{8,9},{9,8},{10,11... | collective-permute-start | bytes 3932168 | tf_op jit(solution)/shard_map/ppermute | solution.py:363
  382.2 6.0 copy-start.19
  388.2 12.2 copy-start.10
  388.2 1.4 copy-start.29
  390.9 32.4 %copy-start.15 = (bf16[8,320,2048]{2,1,0:T(8,128)(2,1)}, bf16[8,320,2048]{2,1,0:T(8,128)(2,1)S(1)}, u32[]{:S(2)}) copy-start(bf16[8,320,2048]{2,1,0:T(8,128)(2,1)S(1)} %get-tuple-element.160) | copy-start | bytes 31457284
  390.9 32.4 %collective-permute-start.3 = (bf16[320,2048]{1,0:T(8,128)(2,1)}, bf16[320,2048]{1,0:T(8,128)(2,1)}, u32[]{:S(2)}, u32[]{:S(2)}) collective-permute-start(bf16[320,2048]{1,0:T(8,128)(2,1)} %get-tuple-element.161), channel_id=1, source_target_pairs={{0,2},{1,3},{2,4},{3,5},{4,6},{5,7},{6,0},{7,1},{8,10},{9,11},{10,... | collective-permute-start | bytes 3932168 | tf_op jit(solution)/shard_map/ppermute | solution.py:352
  397.8 58.7 %collective-permute-start.2 = (bf16[320,2048]{1,0:T(8,128)(2,1)}, bf16[320,2048]{1,0:T(8,128)(2,1)}, u32[]{:S(2)}, u32[]{:S(2)}) collective-permute-start(bf16[320,2048]{1,0:T(8,128)(2,1)} %get-tuple-element.161), channel_id=1, source_target_pairs={{0,1},{1,0},{2,3},{3,2},{4,5},{5,4},{6,7},{7,6},{8,9},{9,8},{10,11... | collective-permute-start | bytes 3932168 | tf_op jit(solution)/shard_map/ppermute | solution.py:363
  423.4 38.3 %collective-permute-start.4 = (bf16[320,2048]{1,0:T(8,128)(2,1)}, bf16[320,2048]{1,0:T(8,128)(2,1)}, u32[]{:S(2)}, u32[]{:S(2)}) collective-permute-start(bf16[320,2048]{1,0:T(8,128)(2,1)} %collective-permute-done.3), channel_id=1, source_target_pairs={{0,1},{1,0},{2,3},{3,2},{4,5},{5,4},{6,7},{7,6},{8,9},{9,8},{10,11... | collective-permute-start | bytes 3932168 | tf_op jit(solution)/shard_map/ppermute | solution.py:363
  423.4 33.2 %collective-permute-start.5 = (bf16[320,2048]{1,0:T(8,128)(2,1)}, bf16[320,2048]{1,0:T(8,128)(2,1)S(1)}, u32[]{:S(2)}, u32[]{:S(2)}) collective-permute-start(bf16[320,2048]{1,0:T(8,128)(2,1)} %collective-permute-done.3), channel_id=1, source_target_pairs={{0,2},{1,3},{2,4},{3,5},{4,6},{5,7},{6,0},{7,1},{8,10},{9,11},{10,... | collective-permute-start | bytes 3932168 | tf_op jit(solution)/shard_map/ppermute | solution.py:352
  423.4 31.5 %copy-start.20 = (bf16[64,2048]{1,0:T(8,128)(2,1)}, bf16[64,2048]{1,0:T(8,128)(2,1)S(1)}, u32[]{:S(2)}) copy-start(bf16[64,2048]{1,0:T(8,128)(2,1)S(1)} %broadcast_in_dim.130) | copy-start | bytes 786436
  456.6 32.2 %collective-permute-start.7 = (bf16[320,2048]{1,0:T(8,128)(2,1)S(1)}, bf16[320,2048]{1,0:T(8,128)(2,1)S(1)}, u32[]{:S(2)}, u32[]{:S(2)}) collective-permute-start(bf16[320,2048]{1,0:T(8,128)(2,1)S(1)} %collective-permute-done.5), channel_id=1, source_target_pairs={{0,2},{1,3},{2,4},{3,5},{4,6},{5,7},{6,0},{7,1},{8,10},{9,11},{10,... | collective-permute-start | bytes 3932168 | tf_op jit(solution)/shard_map/ppermute | solution.py:352
  459.1 30.8 %collective-permute-start.6 = (bf16[320,2048]{1,0:T(8,128)(2,1)S(1)}, bf16[320,2048]{1,0:T(8,128)(2,1)S(1)}, u32[]{:S(2)}, u32[]{:S(2)}) collective-permute-start(bf16[320,2048]{1,0:T(8,128)(2,1)S(1)} %collective-permute-done.5), channel_id=1, source_target_pairs={{0,1},{1,0},{2,3},{3,2},{4,5},{5,4},{6,7},{7,6},{8,9},{9,8},{10,11... | collective-permute-start | bytes 3932168 | tf_op jit(solution)/shard_map/ppermute | solution.py:363
  488.8 3.6 collective-permute-start.8
  659.5 182.9 %reduce-scatter.5.cloned.1.call-start = ((), (), s32[]{:S(2)}) async-start(), calls=%async_computation.7 | async-start | bytes 11796480 | tf_op jit(solution)/shard_map/reduce_scatter | solution.py:743
  717.9 124.5 %copy-start.23 = (f32[1,2,8,128]{3,1,2,0:T(2,128)S(1)}, f32[1,2,8,128]{3,1,2,0:T(2,128)}, u32[]{:S(2)}) copy-start(f32[1,2,8,128]{3,1,2,0:T(2,128)} %copy-done.22) | copy-start | bytes 24580
  717.9 124.5 %copy-start.30 = (f32[320]{0:T(512)S(1)}, f32[320]{0:T(512)}, u32[]{:S(2)}) copy-start(f32[320]{0:T(512)} %copy-done.29) | copy-start | bytes 3844
  846.6 1.3 copy-start.17
  846.6 338.2 %all-reduce.8.cloned.1.call-start = ((), (), s32[]{:S(2)}) async-start(), calls=%async_computation.12 | async-start | bytes 36700160 | tf_op jit(solution)/shard_map/psum | solution.py:608
  850.9 1.5 copy-start.13
  852.4 12.1 copy-start.21
  859.8 36.8 %all-to-all-start.1 = ((bf16[320,8,256]{2,0,1:T(8,128)(2,1)}), bf16[320,8,256]{2,0,1:T(8,128)(2,1)S(1)}, u32[]{:S(2)}, u32[]{:S(2)}) async-start(bf16[320,8,256]{2,0,1:T(8,128)(2,1)} %fusion.15), calls=%async_computation.2 | async-start | bytes 2621440 | tf_op jit(solution)/shard_map/all_to_all | solution.py:754
  864.4 320.4 %reduce-scatter.11.cloned.1.call-start = ((), (), s32[]{:S(2)}) async-start(), calls=%async_computation.10 | async-start | bytes 10027008 | tf_op jit(solution)/shard_map/reduce_scatter | solution.py:766
  896.7 7.2 copy-start.18
  907.9 323.6 %reduce-scatter.7.cloned.1.call-start = ((), (), s32[]{:S(2)}) async-start(), calls=%async_computation.8 | async-start | bytes 11796480 | tf_op jit(solution)/shard_map/reduce_scatter | solution.py:764
  908.5 389.0 %all-reduce.10.cloned.1.call-start = ((), (), s32[]{:S(2)}) async-start(), calls=%async_computation.13 | async-start | bytes 8912896 | tf_op jit(solution)/shard_map/psum | solution.py:789
  908.7 14.1 %copy-start.25 = (f32[8,320]{1,0:T(8,128)S(1)}, f32[8,320]{1,0:T(8,128)}, u32[]{:S(2)}) copy-start(f32[8,320]{1,0:T(8,128)} %copy-done.24) | copy-start | bytes 30724
  908.7 15.6 %copy-start.6 = (s32[10,1,256]{2,1,0:T(1,128)S(1)}, s32[10,1,256]{2,1,0:T(1,128)}, u32[]{:S(2)}) copy-start(s32[10,1,256]{2,1,0:T(1,128)} %copy-done.5) | copy-start | bytes 30724
  908.8 15.6 %copy-start.8 = (s32[1,2]{1,0:T(1,128)S(1)}, s32[1,2]{1,0:T(1,128)}, u32[]{:S(2)}) copy-start(s32[1,2]{1,0:T(1,128)} %param.17) | copy-start | bytes 28
  1184.9 0.8 copy-start.35
  1184.9 1.3 copy-start.12
  1184.9 129.6 %reduce-scatter.9.cloned.1.call-start = ((), (), s32[]{:S(2)}) async-start(), calls=%async_computation.9 | async-start | bytes 11796480 | tf_op jit(solution)/shard_map/reduce_scatter | solution.py:798
  1186.6 15.9 %slice-start = ((s8[18350080]{0:T(1024)(128)(4,1)}), s8[4194304]{0:T(1024)(128)(4,1)S(1)}, s32[]{:S(2)}) async-start(s8[18350080]{0:T(1024)(128)(4,1)} %bitcast.153), calls=%async_computation.14 | async-start | bytes 8388608
  1186.6 15.9 %slice-start.1 = ((s8[18350080]{0:T(1024)(128)(4,1)}), s8[4194304]{0:T(1024)(128)(4,1)S(1)}, s32[]{:S(2)}) async-start(s8[18350080]{0:T(1024)(128)(4,1)} %bitcast.153), calls=%async_computation.15 | async-start | bytes 8388608
  1192.0 10.5 slice-start.2
  1192.0 10.5 slice-start.3
  1192.0 10.5 slice-start.4
  1204.7 6.7 copy-start.9
  1314.5 2.1 copy-start.14
  1316.6 3.6 copy-start.1
  (1 other events, 0.6 us)
Sparse Core Ops, SparseCore 0:
  659.6 182.7 all-reduce.5
  851.4 333.3 all-reduce.7
  1188.9 108.5 all-reduce.9
Sparse Core Ops, SparseCore 1:
  718.1 112.3 reduce-scatter.4
  908.0 95.0 reduce-scatter.10
  1005.3 161.0 reduce-scatter.6
  1188.0 109.2 reduce-scatter.8

commit v2 on v1

--- a/solution.py
+++ b/solution.py
@@ -42,15 +42,21 @@
     return (jnp.cos(angle), jnp.sin(angle))
 
 
-def pair_block(ref, index, size):
-    block = ref[:, pl.ds(pl.multiple_of(index * size, size), size), :]
-    return block.reshape(block.shape[0] * size, block.shape[2])
-
-
-def put_block(ref, index, size, block):
-    ref[:, pl.ds(pl.multiple_of(index * size, size), size), :] = block.reshape(
-        ref.shape[0], size, block.shape[1]
-    )
+def pair_block(ref, index, size, head=0):
+    block = ref[
+        :,
+        pl.ds(pl.multiple_of(index * size, size), size),
+        head * HEAD_DIM : (head + 1) * HEAD_DIM,
+    ]
+    return block.reshape(block.shape[0] * size, HEAD_DIM)
+
+
+def put_block(ref, index, size, block, head=0):
+    ref[
+        :,
+        pl.ds(pl.multiple_of(index * size, size), size),
+        head * HEAD_DIM : (head + 1) * HEAD_DIM,
+    ] = block.reshape(ref.shape[0], size, HEAD_DIM)
 
 
 def first_block(first_length, index, width):
@@ -64,10 +70,9 @@
 
 def attend_kernel(
     size,
+    held,
     lengths,
-    query_in,
-    key_in,
-    value_in,
+    projected,
     cosine,
     sine,
     at_col,
@@ -78,36 +83,43 @@
     out,
     log_total,
 ):
-    devices, rows, _ = query_in.shape
+    devices, rows, _ = projected.shape
     width = size * devices
     first_length = lengths[0]
     factor = HEAD_DIM ** (-0.5)
 
     def prepare(index, carry):
         wave, ripple = pair_block(cosine, index, size), pair_block(sine, index, size)
-        for source, target in ((query_in, query), (key_in, keyed)):
-            block = pair_block(source, index, size)
-            block = block * wave + pltpu.roll(block, HEAD_DIM // 2, 1) * ripple
-            put_block(target, index, size, block.astype(LOW))
-        put_block(value, index, size, pair_block(value_in, index, size).astype(LOW))
+        for head in range(held):
+            for place, target in ((0, query), (held, keyed)):
+                block = pair_block(projected, index, size, place + head)
+                block = block * wave + pltpu.roll(block, HEAD_DIM // 2, 1) * ripple
+                put_block(target, index, size, block.astype(LOW), head)
+            block = pair_block(projected, index, size, 2 * held + head)
+            put_block(value, index, size, block.astype(LOW), head)
         return carry
 
     lax.fori_loop(0, rows // size, prepare, 0)
 
     def for_queries(index, carry):
-        block = pair_block(query, index, size)
+        blocks = [pair_block(query, index, size, head) for head in range(held)]
         places = pair_block(at_col, index, size)[:, :1]
 
-        def for_keys(other, state):
-            peak, total, summed = state
-            raw = mm_nt(block, pair_block(keyed, other, size)) * factor
-            raw = jnp.where(span_mask(places, at_row[other], first_length), raw, NEG)
-            higher = jnp.maximum(peak, jnp.max(raw, axis=1, keepdims=True))
-            lifted = jnp.exp(raw - higher)
-            fade = jnp.exp(peak - higher)
-            total = total * fade + jnp.sum(lifted, axis=1, keepdims=True)
-            summed = summed * fade + mm(lifted.astype(LOW), pair_block(value, other, size))
-            return higher, total, summed
+        def for_keys(other, states):
+            seen = span_mask(places, at_row[other], first_length)
+            out_states = []
+            for head, (peak, total, summed) in enumerate(states):
+                raw = mm_nt(blocks[head], pair_block(keyed, other, size, head)) * factor
+                raw = jnp.where(seen, raw, NEG)
+                higher = jnp.maximum(peak, jnp.max(raw, axis=1, keepdims=True))
+                lifted = jnp.exp(raw - higher)
+                fade = jnp.exp(peak - higher)
+                total = total * fade + jnp.sum(lifted, axis=1, keepdims=True)
+                summed = summed * fade + mm(
+                    lifted.astype(LOW), pair_block(value, other, size, head)
+                )
+                out_states.append((higher, total, summed))
+            return tuple(out_states)
 
         start = (
             jnp.full((width, 1), 2 * NEG, WIDE),
@@ -115,11 +127,11 @@
             jnp.zeros((width, HEAD_DIM), WIDE),
         )
         lowest = first_block(first_length, index, width)
-        peak, total, summed = lax.fori_loop(lowest, index + 1, for_keys, start)
-        put_block(out, index, size, (summed / total).astype(LOW))
-        put_block(
-            log_total, index, size, jnp.broadcast_to(peak + jnp.log(total), (width, HEAD_DIM))
-        )
+        states = lax.fori_loop(lowest, index + 1, for_keys, (start,) * held)
+        for head, (peak, total, summed) in enumerate(states):
+            put_block(out, index, size, (summed / total).astype(LOW), head)
+            logs = jnp.broadcast_to(peak + jnp.log(total), (width, HEAD_DIM))
+            put_block(log_total, index, size, logs, head)
         return carry
 
     lax.fori_loop(0, rows // size, for_queries, 0)
@@ -127,6 +139,7 @@
 
 def attend_back_kernel(
     size,
+    held,
     lengths,
     query,
     keyed,
@@ -139,12 +152,8 @@
     scale_row,
     at_col,
     at_row,
-    query_back,
-    key_back,
-    value_back,
-    query_scaled,
-    key_scaled,
-    value_scaled,
+    projected_back,
+    scaled_back,
     query_sum,
     key_sum,
     value_sum,
@@ -157,32 +166,39 @@
     value_sum[...] = jnp.zeros_like(value_sum)
 
     def for_queries(index, carry):
-        block = pair_block(query, index, size)
         places = pair_block(at_col, index, size)[:, :1]
-        logs = pair_block(log_total, index, size)[:, :1]
-        pushed = pair_block(attended_back, index, size)
-        row_dot = jnp.sum(
-            pushed.astype(WIDE) * pair_block(attended, index, size).astype(WIDE),
-            axis=1,
-            keepdims=True,
-        )
-
-        def for_keys(other, summed):
-            key_block = pair_block(keyed, other, size)
-            raw = mm_nt(block, key_block) * factor
-            raw = jnp.where(span_mask(places, at_row[other], first_length), raw, NEG)
-            probs = jnp.exp(raw - logs)
-            prob_back = mm_nt(pushed, pair_block(value, other, size))
-            score_back = (probs * (prob_back - row_dot)).astype(LOW)
+        held_now = []
+        for head in range(held):
+            pushed = pair_block(attended_back, index, size, head)
+            row_dot = jnp.sum(
+                pushed.astype(WIDE) * pair_block(attended, index, size, head).astype(WIDE),
+                axis=1,
+                keepdims=True,
+            )
+            logs = pair_block(log_total, index, size, head)[:, :1]
+            held_now.append((pair_block(query, index, size, head), pushed, row_dot, logs))
+
+        def for_keys(other, sums):
+            seen = span_mask(places, at_row[other], first_length)
             here = pl.ds(pl.multiple_of(other * width, width), width)
-            value_sum[here, :] += mm_tn(probs.astype(LOW), pushed)
-            key_sum[here, :] += mm_tn(score_back, block)
-            return summed + mm(score_back, key_block)
+            out_sums = []
+            for head, (block, pushed, row_dot, logs) in enumerate(held_now):
+                key_block = pair_block(keyed, other, size, head)
+                raw = jnp.where(seen, mm_nt(block, key_block) * factor, NEG)
+                probs = jnp.exp(raw - logs)
+                prob_back = mm_nt(pushed, pair_block(value, other, size, head))
+                score_back = (probs * (prob_back - row_dot)).astype(LOW)
+                value_sum[head, here, :] += mm_tn(probs.astype(LOW), pushed)
+                key_sum[head, here, :] += mm_tn(score_back, block)
+                out_sums.append(sums[head] + mm(score_back, key_block))
+            return tuple(out_sums)
 
         lowest = first_block(first_length, index, width)
-        query_sum[pl.ds(pl.multiple_of(index * width, width), width), :] = lax.fori_loop(
-            lowest, index + 1, for_keys, jnp.zeros((width, HEAD_DIM), WIDE)
-        )
+        start = (jnp.zeros((width, HEAD_DIM), WIDE),) * held
+        sums = lax.fori_loop(lowest, index + 1, for_keys, start)
+        here = pl.ds(pl.multiple_of(index * width, width), width)
+        for head in range(held):
+            query_sum[head, here, :] = sums[head]
         return carry
 
     lax.fori_loop(0, rows // size, for_queries, 0)
@@ -191,55 +207,36 @@
         wave, ripple = pair_block(cosine, index, size), pair_block(sine, index, size)
         scale = pair_block(scale_row, index, size)[:, :1]
         here = pl.ds(pl.multiple_of(index * width, width), width)
-        for source, target, scaled in (
-            (query_sum, query_back, query_scaled),
-            (key_sum, key_back, key_scaled),
-        ):
-            block = source[here, :] * factor
-            block = block * wave - pltpu.roll(block, HEAD_DIM // 2, 1) * ripple
-            block = block.astype(LOW)
-            put_block(target, index, size, block)
-            put_block(scaled, index, size, (block.astype(WIDE) * scale).astype(LOW))
-        block = value_sum[here, :].astype(LOW)
-        put_block(value_back, index, size, block)
-        put_block(value_scaled, index, size, (block.astype(WIDE) * scale).astype(LOW))
+        for head in range(held):
+            for place, source in ((0, query_sum), (held, key_sum)):
+                block = source[head, here, :] * factor
+                block = block * wave - pltpu.roll(block, HEAD_DIM // 2, 1) * ripple
+                block = block.astype(LOW)
+                put_block(projected_back, index, size, block, place + head)
+                put_block(
+                    scaled_back, index, size, (block.astype(WIDE) * scale).astype(LOW), place + head
+                )
+            block = value_sum[head, here, :].astype(LOW)
+            put_block(projected_back, index, size, block, 2 * held + head)
+            block = (block.astype(WIDE) * scale).astype(LOW)
+            put_block(scaled_back, index, size, block, 2 * held + head)
         return carry
 
     lax.fori_loop(0, rows // size, finish, 0)
-
-
-def work(micros):
-    return pl.CostEstimate(
-        flops=int(micros * 1e9), bytes_accessed=int(micros * 3e6), transcendentals=0
-    )
-
-
-def head_spec(devices, rows, first):
-    return pl.BlockSpec((devices, rows, HEAD_DIM), lambda head: (0, 0, first + head))
 
 
 def attend(lengths, projected, cosine, sine, at_col, at_row, held, size):
     devices, rows, _ = projected.shape
-    whole = pl.BlockSpec((devices, rows, HEAD_DIM), lambda head: (0, 0, 0))
     low = jax.ShapeDtypeStruct((devices, rows, held * HEAD_DIM), LOW)
+    inside = pl.BlockSpec(memory_space=pltpu.VMEM)
     return pl.pallas_call(
-        functools.partial(attend_kernel, size),
-        grid=(held,),
-        in_specs=[
-            pl.BlockSpec(memory_space=pltpu.SMEM),
-            head_spec(devices, rows, 0),
-            head_spec(devices, rows, held),
-            head_spec(devices, rows, 2 * held),
-            whole,
-            whole,
-            whole,
-            pl.BlockSpec(at_row.shape, lambda head: (0, 0, 0)),
-        ],
-        out_specs=[head_spec(devices, rows, 0)] * 5,
+        functools.partial(attend_kernel, size, held),
+        in_specs=[pl.BlockSpec(memory_space=pltpu.SMEM)] + [inside] * 5,
+        out_specs=[inside] * 5,
         out_shape=[low] * 4 + [jax.ShapeDtypeStruct(low.shape, WIDE)],
         cost_estimate=work(30),
-        compiler_params=pltpu.CompilerParams(vmem_limit_bytes=48 * 2**20),
-    )(lengths, projected, projected, projected, cosine, sine, at_col, at_row)
+        compiler_params=pltpu.CompilerParams(vmem_limit_bytes=56 * 2**20),
+    )(lengths, projected, cosine, sine, at_col, at_row)
 
 
 def attend_back(
@@ -247,52 +244,80 @@
     at_col, at_row, held, size,
 ):
     devices, rows, _ = query.shape
-    whole = pl.BlockSpec((devices, rows, HEAD_DIM), lambda head: (0, 0, 0))
-    own = head_spec(devices, rows, 0)
-    low = jax.ShapeDtypeStruct((devices, rows, held * HEAD_DIM), LOW)
+    low = jax.ShapeDtypeStruct((devices, rows, 3 * held * HEAD_DIM), LOW)
+    inside = pl.BlockSpec(memory_space=pltpu.VMEM)
     return pl.pallas_call(
-        functools.partial(attend_back_kernel, size),
-        grid=(held,),
-        in_specs=[
-            pl.BlockSpec(memory_space=pltpu.SMEM),
-            own,
-            own,
-            own,
-            own,
-            own,
-            own,
-            whole,
-            whole,
-            whole,
-            whole,
-            pl.BlockSpec(at_row.shape, lambda head: (0, 0, 0)),
-        ],
-        out_specs=[own] * 6,
-        out_shape=[low] * 6,
-        scratch_shapes=[pltpu.VMEM((devices * rows, HEAD_DIM), WIDE)] * 3,
-        compiler_params=pltpu.CompilerParams(vmem_limit_bytes=48 * 2**20),
+        functools.partial(attend_back_kernel, size, held),
+        in_specs=[pl.BlockSpec(memory_space=pltpu.SMEM)] + [inside] * 11,
+        out_specs=[inside] * 2,
+        out_shape=[low] * 2,
+        cost_estimate=work(1),
+        scratch_shapes=[pltpu.VMEM((held, devices * rows, HEAD_DIM), WIDE)] * 3,
+        compiler_params=pltpu.CompilerParams(vmem_limit_bytes=56 * 2**20),
     )(
         lengths, query, keyed, value, attended, pushed, log_total, cosine, sine, scale_row,
         at_col, at_row,
     )
 
 
+def work(micros):
+    return pl.CostEstimate(
+        flops=int(micros * 1e9), bytes_accessed=int(micros * 3e6), transcendentals=0
+    )
+
+
 def chunks_of(total):
     return [(start, min(256, total - start)) for start in range(0, total, 256)]
 
 
-def middle_kernel(
-    experts, hidden, weights, chosen, spread, back, act_out, grad_out, strengths
-):
+def ring_blocks(block, devices, first, last):
+    ring = [(i, (i + 2) % devices) for i in range(devices)]
+    blocks = [block]
+    for _ in range(first, last):
+        blocks.append(lax.ppermute(blocks[-1], "fsdp", ring))
+    return blocks
+
+
+def ring_place(blocks, devices):
+    mine = lax.axis_index("fsdp")
+    twin = [(i, i ^ 1) for i in range(devices)]
+    whole = jnp.zeros((devices,) + blocks[0].shape, blocks[0].dtype)
+    for step, block in enumerate(blocks):
+        owner = lax.rem(mine + devices - 2 * step, devices)
+        whole = lax.dynamic_update_index_in_dim(whole, block, owner, 0)
+        other = lax.ppermute(block, "fsdp", twin)
+        whole = lax.dynamic_update_index_in_dim(whole, other, owner ^ 1, 0)
+    return whole
+
+
+def remote(source, target, sent, arrived, where):
+    return pltpu.make_async_remote_copy(
+        src_ref=source,
+        dst_ref=target,
+        send_sem=sent,
+        recv_sem=arrived,
+        device_id=where,
+        device_id_type=pl.DeviceIdType.MESH,
+    )
+
+
+def open_kernel(peers):
+    barrier = pltpu.get_barrier_semaphore()
+    for peer in peers:
+        pl.semaphore_signal(
+            barrier, inc=1, device_id=peer, device_id_type=pl.DeviceIdType.MESH
+        )
+    pl.semaphore_wait(barrier, len(peers))
+
+
+def middle_block(experts, rows, cot, weights, weight_down, named, spread, act_out, grad_out, strengths):
     total = act_out.shape[1]
-    rows = hidden[...]
     lane = lax.broadcasted_iota(jnp.int32, (rows.shape[0], 128), 1)
     logits = mm_nt(rows, weights[2 * total :, :])
     sigma = jax.nn.sigmoid(logits)
     masked = jnp.where((lane >= 1) & (lane <= experts), logits, NEG)
     lifted = jnp.exp(masked - jnp.max(masked, axis=1, keepdims=True))
     normal = lifted / jnp.sum(lifted, axis=1, keepdims=True)
-    named = chosen[...].astype(WIDE)
     strength = jnp.where(lane == 0, sigma, normal * named)
     high = strength.astype(LOW)
     rest = (strength - high.astype(WIDE)).astype(LOW)
@@ -301,8 +326,8 @@
         here = pl.ds(start, size)
         gate = mm_nt(rows, weights[start : start + size, :])
         up = mm_nt(rows, weights[total + start : total + start + size, :])
+        pushed = mm_nt(cot, weight_down[start : start + size, :])
         wide = mm(high, spread[:, here]) + mm(rest, spread[:, here])
-        pushed = back[:, here].astype(WIDE)
         curve = jax.nn.sigmoid(gate)
         silu = gate * curve
         act = silu * up
@@ -318,71 +343,123 @@
     grad_out[:, 2 * total :] = logit_grad.astype(LOW)
 
 
-def middle(hidden, weights, chosen, spread, back, experts):
-    group, width = hidden.shape
-    total = back.shape[1]
-    rows = group // 5
-    by_rows = lambda columns: pl.BlockSpec((rows, columns), lambda i: (i, 0))
-    held = lambda shape: pl.BlockSpec(shape, lambda i: (0, 0), pipeline_mode=pl.Buffered(1))
+def middle_kernel(
+    devices,
+    experts,
+    hidden,
+    cot_all,
+    weights_far,
+    down_far,
+    chosen,
+    spread,
+    hidden_all,
+    act_all,
+    grad_all,
+    weights,
+    weight_down,
+    strengths,
+    ring_sent,
+    ring_got,
+    twin_sent,
+    twin_got,
+    local_done,
+):
+    mine = lax.axis_index("fsdp")
+    steps = devices // 2
+    rows, width = hidden.shape
+    total = act_all.shape[2]
+    right = lax.rem(mine + 2, devices)
+    left = lax.rem(mine + devices - 2, devices)
+    twin = mine + 1 - 2 * lax.rem(mine, 2)
+    open_kernel([{"fsdp": right}, {"fsdp": left}, {"fsdp": twin}])
+    loads = [
+        pltpu.make_async_copy(hidden, hidden_all.at[mine], local_done.at[0]),
+        pltpu.make_async_copy(weights_far, weights, local_done.at[1]),
+        pltpu.make_async_copy(down_far, weight_down, local_done.at[2]),
+    ]
+    for one in loads:
+        one.start()
+    loads[0].wait()
+
+    def along(s, where, sent, got):
+        block = hidden_all.at[lax.rem(mine + devices - 2 * s, devices)]
+        return remote(block, block, sent.at[s], got.at[s], {"fsdp": where})
+
+    def body(rows_in, cot_in, named, act_out, grad_out):
+        middle_block(
+            experts,
+            rows_in[0],
+            cot_in[0],
+            weights,
+            weight_down,
+            named[0].astype(WIDE),
+            spread,
+            act_out.at[0],
+            grad_out.at[0],
+            strengths,
+        )
+
+    def step(s, carry):
+        @pl.when(s > 0)
+        def _():
+            along(s - 1, right, ring_sent, ring_got).wait_recv()
+
+        @pl.when(s < steps - 1)
+        def _():
+            along(s, right, ring_sent, ring_got).start()
+
+        along(s, twin, twin_sent, twin_got).start()
+        along(s, twin, twin_sent, twin_got).wait_recv()
+
+        @pl.when(s == 0)
+        def _():
+            loads[1].wait()
+            loads[2].wait()
+
+        first = lax.rem(mine - lax.rem(mine, 2) + devices - 2 * s, devices)
+        by_rows = lambda columns: pl.BlockSpec((1, rows, columns), lambda i: (first + i, 0, 0))
+        pltpu.emit_pipeline(
+            body,
+            grid=(2,),
+            in_specs=[by_rows(width), by_rows(width), by_rows(128)],
+            out_specs=[by_rows(total), by_rows(2 * total + 128)],
+        )(hidden_all, cot_all, chosen, act_all, grad_all)
+        return carry
+
+    lax.fori_loop(0, steps, step, 0)
+    for s in range(steps):
+        if s < steps - 1:
+            along(s, right, ring_sent, ring_got).wait_send()
+        along(s, twin, twin_sent, twin_got).wait_send()
+
+
+def middle(hidden, cot_all, weights, weight_down, chosen, spread, experts):
+    devices, rows, width = cot_all.shape
+    total = weight_down.shape[0]
+    dma = pltpu.SemaphoreType.DMA
+    anywhere = pl.BlockSpec(memory_space=pl.ANY)
+    inside = pl.BlockSpec(memory_space=pltpu.VMEM)
+    low = lambda columns: jax.ShapeDtypeStruct((devices, rows, columns), LOW)
     return pl.pallas_call(
-        functools.partial(middle_kernel, experts),
-        grid=(group // rows,),
-        in_specs=[
-            by_rows(width),
-            held(weights.shape),
-            by_rows(128),
-            held(spread.shape),
-            by_rows(total),
+        functools.partial(middle_kernel, devices, experts),
+        in_specs=[inside, anywhere, anywhere, anywhere, anywhere, inside],
+        out_specs=[anywhere] * 3,
+        out_shape=[low(width), low(total), low(2 * total + 128)],
+        scratch_shapes=[
+            pltpu.VMEM(weights.shape, LOW),
+            pltpu.VMEM(weight_down.shape, LOW),
+            pltpu.VMEM((rows, 128), WIDE),
+            dma((devices // 2,)),
+            dma((devices // 2,)),
+            dma((devices // 2,)),
+            dma((devices // 2,)),
+            dma((3,)),
         ],
-        out_specs=[by_rows(total), by_rows(weights.shape[0])],
-        out_shape=[
-            jax.ShapeDtypeStruct((group, total), LOW),
-            jax.ShapeDtypeStruct((group, weights.shape[0]), LOW),
-        ],
-        scratch_shapes=[pltpu.VMEM((rows, 128), WIDE)],
-        cost_estimate=work(55),
-        compiler_params=pltpu.CompilerParams(vmem_limit_bytes=58 * 2**20),
-    )(hidden, weights, chosen, spread, back)
-
-
-def ring_blocks(block, devices, first, last):
-    ring = [(i, (i + 2) % devices) for i in range(devices)]
-    blocks = [block]
-    for _ in range(first, last):
-        blocks.append(lax.ppermute(blocks[-1], "fsdp", ring))
-    return blocks
-
-
-def ring_place(blocks, devices):
-    mine = lax.axis_index("fsdp")
-    twin = [(i, i ^ 1) for i in range(devices)]
-    whole = jnp.zeros((devices,) + blocks[0].shape, blocks[0].dtype)
-    for step, block in enumerate(blocks):
-        owner = lax.rem(mine + devices - 2 * step, devices)
-        whole = lax.dynamic_update_index_in_dim(whole, block, owner, 0)
-        other = lax.ppermute(block, "fsdp", twin)
-        whole = lax.dynamic_update_index_in_dim(whole, other, owner ^ 1, 0)
-    return whole
-
-
-def remote(source, target, sent, arrived, where):
-    return pltpu.make_async_remote_copy(
-        src_ref=source,
-        dst_ref=target,
-        send_sem=sent,
-        recv_sem=arrived,
-        device_id=where,
-        device_id_type=pl.DeviceIdType.MESH,
-    )
-
-
-def open_kernel(peers):
-    barrier = pltpu.get_barrier_semaphore()
-    for peer in peers:
-        pl.semaphore_signal(
-            barrier, inc=1, device_id=peer, device_id_type=pl.DeviceIdType.MESH
-        )
-    pl.semaphore_wait(barrier, len(peers))
+        cost_estimate=work(110),
+        compiler_params=pltpu.CompilerParams(
+            collective_id=1, has_side_effects=True, vmem_limit_bytes=60 * 2**20
+        ),
+    )(hidden, cot_all, weights, weight_down, chosen, spread)
 
 
 def gather_kernel(
@@ -466,6 +543,24 @@
             {"fsdp": right},
         ).wait_recv()
 
+    shared = {}
+
+    def share_cross(s):
+        source = share if s == 0 else share_all.at[owners[s], copy]
+        for k in range(1, reps):
+            shared[k, s] = begin(
+                remote(
+                    source,
+                    share_all.at[owners[s], copy],
+                    share_sent.at[k - 1, s],
+                    share_got.at[k - 1, s],
+                    {"rep": lax.rem(copy + k, reps)},
+                )
+            )
+
+    ring_step(1, 0)
+    ring_step(2, 0)
+    ring_step(0, 0)
     deals = []
     for k in range(1, devices):
         peer = lax.rem(mine + k, devices)
@@ -480,16 +575,14 @@
                 )
             )
         )
-    ring_step(1, 0)
-    ring_step(2, 0)
-    ring_step(0, 0)
+    share_cross(0)
     for one in locals_:
         one.start()
     for s in range(1, steps):
         for j in (1, 2):
             ring_wait(j, s - 1)
             ring_step(j, s)
-
+        share_cross(s)
     if steps > 1:
         ring_wait(0, 0)
         ring_step(0, 1)
@@ -509,28 +602,13 @@
                 )
             )
         )
-    shared = []
-    for k in range(1, reps):
-        for s in range(steps):
-            source = share if s == 0 else share_all.at[owners[s], copy]
-            shared.append(
-                begin(
-                    remote(
-                        source,
-                        share_all.at[owners[s], copy],
-                        share_sent.at[k - 1, s],
-                        share_got.at[k - 1, s],
-                        {"rep": lax.rem(copy + k, reps)},
-                    )
-                )
-            )
     if steps > 2:
         ring_wait(0, 1)
         ring_step(0, 2)
-    for k in range(1, reps):
-        origin = lax.rem(copy + reps - k, reps)
-        for s in range(steps):
-            shared[(k - 1) * steps + s].wait_recv()
+    for s in range(steps):
+        for k in range(1, reps):
+            origin = lax.rem(copy + reps - k, reps)
+            shared[k, s].wait_recv()
             begin(
                 remote(
                     share_all.at[owners[s], origin],
@@ -660,7 +738,7 @@
     small = small.reshape(devices, -1)[:, :length]
     cot_in, _ = lax.optimization_barrier((cotangent, token_all))
     steps = devices // 2
-    cot_blocks = ring_blocks(cot_in, devices, 0, steps // 2)
+    cot_blocks = ring_blocks(cot_in, devices, 0, 1)
 
     gain_two = small[:, :part].reshape(width).astype(WIDE)
     gate_weight = small[:, part : 2 * part].reshape(width, 1)
@@ -670,7 +748,32 @@
     choice_weight = jnp.concatenate(
         [gate_weight, router, jnp.zeros((width, 127 - experts), LOW)], axis=1
     )
+    scale_all = scale_of(token_all.astype(WIDE))
+    projected = scale_all * mm(token_all, weight_mine) + bias_mine
+    first_length = lengths[0, 0]
+    second = (dealing >= first_length).astype(jnp.int32)
+    cosine, sine = rope_tables(dealing - second * first_length)
+    shape = (devices, rows, HEAD_DIM)
+    cosine = jnp.concatenate([cosine, cosine], axis=1).reshape(shape)
+    sine = jnp.concatenate([-sine, sine], axis=1).reshape(shape)
+    size = 256 // devices
+    at_col = jnp.broadcast_to(dealing.reshape(devices, rows, 1), shape)
+    at_row = dealing.reshape(devices, rows // size, size).transpose(1, 0, 2)
+    at_row = at_row.reshape(rows // size, 1, devices * size)
+    scale_row = jnp.broadcast_to(scale_all.reshape(devices, rows, 1), shape)
+    projected, first_step = lax.optimization_barrier((projected, cot_blocks[1]))
+    cot_blocks = [cot_blocks[0]] + ring_blocks(first_step, devices, 1, steps // 2)
+    query, keyed, value, attended_mine, log_total = attend(
+        lengths[0], projected.reshape(devices, rows, 3 * part), cosine, sine, at_col, at_row,
+        held, size,
+    )
+    attended = attended_mine.reshape(group, part)
+    cot_blocks = cot_blocks[:-1] + ring_blocks(cot_blocks[-1], devices, steps // 2, steps - 1)
+    cot_all = ring_place(cot_blocks, devices).reshape(group, width)
     full = -(-total // 128) * 128
+    shared_in, shared_out, expert_in, expert_out, _ = lax.optimization_barrier(
+        (shared_in, shared_out, expert_in, expert_out, attended_mine)
+    )
     expert_rows = expert_in.transpose(0, 1, 3, 2)
     expert_down = expert_out
     if hidden > units:
@@ -687,37 +790,12 @@
         [shared_out, expert_down.reshape(experts * hidden, width), fill], axis=0
     )
 
-    scale_all = scale_of(token_all.astype(WIDE))
-    projected = scale_all * mm(token_all, weight_mine) + bias_mine
-    first_length = lengths[0, 0]
-    second = (dealing >= first_length).astype(jnp.int32)
-    cosine, sine = rope_tables(dealing - second * first_length)
-    shape = (devices, rows, HEAD_DIM)
-    cosine = jnp.concatenate([cosine, cosine], axis=1).reshape(shape)
-    sine = jnp.concatenate([-sine, sine], axis=1).reshape(shape)
-    size = 256 // devices
-    at_col = jnp.broadcast_to(dealing.reshape(devices, rows, 1), shape)
-    at_row = dealing.reshape(devices, rows // size, size).transpose(1, 0, 2)
-    at_row = at_row.reshape(rows // size, 1, devices * size)
-    scale_row = jnp.broadcast_to(scale_all.reshape(devices, rows, 1), shape)
-    query, keyed, value, attended_mine, log_total = attend(
-        lengths[0], projected.reshape(devices, rows, 3 * part), cosine, sine, at_col, at_row,
-        held, size,
-    )
-    attended, halfway = lax.optimization_barrier(
-        (attended_mine.reshape(group, part), cot_blocks[-1])
-    )
-    cot_blocks = cot_blocks[:-1] + ring_blocks(halfway, devices, steps // 2, steps - 1)
-    cot_all = ring_place(cot_blocks, devices).reshape(group, width)
     attended = lax.all_to_all(attended, "fsdp", split_axis=0, concat_axis=1, tiled=True)
 
     residual = tokens.astype(WIDE) + mm(attended, weight_output)
     scale_two = scale_of(residual)
     unit = residual * scale_two
     hidden_two = (unit * gain_two).astype(LOW)
-    hidden_blocks = ring_blocks(hidden_two, devices, 0, steps - 1)
-    hidden_all = ring_place(hidden_blocks, devices).reshape(group, width)
-
     lane = jnp.arange(128, dtype=jnp.int32)
     chosen = jnp.any(routes[:, :, None] + 1 == lane[None, None, :], axis=1).astype(LOW)
     owner = jnp.concatenate(
@@ -728,20 +806,30 @@
         ]
     )
     spread = (owner[None, :] == lane[:, None]).astype(LOW)
-    back = mm_nt(cot_all, weight_down, LOW)
-    act_low, grads = middle(hidden_all, weights, chosen, spread, back, experts)
+    hidden_all, act_low, grads = middle(
+        hidden_two,
+        cot_all.reshape(devices, rows, width),
+        weights,
+        weight_down,
+        chosen.reshape(devices, rows, 128),
+        spread,
+        experts,
+    )
+    hidden_all = hidden_all.reshape(group, width)
+    act_low = act_low.reshape(group, full)
+    grads = grads.reshape(group, 2 * full + 128)
 
     down_grad = mm_tn(act_low, cot_all, LOW)
+    grads, down_grad = lax.optimization_barrier((grads, down_grad))
+    down_grad = reduce_rep(down_grad)
+    hidden_back = mm(grads, weights, LOW)
+    act_low, grads, hidden_back = lax.optimization_barrier((act_low, grads, hidden_back))
+    hidden_back = lax.psum_scatter(hidden_back, "fsdp", scatter_dimension=0, tiled=True)
+    hidden_back = hidden_back.astype(WIDE)
     in_grad = mm_tn(grads, hidden_all, LOW)
     choice_weight_grad = in_grad[2 * full :].T
-    grads, down_grad, in_grad = lax.optimization_barrier((grads, down_grad, in_grad))
-    down_grad = reduce_rep(down_grad)
-    hidden_back = mm(grads, weights, LOW)
-    act_low, in_grad, hidden_back = lax.optimization_barrier((act_low, in_grad, hidden_back))
     in_grad, down_grad = lax.optimization_barrier((in_grad, down_grad))
     in_grad = reduce_rep(in_grad)
-    hidden_back = lax.psum_scatter(hidden_back, "fsdp", scatter_dimension=0, tiled=True)
-    hidden_back = hidden_back.astype(WIDE)
     layered = mm(act_low, weight_down, LOW)
 
     gain_two_grad = jnp.sum(hidden_back * unit, axis=0)
@@ -760,17 +848,14 @@
         lane[None, :] == experts + 1, gain_two_grad[:, None].astype(LOW), choice_weight_grad
     )
     output_grad = jnp.concatenate([mm_tn(attended_held, output_low, LOW), extra], axis=1)
-    layered, output_grad = lax.optimization_barrier((layered, output_grad))
-    layered = lax.psum_scatter(layered, "fsdp", scatter_dimension=0, tiled=True)
-    mixed = (residual + layered.astype(WIDE)).astype(LOW)
     output_grad = lax.psum_scatter(output_grad, "fsdp", scatter_dimension=0, tiled=True)
 
     parts = attend_back(
         lengths[0], query, keyed, value, attended_mine, attended_back, log_total, cosine, sine,
         scale_row, at_col, at_row, held, size,
     )
-    projected_back = jnp.concatenate(parts[:3], axis=2).reshape(group, 3 * part)
-    scaled_back = jnp.concatenate(parts[3:], axis=2).reshape(group, 3 * part)
+    projected_back = parts[0].reshape(group, 3 * part)
+    scaled_back = parts[1].reshape(group, 3 * part)
     bias_grad = jnp.sum(projected_back.astype(WIDE), axis=0)
     weight_grad = mm_tn(token_all, scaled_back, LOW)
     bias_rows = jnp.broadcast_to(
@@ -780,13 +865,17 @@
     weight_grad = lax.all_to_all(
         weight_grad, "fsdp", split_axis=0, concat_axis=2, tiled=False
     ).reshape(part + 16, 3 * width)
-    weight_grad, projected_back = lax.optimization_barrier((weight_grad, projected_back))
+    weight_grad, projected_back, layered = lax.optimization_barrier(
+        (weight_grad, projected_back, layered)
+    )
     token_back = mm_nt(projected_back, weight_mine, LOW)
-    weight_grad, _ = lax.optimization_barrier((weight_grad, token_back))
-    weight_grad, output_grad, in_grad, down_grad = lax.optimization_barrier(
-        (weight_grad, output_grad, in_grad, down_grad)
-    )
-    weight_grad, output_grad = lax.psum((weight_grad, output_grad), "rep")
+    pushed = lax.psum_scatter(token_back, "fsdp", scatter_dimension=0, tiled=True).astype(WIDE)
+    output_grad, weight_grad, in_grad, down_grad, pushed = lax.optimization_barrier(
+        (output_grad, weight_grad, in_grad, down_grad, pushed)
+    )
+    weight_grad, output_grad = reduce_rep((weight_grad, output_grad))
+    layered = lax.psum_scatter(layered, "fsdp", scatter_dimension=0, tiled=True)
+    mixed = (residual + layered.astype(WIDE)).astype(LOW)
     bias_grad = weight_grad[part].astype(WIDE).reshape(devices, 3 * part)
     bias_grad = lax.dynamic_slice_in_dim(bias_grad, mine, 1, 0)[0]
     weight_grad = weight_grad[:part].astype(WIDE)
@@ -795,7 +884,6 @@
     first_gain_grad = jnp.sum(weight_grad * projection.astype(WIDE), axis=1)
     projection_grad = weight_grad * gain_one[:, None]
 
-    pushed = lax.psum_scatter(token_back, "fsdp", scatter_dimension=0, tiled=True).astype(WIDE)
     inputs = tokens.astype(WIDE)
     scale_one = scale_of(inputs)
     unit_one = inputs * scale_one

time: 1340 us -> 1410 us (1.052)
  waiting for transfers between devices: 336 us -> 574 us
  blocking collectives: 133 us -> 0 us
  matrix products: 268 us -> 237 us
  local copies, waits for them, and re-layouts: 159 us -> 139 us
  Pallas kernels: 325 us -> 343 us
    psum x2 -> x3, waiting for transfers between devices: 154 us -> 337 us  [reduce_rep(): return lax.psum(values, 'rep')]
    all_to_all x1 -> x0, blocking collectives: 133 us -> none  [shards(): lax.all_to_all(weight_grad, 'fsdp', split_axis=0, concat_axis=2, tiled=Fa...]
    reduce_scatter x1, waiting for transfers between devices: 0.01 us -> 112 us  [shards(): lax.psum_scatter(hidden_back, 'fsdp', scatter_dimension=0, tiled=True)]
    ppermute x6 -> x3, waiting for transfers between devices: 113 us -> 18.9 us  [ring_blocks(): blocks.append(lax.ppermute(blocks[-1], 'fsdp', ring))]
    psum x1 -> x0, waiting for transfers between devices: 62.5 us -> none  [shards(): weight_grad, output_grad = lax.psum((weight_grad, output_grad), 'rep')]
    all_to_all x0 -> x1, waiting for transfers between devices: none -> 43.6 us  [shards(): lax.all_to_all(weight_grad, 'fsdp', split_axis=0, concat_axis=2, tiled=Fa...]
    reduce_scatter x1, waiting for transfers between devices: 0.01 us -> 42.4 us  [shards(): lax.psum_scatter(token_back, 'fsdp', scatter_dimension=0, tiled=True)]
    pallas_call x3, Pallas kernels: 170 us -> 209 us  [the longest x1 129 us: middle(): pl.pallas_call(functools.partial(middle_kernel, devices, experts), in_spe...]
  transfers between devices with their start and end apart: 23 -> 17, of which waited for: 9 -> 7; matrix products, arithmetic and copies ran while one was open for 29% -> 23% of each run, Pallas kernels for 7% -> 6%
where the time goes in v2:
time: 1410 us
  waiting for transfers between devices  574 us (41%)
  Pallas kernels  343 us (24%)
  matrix products  237 us (17%)
  local copies, waits for them, and re-layouts  139 us (10%)
  other arithmetic  79.3 us (6%)
  starting transfers between devices  18.1 us (1%)
  between operations  16.5 us (1%)
    psum x3, waiting for transfers between devices, reduce_rep(): return lax.psum(values, 'rep')  337 us
    dot_general x10, matrix products, dot(): lax.dot_general(left, right, ((dims[0], dims[1]), ((), ())), preferred_el...  237 us
    pallas_call x1, Pallas kernels, gather_all(): pl.pallas_call(functools.partial(gather_kernel, devices, reps), in_specs=...  134 us
    pallas_call x1, Pallas kernels, middle(): pl.pallas_call(functools.partial(middle_kernel, devices, experts), in_spe...  129 us
    reduce_scatter x1, waiting for transfers between devices, shards(): lax.psum_scatter(hidden_back, 'fsdp', scatter_dimension=0, tiled=True)  112 us
    all_to_all x1, waiting for transfers between devices, shards(): lax.all_to_all(weight_grad, 'fsdp', split_axis=0, concat_axis=2, tiled=Fa...  43.6 us
    reduce_scatter x1, waiting for transfers between devices, shards(): lax.psum_scatter(token_back, 'fsdp', scatter_dimension=0, tiled=True)  42.4 us
    pallas_call x1, Pallas kernels, attend_back(): pl.pallas_call(functools.partial(attend_back_kernel, size, held), in_spec...  41.7 us
  transfers between devices with their start and end apart: 17, of which 7 were waited for; matrix products, arithmetic and copies ran while one was open for 23% of the time, Pallas kernels for 6%

profile of v2, /device:TPU:0, one launch (start us, length us, event | category | flops | bytes accessed | tf_op | source)
XLA Modules:
  0.0 1406.1 jit_solution(12186029844483541247)
XLA Ops:
  14.1 134.4 %shard_map.255 = (bf16[8,320,2048]{2,1,0:T(8,128)(2,1)}, bf16[8,4,64,768]{3,2,1,0:T(8,128)(2,1)}, bf16[8,4,64,2048]{3,2,1,0:T(8,128)(2,1)}, bf16[8,32,128]{2,1,0:T(8,128)(2,1)}) custom-call(bf16[320,2048]{1,0:T(8,128)(2,1)} %token_.1, bf16[8,64,768]{2,1,0:T(8,128)(2,1)} %reshape.256.strip, bf16[64,2048]{1,0:T(8,128)(2,1)} %constant_dynamic-slice_fusion.share, ...), custom_call_target="tpu_custom_call" | custom-call | flops 99999997952 | bytes 300000000 | tf_op jit(solution)/shard_map/pallas_call | solution.py:655
  149.9 6.1 multiply_reduce_fusion
  158.5 2.2 fusion.1
  161.7 6.2 fusion.23
  168.0 14.0 multiply_add_fusion
  182.1 4.4 pad_maximum_fusion.2
  186.4 5.4 broadcast_in_dim.101
  191.9 2.5 bitcast_dynamic-update-slice_fusion.9
  197.1 38.0 %shard_map.256 = (bf16[8,320,256]{2,1,0:T(8,128)(2,1)}, bf16[8,320,256]{2,1,0:T(8,128)(2,1)}, bf16[8,320,256]{2,1,0:T(8,128)(2,1)}, bf16[8,320,256]{2,1,0:T(8,128)(2,1)}, f32[8,320,256]{2,1,0:T(8,128)}) custom-call(s32[2]{0:T(128)} %bitcast.165, f32[8,320,768]{2,1,0:T(8,128)} %bitcast.176, f32[8,320,128]{2,1,0:T(8,128)} %get-tuple-element.158.cosine, ...), custom_call_target="tpu_custom_call" | custom-call | flops 30000001024 | bytes 90000000 | tf_op jit(solution)/shard_map/pallas_call | solution.py:232
  235.2 5.0 all-to-all-start
  240.8 3.8 bitcast_dynamic-update-slice_fusion.1
  244.6 11.2 fusion.34
  255.8 6.3 constant_dynamic-update-slice_fusion.1
  262.8 3.8 bitcast_dynamic-update-slice_fusion
  266.6 3.5 constant_dynamic-update-slice_fusion
  270.8 3.0 bitcast_dynamic-update-slice_fusion.8
  273.8 2.5 bitcast_dynamic-update-slice_fusion.7
  277.3 4.1 pad_maximum_fusion.down_far
  281.9 1.7 collective-permute-start.5
  283.6 2.5 bitcast_dynamic-update-slice_fusion.6
  286.1 2.5 bitcast_dynamic-update-slice_fusion.5
  290.2 5.9 multiply_reduce_fusion.1
  296.2 18.9 %collective-permute-done.5 = bf16[320,2048]{1,0:T(8,128)(2,1)} collective-permute-done((bf16[320,2048]{1,0:T(8,128)(2,1)}, bf16[320,2048]{1,0:T(8,128)(2,1)}, u32[]{:S(2)}, u32[]{:S(2)}) %collective-permute-start.5) | collective-permute-done | bytes 1310752 | tf_op jit(solution)/shard_map/ppermute | solution.py:277
  316.4 2.5 bitcast_dynamic-update-slice_fusion.4
  318.9 2.5 bitcast_dynamic-update-slice_fusion.3
  322.6 128.8 %shard_map.257 = (bf16[8,320,2048]{2,1,0:T(8,128)(2,1)}, bf16[8,320,2176]{2,1,0:T(8,128)(2,1)}, bf16[8,320,4480]{2,1,0:T(8,128)(2,1)}) custom-call(bf16[320,2048]{1,0:T(8,128)(2,1)} %multiply_convert_fusion.hidden, bf16[8,320,2048]{2,1,0:T(8,128)(2,1)} %bitcast_dynamic-update-slice_fusion.2.cot_all, bf16[4480,2048]{1,0:T(8,128)(2,1)} %fusion.22.weights_far, ...), custom_call_target="tpu_custom_call" | custom-call | flops 109999996928 | bytes 330000000 | tf_op jit(solution)/shard_map/pallas_call | solution.py:443
  451.4 30.6 %convolution_bitcast_fusion = bf16[2176,2048]{1,0:T(8,128)(2,1)} fusion(bf16[8,320,2176]{2,1,0:T(8,128)(2,1)} %get-tuple-element.66, bf16[8,320,2048]{2,1,0:T(8,128)(2,1)} %bitcast_dynamic-update-slice_fusion.2.cot_all), kind=kOutput, calls=%fused_computation.3 | convolution fusion | flops 22817013760 | bytes 30539776 | tf_op jit(solution)/shard_map/dot_general | solution.py:19
  481.9 58.3 %fusion.36 = bf16[2560,2048]{1,0:T(8,128)(2,1)} fusion(bf16[2560,4480]{1,0:T(8,128)(2,1)} %bitcast.170, bf16[4480,2048]{1,0:T(8,128)(2,1)} %fusion.22.weights_far), kind=kOutput, calls=%fused_computation.98 | convolution fusion | flops 46976204800 | bytes 51773440 | tf_op jit(solution)/shard_map/dot_general | solution.py:19
  540.2 112.2 %reduce-scatter.5.cloned.1.call-done = bf16[320,2048]{1,0:T(8,128)(2,1)} async-done(((bf16[2560,2048]{1,0:T(8,128)(2,1)}), bf16[320,2048]{1,0:T(8,128)(2,1)}) %reduce-scatter.5.cloned.1.call-update) | async-done | bytes 1310736 | tf_op jit(solution)/shard_map/reduce_scatter | solution.py:827
  652.5 3.8 fusion.13
  656.3 2.1 fusion.12
  660.0 7.4 fusion.15
  667.4 3.6 all-to-all-start.1
  671.1 13.7 copy.61
  684.8 18.4 %all-to-all-done.1 = bf16[320,8,256]{2,0,1:T(8,128)(2,1)S(1)} async-done(((bf16[320,8,256]{2,0,1:T(8,128)(2,1)}), bf16[320,8,256]{2,0,1:T(8,128)(2,1)S(1)}, u32[]{:S(2)}, u32[]{:S(2)}) %all-to-all-start.1) | async-done | bytes 1310752 | tf_op jit(solution)/shard_map/all_to_all | solution.py:842
  704.6 41.7 %shard_map.258 = (bf16[8,320,768]{2,1,0:T(8,128)(2,1)}, bf16[8,320,768]{2,1,0:T(8,128)(2,1)}) custom-call(s32[2]{0:T(128)} %bitcast.166, bf16[8,320,256]{2,1,0:T(8,128)(2,1)} %get-tuple-element.58.query, bf16[8,320,256]{2,1,0:T(8,128)(2,1)} %get-tuple-element.59.keyed, bf16[8,320,256]{2,1,0:T(8,128)(2,1)} %get-tuple-element.60.value, ...), custom_call_target="tpu_custom_call" | custom-call | flops 1000000000 | bytes 3000000 | tf_op jit(solution)/shard_map/pallas_call | solution.py:249
  746.4 6.4 copy.63
  752.7 2.7 reduce_sum.78
  755.5 12.5 fusion.37
  768.0 2.0 maximum_bitcast_fusion
  770.0 4.6 all-to-all-start.2
  774.7 32.1 %fusion.33 = bf16[2560,2048]{1,0:T(8,128)(2,1)} fusion(bf16[2560,2176]{1,0:T(8,128)(2,1)} %bitcast.172, bf16[64,2048]{1,0:T(8,128)(2,1)S(1)} %copy-done.17, bf16[1408,2048]{1,0:T(8,128)(2,1)} %bitcast.142, bf16[704,2048]{1,0:T(8,128)(2,1)} %param.29), kind=kOutput, calls=%fused_computation.95 | convolution fusion | flops 22843752448 | bytes 30539776 | tf_op jit(solution)/shard_map/dot_general | solution.py:19
  806.8 43.6 %all-to-all-done.2 = bf16[8,272,3,1,256]{4,1,2,3,0:T(8,128)(2,1)} async-done(((bf16[8,272,3,1,256]{4,1,2,3,0:T(8,128)(2,1)}), bf16[8,272,3,1,256]{4,1,2,3,0:T(8,128)(2,1)}, u32[]{:S(2)}, u32[]{:S(2)}) %all-to-all-start.2) | async-done | bytes 3342368 | tf_op jit(solution)/shard_map/all_to_all | solution.py:865
  850.4 4.9 copy.65
  855.3 5.9 reshape_squeeze.11
  861.2 13.5 fusion.39
  874.8 55.9 %fusion.38 = bf16[4480,2048]{1,0:T(8,128)(2,1)} fusion(bf16[2560,4480]{1,0:T(8,128)(2,1)} %bitcast.171, bf16[2560,2048]{1,0:T(8,128)(2,1)} %bitcast.173), kind=kOutput, calls=%fused_computation.100 | convolution fusion | flops 46976204800 | bytes 51773440 | tf_op jit(solution)/shard_map/dot_general | solution.py:19
  933.2 6.6 fusion.18
  939.8 4.2 pad_maximum_fusion.1
  944.7 42.4 %reduce-scatter.11.cloned.1.call-done = bf16[320,2048]{1,0:T(8,128)(2,1)} async-done(((bf16[2560,2048]{1,0:T(8,128)(2,1)}), bf16[320,2048]{1,0:T(8,128)(2,1)}) %reduce-scatter.11.cloned.1.call-update) | async-done | bytes 1310736 | tf_op jit(solution)/shard_map/reduce_scatter | solution.py:872
  987.1 3.1 convert_element_type.131
  990.2 282.1 %all-reduce.8.cloned.1.call-done = bf16[4480,2048]{1,0:T(8,128)(2,1)} async-done(((bf16[4480,2048]{1,0:T(8,128)(2,1)}), bf16[4480,2048]{1,0:T(8,128)(2,1)}) %all-reduce.8.cloned.1.call-update) | async-done | bytes 18350096 | tf_op jit(solution)/shard_map/psum | solution.py:686
  1272.7 8.9 slice.110
  1281.6 3.3 slice.108
  1284.9 9.5 slice.88
  1295.4 5.4 copy-done.2
  1300.7 3.1 convert_bitcast_fusion
  1303.9 8.2 copy.67
  1312.6 4.1 add_convert_fusion
  1316.8 3.8 fusion.9
  1320.6 8.7 convert_bitcast_fusion.1
  1329.3 55.0 %all-reduce.10.cloned.1.call-done = (bf16[272,6144]{1,0:T(8,128)(2,1)}, bf16[256,2176]{0,1:T(8,128)(2,1)}) async-done(((bf16[272,6144]{1,0:T(8,128)(2,1)}, bf16[256,2176]{0,1:T(8,128)(2,1)}), (bf16[272,6144]{1,0:T(8,128)(2,1)}, bf16[256,2176]{0,1:T(8,128)(2,1)})) %all-reduce.10.cloned.1.call-update) | async-done | bytes 4456464 | tf_op jit(solution)/shard_map/psum | solution.py:686
  1388.9 7.2 convert_multiply_fusion
  1396.1 1.8 copy.66
  (181 shorter events, 34.5 us)
Async XLA Ops:
  8.0 4.5 copy-start
  8.0 5.2 copy-start.28
  8.0 5.4 copy-start.30
  8.0 5.4 copy-start.32
  8.1 5.4 copy-start.31
  148.5 7.5 copy-start.22
  148.5 7.6 copy-start.23
  148.5 7.9 copy-start.29
  148.5 9.9 copy-start.24
  148.5 46.8 %collective-permute-start = (bf16[320,2048]{1,0:T(8,128)(2,1)}, bf16[320,2048]{1,0:T(8,128)(2,1)}, u32[]{:S(2)}, u32[]{:S(2)}) collective-permute-start(bf16[320,2048]{1,0:T(8,128)(2,1)} %param.20), channel_id=1, source_target_pairs={{0,2},{1,3},{2,4},{3,5},{4,6},{5,7},{6,0},{7,1},{8,10},{9,11},{10,... | collective-permute-start | bytes 3932168 | tf_op jit(solution)/shard_map/ppermute | solution.py:277
  149.8 121.0 %collective-permute-start.1 = (bf16[320,2048]{1,0:T(8,128)(2,1)}, bf16[320,2048]{1,0:T(8,128)(2,1)}, u32[]{:S(2)}, u32[]{:S(2)}) collective-permute-start(bf16[320,2048]{1,0:T(8,128)(2,1)} %param.20), channel_id=1, source_target_pairs={{0,1},{1,0},{2,3},{3,2},{4,5},{5,4},{6,7},{7,6},{8,9},{9,8},{10,11... | collective-permute-start | bytes 3932168 | tf_op jit(solution)/shard_map/ppermute | solution.py:288
  156.3 0.6 copy-start.20
  158.5 156.6 %copy-start.18 = (f32[1,2,8,128]{3,1,2,0:T(2,128)}, f32[1,2,8,128]{3,1,2,0:T(2,128)S(1)}, u32[]{:S(2)}) copy-start(f32[1,2,8,128]{3,1,2,0:T(2,128)S(1)} %copy.72) | copy-start | bytes 24580
  195.3 88.3 %collective-permute-start.2 = (bf16[320,2048]{1,0:T(8,128)(2,1)}, bf16[320,2048]{1,0:T(8,128)(2,1)}, u32[]{:S(2)}, u32[]{:S(2)}) collective-permute-start(bf16[320,2048]{1,0:T(8,128)(2,1)} %collective-permute-done), channel_id=1, source_target_pairs={{0,1},{1,0},{2,3},{3,2},{4,5},{5,4},{6,7},{7,6},{8,9},{9,8},{10,11... | collective-permute-start | bytes 3932168 | tf_op jit(solution)/shard_map/ppermute | solution.py:288
  195.7 85.7 %collective-permute-start.3 = (bf16[320,2048]{1,0:T(8,128)(2,1)}, bf16[320,2048]{1,0:T(8,128)(2,1)}, u32[]{:S(2)}, u32[]{:S(2)}) collective-permute-start(bf16[320,2048]{1,0:T(8,128)(2,1)} %collective-permute-done), channel_id=1, source_target_pairs={{0,2},{1,3},{2,4},{3,5},{4,6},{5,7},{6,0},{7,1},{8,10},{9,11},{10,... | collective-permute-start | bytes 3932168 | tf_op jit(solution)/shard_map/ppermute | solution.py:277
  235.2 53.5 %all-to-all-start = ((bf16[8,320,256]{2,1,0:T(8,128)(2,1)}), bf16[8,320,256]{2,1,0:T(8,128)(2,1)}, u32[]{:S(2)}, u32[]{:S(2)}) async-start(bf16[8,320,256]{2,1,0:T(8,128)(2,1)} %get-tuple-element.56.attended), calls=%async_computation | async-start | bytes 2621440 | tf_op jit(solution)/shard_map/all_to_all | solution.py:793
  240.2 412.3 %reduce-scatter.5.cloned.1.call-start = ((), (), s32[]{:S(2)}) async-start(), calls=%async_computation.7 | async-start | bytes 11796480 | tf_op jit(solution)/shard_map/reduce_scatter | solution.py:827
  255.8 10.8 slice-start.3
  255.8 10.8 slice-start.4
  266.6 10.7 slice-start.5
  266.6 10.7 slice-start.6
  270.1 7.2 copy-start.13
  277.3 4.1 copy-start.16
  281.4 8.8 copy-start.6
  281.4 35.0 %collective-permute-start.4 = (bf16[320,2048]{1,0:T(8,128)(2,1)}, bf16[320,2048]{1,0:T(8,128)(2,1)}, u32[]{:S(2)}, u32[]{:S(2)}) collective-permute-start(bf16[320,2048]{1,0:T(8,128)(2,1)} %collective-permute-done.3), channel_id=1, source_target_pairs={{0,1},{1,0},{2,3},{3,2},{4,5},{5,4},{6,7},{7,6},{8,9},{9,8},{10,11... | collective-permute-start | bytes 3932168 | tf_op jit(solution)/shard_map/ppermute | solution.py:288
  281.9 33.1 %collective-permute-start.5 = (bf16[320,2048]{1,0:T(8,128)(2,1)}, bf16[320,2048]{1,0:T(8,128)(2,1)}, u32[]{:S(2)}, u32[]{:S(2)}) collective-permute-start(bf16[320,2048]{1,0:T(8,128)(2,1)} %collective-permute-done.3), channel_id=1, source_target_pairs={{0,2},{1,3},{2,4},{3,5},{4,6},{5,7},{6,0},{7,1},{8,10},{9,11},{10,... | collective-permute-start | bytes 3932168 | tf_op jit(solution)/shard_map/ppermute | solution.py:277
  290.1 6.0 copy-start.14
  296.1 18.9 %copy-start.3 = (f32[320,2048]{1,0:T(8,128)}, f32[320,2048]{1,0:T(8,128)S(1)}, u32[]{:S(2)}) copy-start(f32[320,2048]{1,0:T(8,128)S(1)} %get-tuple-element.157) | copy-start | bytes 7864324
  296.1 25.3 %copy-start.25 = (f32[320]{0:T(512)}, f32[320]{0:T(512)S(1)}, u32[]{:S(2)}) copy-start(f32[320]{0:T(512)S(1)} %add_rsqrt_fusion.2) | copy-start | bytes 3844
  315.0 6.4 collective-permute-start.6
  540.2 112.3 %copy-start.19 = (f32[1,2,8,128]{3,1,2,0:T(2,128)S(1)}, f32[1,2,8,128]{3,1,2,0:T(2,128)}, u32[]{:S(2)}) copy-start(f32[1,2,8,128]{3,1,2,0:T(2,128)} %copy-done.18) | copy-start | bytes 24580
  540.2 112.3 %copy-start.26 = (f32[320]{0:T(512)S(1)}, f32[320]{0:T(512)}, u32[]{:S(2)}) copy-start(f32[320]{0:T(512)} %copy-done.25) | copy-start | bytes 3844
  652.5 3.8 copy-start.4
  652.5 3.8 copy-start.10
  658.4 1.6 copy-start.8
  667.4 35.7 %all-to-all-start.1 = ((bf16[320,8,256]{2,0,1:T(8,128)(2,1)}), bf16[320,8,256]{2,0,1:T(8,128)(2,1)S(1)}, u32[]{:S(2)}, u32[]{:S(2)}) async-start(bf16[320,8,256]{2,0,1:T(8,128)(2,1)} %fusion.15), calls=%async_computation.2 | async-start | bytes 2621440 | tf_op jit(solution)/shard_map/all_to_all | solution.py:842
  671.0 259.7 %all-reduce.6.cloned.1.call-start = ((), (), s32[]{:S(2)}) async-start(), calls=%async_computation.10 | async-start | bytes 17825792 | tf_op jit(solution)/shard_map/psum | solution.py:686
  684.8 18.4 %copy-start.21 = (f32[8,320]{1,0:T(8,128)S(1)}, f32[8,320]{1,0:T(8,128)}, u32[]{:S(2)}) copy-start(f32[8,320]{1,0:T(8,128)} %copy-done.20) | copy-start | bytes 30724
  703.1 1.5 copy-start.11
  770.0 4.7 copy-start.17
  770.0 80.4 %all-to-all-start.2 = ((bf16[8,272,3,1,256]{4,1,2,3,0:T(8,128)(2,1)}), bf16[8,272,3,1,256]{4,1,2,3,0:T(8,128)(2,1)}, u32[]{:S(2)}, u32[]{:S(2)}) async-start(bf16[8,272,3,1,256]{4,1,2,3,0:T(8,128)(2,1)} %maximum_bitcast_fusion), calls=%async_computation.3 | async-start | bytes 6684672 | tf_op jit(solution)/shard_map/all_to_all | solution.py:865
  774.6 212.5 %reduce-scatter.11.cloned.1.call-start = ((), (), s32[]{:S(2)}) async-start(), calls=%async_computation.12 | async-start | bytes 11796480 | tf_op jit(solution)/shard_map/reduce_scatter | solution.py:872
  874.8 55.9 %copy-start.27 = (bf16[2048]{0:T(1024)(128)(2,1)S(1)}, bf16[2048]{0:T(1024)(128)(2,1)}, u32[]{:S(2)}) copy-start(bf16[2048]{0:T(1024)(128)(2,1)} %get-tuple-element.141) | copy-start | bytes 12292
  931.8 1.3 copy-start.15
  931.9 340.4 %all-reduce.8.cloned.1.call-start = ((), (), s32[]{:S(2)}) async-start(), calls=%async_computation.11 | async-start | bytes 36700160 | tf_op jit(solution)/shard_map/psum | solution.py:686
  932.5 339.8 %reduce-scatter.9.cloned.1.call-start = ((), (), s32[]{:S(2)}) async-start(), calls=%async_computation.9 | async-start | bytes 10027008 | tf_op jit(solution)/shard_map/reduce_scatter | solution.py:851
  944.0 368.6 %reduce-scatter.7.cloned.1.call-start = ((), (), s32[]{:S(2)}) async-start(), calls=%async_computation.8 | async-start | bytes 11796480 | tf_op jit(solution)/shard_map/reduce_scatter | solution.py:877
  944.6 327.7 %copy-start.33 = (bf16[256]{0:T(256)(128)(2,1)S(1)}, bf16[256]{0:T(256)(128)(2,1)}, u32[]{:S(2)}) copy-start(bf16[256]{0:T(256)(128)(2,1)} %param.21) | copy-start | bytes 1540
  944.6 327.7 %copy-start.7 = (bf16[320,2048]{1,0:T(8,128)(2,1)S(1)}, bf16[320,2048]{1,0:T(8,128)(2,1)}, u32[]{:S(2)}) copy-start(bf16[320,2048]{1,0:T(8,128)(2,1)} %token_.1) | copy-start | bytes 3932164
  944.6 439.7 %all-reduce.10.cloned.1.call-start = ((), (), s32[]{:S(2)}) async-start(), calls=%async_computation.13 | async-start | bytes 8912896 | tf_op jit(solution)/shard_map/psum | solution.py:686
  1272.4 9.3 slice-start
  1272.7 8.9 slice-start.1
  1272.7 8.9 slice-start.2
  1294.4 6.3 copy-start.2
  1303.9 8.2 copy-start.5
  1312.6 4.2 copy-start.9
  1384.3 4.5 copy-start.12
  1388.9 9.6 copy-start.1
Sparse Core Ops, SparseCore 0:
  540.4 112.0 reduce-scatter.4
  874.9 112.1 reduce-scatter.10
  989.4 92.9 reduce-scatter.8
  1085.1 107.7 reduce-scatter.6
Sparse Core Ops, SparseCore 1:
  684.9 181.5 all-reduce.5
  936.9 335.4 all-reduce.7
  1276.2 108.1 all-reduce.9

commit v3 on v2

--- a/solution.py
+++ b/solution.py
@@ -865,16 +865,14 @@
     weight_grad = lax.all_to_all(
         weight_grad, "fsdp", split_axis=0, concat_axis=2, tiled=False
     ).reshape(part + 16, 3 * width)
-    weight_grad, projected_back, layered = lax.optimization_barrier(
-        (weight_grad, projected_back, layered)
-    )
+    weight_grad, projected_back = lax.optimization_barrier((weight_grad, projected_back))
     token_back = mm_nt(projected_back, weight_mine, LOW)
+    layered = lax.psum_scatter(layered, "fsdp", scatter_dimension=0, tiled=True)
+    output_grad, weight_grad, in_grad, down_grad, layered = lax.optimization_barrier(
+        (output_grad, weight_grad, in_grad, down_grad, layered)
+    )
+    weight_grad, output_grad = reduce_rep((weight_grad, output_grad))
     pushed = lax.psum_scatter(token_back, "fsdp", scatter_dimension=0, tiled=True).astype(WIDE)
-    output_grad, weight_grad, in_grad, down_grad, pushed = lax.optimization_barrier(
-        (output_grad, weight_grad, in_grad, down_grad, pushed)
-    )
-    weight_grad, output_grad = reduce_rep((weight_grad, output_grad))
-    layered = lax.psum_scatter(layered, "fsdp", scatter_dimension=0, tiled=True)
     mixed = (residual + layered.astype(WIDE)).astype(LOW)
     bias_grad = weight_grad[part].astype(WIDE).reshape(devices, 3 * part)
     bias_grad = lax.dynamic_slice_in_dim(bias_grad, mine, 1, 0)[0]

time: 1410 us -> 1160 us (0.82)
  waiting for transfers between devices: 574 us -> 152 us
  blocking collectives: 0 us -> 179 us
    psum x3, waiting for transfers between devices: 337 us -> 132 us  [reduce_rep(): return lax.psum(values, 'rep')]
    all_to_all x0 -> x2, blocking collectives: none -> 179 us  [the longest x1 121 us: shards(): lax.all_to_all(weight_grad, 'fsdp', split_axis=0, concat_axis=2, tiled=Fa...]
    reduce_scatter x1, waiting for transfers between devices: 112 us -> 0.01 us  [shards(): lax.psum_scatter(hidden_back, 'fsdp', scatter_dimension=0, tiled=True)]
    all_to_all x2 -> x0, waiting for transfers between devices: 61.9 us -> none  [the longest x1 43.6 us: shards(): lax.all_to_all(weight_grad, 'fsdp', split_axis=0, concat_axis=2, tiled=Fa...]
    reduce_scatter x1, waiting for transfers between devices: 42.4 us -> 0.01 us  [shards(): lax.psum_scatter(token_back, 'fsdp', scatter_dimension=0, tiled=True)]
    unnamed x95 -> x89, local copies, waits for them, and re-layouts: 37.4 us -> 40.1 us
  transfers between devices with their start and end apart: 17 -> 15, of which waited for: 7 -> 4; matrix products, arithmetic and copies ran while one was open for 23% -> 35% of each run, Pallas kernels for 6% -> 7%
where the time goes in v3:
time: 1160 us; the launch traced here: 1150 us
  Pallas kernels  343 us (30%)
  matrix products  235 us (20%)
  blocking collectives  179 us (15%)
  waiting for transfers between devices  152 us (13%)
  local copies, waits for them, and re-layouts  140 us (12%)
  other arithmetic  76.2 us (7%)
  between operations  16.4 us (1%)
    dot_general x10, matrix products, dot(): lax.dot_general(left, right, ((dims[0], dims[1]), ((), ())), preferred_el...  235 us
    pallas_call x1, Pallas kernels, gather_all(): pl.pallas_call(functools.partial(gather_kernel, devices, reps), in_specs=...  134 us
    psum x3, waiting for transfers between devices, reduce_rep(): return lax.psum(values, 'rep')  132 us
    pallas_call x1, Pallas kernels, middle(): pl.pallas_call(functools.partial(middle_kernel, devices, experts), in_spe...  129 us
    all_to_all x1, blocking collectives, shards(): lax.all_to_all(weight_grad, 'fsdp', split_axis=0, concat_axis=2, tiled=Fa...  121 us
    all_to_all x1, blocking collectives, shards(): lax.all_to_all(attended_back, 'fsdp', split_axis=1, concat_axis=0, tiled=...  58.1 us
    pallas_call x1, Pallas kernels, attend_back(): pl.pallas_call(functools.partial(attend_back_kernel, size, held), in_spec...  41.6 us
    unnamed x89, local copies, waits for them, and re-layouts  40.1 us
  transfers between devices with their start and end apart: 15, of which 4 were waited for; matrix products, arithmetic and copies ran while one was open for 35% of the time, Pallas kernels for 7%

profile of v3, /device:TPU:0, one launch (start us, length us, event | category | flops | bytes accessed | tf_op | source)
XLA Modules:
  0.0 1151.4 jit_solution(12854002489789541117)
XLA Ops:
  10.8 1.7 reshape.256.strip
  14.1 134.4 %shard_map.255 = (bf16[8,320,2048]{2,1,0:T(8,128)(2,1)}, bf16[8,4,64,768]{3,2,1,0:T(8,128)(2,1)}, bf16[8,4,64,2048]{3,2,1,0:T(8,128)(2,1)}, bf16[8,32,128]{2,1,0:T(8,128)(2,1)}) custom-call(bf16[320,2048]{1,0:T(8,128)(2,1)} %token_.1, bf16[8,64,768]{2,1,0:T(8,128)(2,1)} %reshape.256.strip, bf16[64,2048]{1,0:T(8,128)(2,1)} %constant_dynamic-slice_fusion.share, ...), custom_call_target="tpu_custom_call" | custom-call | flops 99999997952 | bytes 300000000 | tf_op jit(solution)/shard_map/pallas_call | solution.py:655
  149.7 6.1 multiply_reduce_fusion
  158.4 2.2 fusion.1
  161.6 6.2 fusion.21
  167.9 14.0 %multiply_add_fusion = f32[2560,768]{1,0:T(8,128)} fusion(bf16[2560,2048]{1,0:T(8,128)(2,1)} %bitcast.131, bf16[2048,768]{1,0:T(8,128)(2,1)} %bitcast.178, f32[768]{0:T(1024)S(1)} %reshape.277, f32[2560]{0:T(1024)S(1)} %rsqrt.32), kind=kOutput, calls=%fused_computation.8 | convolution fusion | flops 8056995840 | bytes 21509120 | tf_op jit(solution)/shard_map/dot_general | solution.py:19
  182.0 4.4 pad_maximum_fusion.2
  186.4 5.4 broadcast_in_dim.101
  191.8 2.5 bitcast_dynamic-update-slice_fusion.9
  197.1 38.0 %shard_map.256 = (bf16[8,320,256]{2,1,0:T(8,128)(2,1)}, bf16[8,320,256]{2,1,0:T(8,128)(2,1)}, bf16[8,320,256]{2,1,0:T(8,128)(2,1)}, bf16[8,320,256]{2,1,0:T(8,128)(2,1)}, f32[8,320,256]{2,1,0:T(8,128)}) custom-call(s32[2]{0:T(128)} %bitcast.166, f32[8,320,768]{2,1,0:T(8,128)} %bitcast.177, f32[8,320,128]{2,1,0:T(8,128)} %get-tuple-element.156.cosine, ...), custom_call_target="tpu_custom_call" | custom-call | flops 30000001024 | bytes 90000000 | tf_op jit(solution)/shard_map/pallas_call | solution.py:232
  235.1 5.0 all-to-all-start
  240.6 3.8 bitcast_dynamic-update-slice_fusion.1
  244.4 11.2 fusion.32
  255.6 6.3 constant_dynamic-update-slice_fusion.1
  262.6 3.8 bitcast_dynamic-update-slice_fusion
  266.4 3.5 constant_dynamic-update-slice_fusion
  270.6 3.0 bitcast_dynamic-update-slice_fusion.8
  273.6 2.5 bitcast_dynamic-update-slice_fusion.7
  277.1 4.1 pad_maximum_fusion.down_far
  281.7 1.7 collective-permute-start.5
  283.4 2.5 bitcast_dynamic-update-slice_fusion.6
  285.9 2.5 bitcast_dynamic-update-slice_fusion.5
  288.4 1.5 copy.69
  289.9 5.9 multiply_reduce_fusion.1
  295.9 18.9 %collective-permute-done.5 = bf16[320,2048]{1,0:T(8,128)(2,1)} collective-permute-done((bf16[320,2048]{1,0:T(8,128)(2,1)}, bf16[320,2048]{1,0:T(8,128)(2,1)}, u32[]{:S(2)}, u32[]{:S(2)}) %collective-permute-start.5) | collective-permute-done | bytes 1310752 | tf_op jit(solution)/shard_map/ppermute | solution.py:277
  316.1 2.5 bitcast_dynamic-update-slice_fusion.4
  318.7 2.5 bitcast_dynamic-update-slice_fusion.3
  322.3 128.8 %shard_map.257 = (bf16[8,320,2048]{2,1,0:T(8,128)(2,1)}, bf16[8,320,2176]{2,1,0:T(8,128)(2,1)}, bf16[8,320,4480]{2,1,0:T(8,128)(2,1)}) custom-call(bf16[320,2048]{1,0:T(8,128)(2,1)} %multiply_convert_fusion.hidden, bf16[8,320,2048]{2,1,0:T(8,128)(2,1)} %bitcast_dynamic-update-slice_fusion.2.cot_all, bf16[4480,2048]{1,0:T(8,128)(2,1)} %fusion.20.weights_far, ...), custom_call_target="tpu_custom_call" | custom-call | flops 109999996928 | bytes 330000000 | tf_op jit(solution)/shard_map/pallas_call | solution.py:443
  451.1 30.7 %convolution_bitcast_fusion = bf16[2176,2048]{1,0:T(8,128)(2,1)} fusion(bf16[8,320,2176]{2,1,0:T(8,128)(2,1)} %get-tuple-element.62, bf16[8,320,2048]{2,1,0:T(8,128)(2,1)} %bitcast_dynamic-update-slice_fusion.2.cot_all), kind=kOutput, calls=%fused_computation.3 | convolution fusion | flops 22817013760 | bytes 30539776 | tf_op jit(solution)/shard_map/dot_general | solution.py:19
  481.9 58.1 %fusion.34 = bf16[2560,2048]{1,0:T(8,128)(2,1)} fusion(bf16[2560,4480]{1,0:T(8,128)(2,1)} %bitcast.171, bf16[4480,2048]{1,0:T(8,128)(2,1)} %fusion.20.weights_far), kind=kOutput, calls=%fused_computation.98 | convolution fusion | flops 46976204800 | bytes 51773440 | tf_op jit(solution)/shard_map/dot_general | solution.py:19
  540.9 32.0 %fusion.31 = bf16[2560,2048]{1,0:T(8,128)(2,1)} fusion(bf16[2560,2176]{1,0:T(8,128)(2,1)} %bitcast.173, bf16[64,2048]{1,0:T(8,128)(2,1)S(1)} %copy-done.15, bf16[1408,2048]{1,0:T(8,128)(2,1)} %bitcast.143, bf16[704,2048]{1,0:T(8,128)(2,1)} %param.29), kind=kOutput, calls=%fused_computation.95 | convolution fusion | flops 22843752448 | bytes 30539776 | tf_op jit(solution)/shard_map/dot_general | solution.py:19
  573.0 56.1 %fusion.35 = bf16[4480,2048]{1,0:T(8,128)(2,1)} fusion(bf16[2560,4480]{1,0:T(8,128)(2,1)} %bitcast.172, bf16[2560,2048]{1,0:T(8,128)(2,1)} %bitcast.174), kind=kOutput, calls=%fused_computation.99 | convolution fusion | flops 46976204800 | bytes 51773440 | tf_op jit(solution)/shard_map/dot_general | solution.py:19
  629.1 36.1 %all-reduce.6.cloned.1.call-done = bf16[2176,2048]{1,0:T(8,128)(2,1)} async-done(((bf16[2176,2048]{1,0:T(8,128)(2,1)}), bf16[2176,2048]{1,0:T(8,128)(2,1)}) %all-reduce.6.cloned.1.call-update) | async-done | bytes 8912912 | tf_op jit(solution)/shard_map/psum | solution.py:686
  665.2 3.0 fusion.5
  670.7 3.0 fusion.7
  673.8 7.4 fusion.13
  681.2 58.1 %all_to_all.44 = bf16[320,8,256]{2,0,1:T(8,128)(2,1)} all-to-all(bf16[320,8,256]{2,0,1:T(8,128)(2,1)S(1)} %fusion.13), channel_id=1, replica_groups=mesh['rep'=4,'fsdp'=8] {'fsdp'}, dimensions={1} | all-to-all | bytes 2621440 | tf_op jit(solution)/shard_map/all_to_all | solution.py:842
  739.2 4.8 fusion.16
  744.1 4.1 pad_maximum_fusion.1
  748.3 14.1 %copy.62 = bf16[2048,2560]{1,0:T(8,128)(2,1)} copy(bf16[2048,2560]{0,1:T(8,128)(2,1)} %bitcast.132) | data formatting | bytes 20971520 | tf_op jit(solution)/shard_map/dot_general | solution.py:19
  762.4 1.5 broadcast_in_dim.117.scale_row
  763.8 41.6 %shard_map.258 = (bf16[8,320,768]{2,1,0:T(8,128)(2,1)}, bf16[8,320,768]{2,1,0:T(8,128)(2,1)}) custom-call(s32[2]{0:T(128)} %bitcast.167, bf16[8,320,256]{2,1,0:T(8,128)(2,1)} %get-tuple-element.69.query, bf16[8,320,256]{2,1,0:T(8,128)(2,1)} %get-tuple-element.70.keyed, bf16[8,320,256]{2,1,0:T(8,128)(2,1)} %get-tuple-element.71.value, ...), custom_call_target="tpu_custom_call" | custom-call | flops 1000000000 | bytes 3000000 | tf_op jit(solution)/shard_map/pallas_call | solution.py:249
  805.4 6.1 copy.63
  811.6 3.1 reduce_sum.79
  814.7 12.7 %fusion.36 = bf16[8,256,3,256]{3,1,2,0:T(8,128)(2,1)S(1)} fusion(bf16[8,256,2560,1]{2,1,3,0:T(8,128)(2,1)} %bitcast.142, bf16[3,256,2560,1]{2,1,0,3:T(8,128)(2,1)} %bitcast.151), kind=kOutput, calls=%fused_computation.100 | convolution fusion | flops 8053063680 | bytes 17563648 | tf_op jit(solution)/shard_map/dot_general | solution.py:19
  827.7 121.2 %all_to_all.45 = bf16[8,272,3,1,256]{4,1,2,3,0:T(8,128)(2,1)S(1)} all-to-all(bf16[8,272,3,1,256]{4,1,2,3,0:T(8,128)(2,1)S(1)} %maximum_bitcast_fusion), channel_id=1, replica_groups=mesh['rep'=4,'fsdp'=8] {'fsdp'}, dimensions={0} | all-to-all | bytes 6684672 | tf_op jit(solution)/shard_map/all_to_all | solution.py:865
  948.9 3.0 copy.65
  951.9 6.0 reshape_squeeze.11
  957.9 50.4 %all-reduce.8.cloned.1.call-done = bf16[4480,2048]{1,0:T(8,128)(2,1)} async-done(((bf16[4480,2048]{1,0:T(8,128)(2,1)}), bf16[4480,2048]{1,0:T(8,128)(2,1)}) %all-reduce.8.cloned.1.call-update) | async-done | bytes 18350096 | tf_op jit(solution)/shard_map/psum | solution.py:686
  1008.4 13.7 %fusion.37 = bf16[2560,2048]{1,0:T(8,128)(2,1)} fusion(bf16[2560,768]{1,0:T(8,128)(2,1)} %bitcast.149, bf16[2048,768]{1,0:T(8,128)(2,1)} %bitcast.179), kind=kOutput, calls=%fused_computation.101 | convolution fusion | flops 8053063680 | bytes 17563648 | tf_op jit(solution)/shard_map/dot_general | solution.py:19
  1023.8 9.3 slice.110
  1033.1 3.3 slice.108
  1036.4 9.2 slice.88
  1046.5 5.9 copy-done.2
  1052.5 3.1 convert_bitcast_fusion
  1055.6 8.8 copy.67
  1064.5 1.4 add_convert_fusion
  1065.9 9.4 convert_bitcast_fusion.1
  1075.3 45.6 %all-reduce.10.cloned.1.call-done = (bf16[272,6144]{1,0:T(8,128)(2,1)}, bf16[256,2176]{0,1:T(8,128)(2,1)}) async-done(((bf16[272,6144]{1,0:T(8,128)(2,1)}, bf16[256,2176]{0,1:T(8,128)(2,1)}), (bf16[272,6144]{1,0:T(8,128)(2,1)}, bf16[256,2176]{0,1:T(8,128)(2,1)})) %all-reduce.10.cloned.1.call-update) | async-done | bytes 4456464 | tf_op jit(solution)/shard_map/psum | solution.py:686
  1120.9 2.7 slice_convert_fusion
  1123.6 2.9 copy.66
  1130.2 8.0 convert_multiply_fusion
  1138.1 2.1 fusion.9
  1140.3 3.5 fusion.11
  (172 shorter events, 27.9 us)
Async XLA Ops:
  8.0 4.5 copy-start
  8.0 5.2 copy-start.25
  8.0 5.4 copy-start.27
  8.0 5.4 copy-start.29
  8.1 5.4 copy-start.28
  148.5 7.4 copy-start.20
  148.5 7.5 copy-start.21
  148.5 7.8 copy-start.26
  148.5 9.8 copy-start.22
  148.5 46.7 %collective-permute-start = (bf16[320,2048]{1,0:T(8,128)(2,1)}, bf16[320,2048]{1,0:T(8,128)(2,1)}, u32[]{:S(2)}, u32[]{:S(2)}) collective-permute-start(bf16[320,2048]{1,0:T(8,128)(2,1)} %param.20), channel_id=1, source_target_pairs={{0,2},{1,3},{2,4},{3,5},{4,6},{5,7},{6,0},{7,1},{8,10},{9,11},{10,... | collective-permute-start | bytes 3932168 | tf_op jit(solution)/shard_map/ppermute | solution.py:277
  149.7 120.9 %collective-permute-start.1 = (bf16[320,2048]{1,0:T(8,128)(2,1)}, bf16[320,2048]{1,0:T(8,128)(2,1)}, u32[]{:S(2)}, u32[]{:S(2)}) collective-permute-start(bf16[320,2048]{1,0:T(8,128)(2,1)} %param.20), channel_id=1, source_target_pairs={{0,1},{1,0},{2,3},{3,2},{4,5},{5,4},{6,7},{7,6},{8,9},{9,8},{10,11... | collective-permute-start | bytes 3932168 | tf_op jit(solution)/shard_map/ppermute | solution.py:288
  156.2 0.6 copy-start.18
  158.3 156.5 %copy-start.16 = (f32[1,2,8,128]{3,1,2,0:T(2,128)}, f32[1,2,8,128]{3,1,2,0:T(2,128)S(1)}, u32[]{:S(2)}) copy-start(f32[1,2,8,128]{3,1,2,0:T(2,128)S(1)} %copy.72) | copy-start | bytes 24580
  195.2 88.2 %collective-permute-start.2 = (bf16[320,2048]{1,0:T(8,128)(2,1)}, bf16[320,2048]{1,0:T(8,128)(2,1)}, u32[]{:S(2)}, u32[]{:S(2)}) collective-permute-start(bf16[320,2048]{1,0:T(8,128)(2,1)} %collective-permute-done), channel_id=1, source_target_pairs={{0,1},{1,0},{2,3},{3,2},{4,5},{5,4},{6,7},{7,6},{8,9},{9,8},{10,11... | collective-permute-start | bytes 3932168 | tf_op jit(solution)/shard_map/ppermute | solution.py:288
  195.7 85.5 %collective-permute-start.3 = (bf16[320,2048]{1,0:T(8,128)(2,1)}, bf16[320,2048]{1,0:T(8,128)(2,1)}, u32[]{:S(2)}, u32[]{:S(2)}) collective-permute-start(bf16[320,2048]{1,0:T(8,128)(2,1)} %collective-permute-done), channel_id=1, source_target_pairs={{0,2},{1,3},{2,4},{3,5},{4,6},{5,7},{6,0},{7,1},{8,10},{9,11},{10,... | collective-permute-start | bytes 3932168 | tf_op jit(solution)/shard_map/ppermute | solution.py:277
  235.1 53.3 %all-to-all-start = ((bf16[8,320,256]{2,1,0:T(8,128)(2,1)}), bf16[8,320,256]{2,1,0:T(8,128)(2,1)}, u32[]{:S(2)}, u32[]{:S(2)}) async-start(bf16[8,320,256]{2,1,0:T(8,128)(2,1)} %get-tuple-element.55.attended), calls=%async_computation | async-start | bytes 2621440 | tf_op jit(solution)/shard_map/all_to_all | solution.py:793
  240.1 425.1 %all-reduce.6.cloned.1.call-start = ((), (), s32[]{:S(2)}) async-start(), calls=%async_computation.9 | async-start | bytes 17825792 | tf_op jit(solution)/shard_map/psum | solution.py:686
  255.6 10.8 slice-start.3
  255.6 10.8 slice-start.4
  266.4 10.7 slice-start.5
  266.4 10.7 slice-start.6
  269.9 7.2 copy-start.10
  277.1 4.1 copy-start.14
  281.2 8.8 copy-start.5
  281.2 35.0 %collective-permute-start.4 = (bf16[320,2048]{1,0:T(8,128)(2,1)}, bf16[320,2048]{1,0:T(8,128)(2,1)}, u32[]{:S(2)}, u32[]{:S(2)}) collective-permute-start(bf16[320,2048]{1,0:T(8,128)(2,1)} %collective-permute-done.3), channel_id=1, source_target_pairs={{0,1},{1,0},{2,3},{3,2},{4,5},{5,4},{6,7},{7,6},{8,9},{9,8},{10,11... | collective-permute-start | bytes 3932168 | tf_op jit(solution)/shard_map/ppermute | solution.py:288
  281.7 33.1 %collective-permute-start.5 = (bf16[320,2048]{1,0:T(8,128)(2,1)}, bf16[320,2048]{1,0:T(8,128)(2,1)}, u32[]{:S(2)}, u32[]{:S(2)}) collective-permute-start(bf16[320,2048]{1,0:T(8,128)(2,1)} %collective-permute-done.3), channel_id=1, source_target_pairs={{0,2},{1,3},{2,4},{3,5},{4,6},{5,7},{6,0},{7,1},{8,10},{9,11},{10,... | collective-permute-start | bytes 3932168 | tf_op jit(solution)/shard_map/ppermute | solution.py:277
  289.9 6.0 copy-start.12
  295.9 18.9 %copy-start.3 = (f32[320,2048]{1,0:T(8,128)}, f32[320,2048]{1,0:T(8,128)S(1)}, u32[]{:S(2)}) copy-start(f32[320,2048]{1,0:T(8,128)S(1)} %get-tuple-element.155) | copy-start | bytes 7864324
  295.9 25.3 %copy-start.23 = (f32[320]{0:T(512)}, f32[320]{0:T(512)S(1)}, u32[]{:S(2)}) copy-start(f32[320]{0:T(512)S(1)} %add_rsqrt_fusion.2) | copy-start | bytes 3844
  314.8 6.4 collective-permute-start.6
  481.8 183.4 %reduce-scatter.5.cloned.1.call-start = ((), (), s32[]{:S(2)}) async-start(), calls=%async_computation.7 | async-start | bytes 11796480 | tf_op jit(solution)/shard_map/reduce_scatter | solution.py:827
  540.0 0.9 copy-start.15
  540.0 417.9 %reduce-scatter.9.cloned.1.call-start = ((), (), s32[]{:S(2)}) async-start(), calls=%async_computation.11 | async-start | bytes 11796480 | tf_op jit(solution)/shard_map/reduce_scatter | solution.py:870
  573.0 92.2 %copy-start.17 = (f32[1,2,8,128]{3,1,2,0:T(2,128)S(1)}, f32[1,2,8,128]{3,1,2,0:T(2,128)}, u32[]{:S(2)}) copy-start(f32[1,2,8,128]{3,1,2,0:T(2,128)} %copy-done.16) | copy-start | bytes 24580
  573.0 92.2 %copy-start.24 = (f32[320]{0:T(512)S(1)}, f32[320]{0:T(512)}, u32[]{:S(2)}) copy-start(f32[320]{0:T(512)} %copy-done.23) | copy-start | bytes 3844
  669.4 1.3 copy-start.9
  669.4 338.9 %all-reduce.8.cloned.1.call-start = ((), (), s32[]{:S(2)}) async-start(), calls=%async_computation.10 | async-start | bytes 36700160 | tf_op jit(solution)/shard_map/psum | solution.py:686
  670.2 338.2 %reduce-scatter.7.cloned.1.call-start = ((), (), s32[]{:S(2)}) async-start(), calls=%async_computation.8 | async-start | bytes 10027008 | tf_op jit(solution)/shard_map/reduce_scatter | solution.py:851
  673.8 65.5 %copy-start.7 = (f32[320,2048]{1,0:T(8,128)}, f32[320,2048]{1,0:T(8,128)S(1)}, u32[]{:S(2)}) copy-start(f32[320,2048]{1,0:T(8,128)S(1)} %fusion.7) | copy-start | bytes 7864324
  673.8 65.5 %copy-start.13 = (bf16[8,40,8,256]{3,2,0,1:T(8,128)(2,1)S(1)}, bf16[8,40,8,256]{3,2,0,1:T(8,128)(2,1)}, u32[]{:S(2)}) copy-start(bf16[8,40,8,256]{3,2,0,1:T(8,128)(2,1)} %copy-done.12) | copy-start | bytes 3932164
  748.2 372.7 %all-reduce.10.cloned.1.call-start = ((), (), s32[]{:S(2)}) async-start(), calls=%async_computation.13 | async-start | bytes 8912896 | tf_op jit(solution)/shard_map/psum | solution.py:686
  748.3 14.1 %copy-start.19 = (f32[8,320]{1,0:T(8,128)S(1)}, f32[8,320]{1,0:T(8,128)}, u32[]{:S(2)}) copy-start(f32[8,320]{1,0:T(8,128)} %copy-done.18) | copy-start | bytes 30724
  1008.3 129.8 %reduce-scatter.11.cloned.1.call-start = ((), (), s32[]{:S(2)}) async-start(), calls=%async_computation.12 | async-start | bytes 11796480 | tf_op jit(solution)/shard_map/reduce_scatter | solution.py:875
  1022.1 0.7 copy-start.30
  1022.1 1.3 copy-start.6
  1022.1 11.0 slice-start
  1023.5 9.6 slice-start.1
  1023.8 9.3 slice-start.2
  1045.6 6.8 copy-start.2
  1055.6 8.9 copy-start.4
  1055.6 8.9 copy-start.11
  1138.1 2.1 copy-start.8
  1140.2 3.6 copy-start.1
Sparse Core Ops, SparseCore 0:
  481.9 183.2 all-reduce.5
  674.8 333.4 all-reduce.7
  1012.3 108.5 all-reduce.9
Sparse Core Ops, SparseCore 1:
  540.1 112.6 reduce-scatter.4
  655.5 128.7 reduce-scatter.8
  786.5 144.2 reduce-scatter.6
  1022.2 109.2 reduce-scatter.10

commit v4 on v3

--- a/solution.py
+++ b/solution.py
@@ -828,6 +828,7 @@
     hidden_back = hidden_back.astype(WIDE)
     in_grad = mm_tn(grads, hidden_all, LOW)
     choice_weight_grad = in_grad[2 * full :].T
+    in_grad = jnp.concatenate([in_grad[:total], in_grad[full : full + total]], axis=0)
     in_grad, down_grad = lax.optimization_barrier((in_grad, down_grad))
     in_grad = reduce_rep(in_grad)
     layered = mm(act_low, weight_down, LOW)
@@ -889,9 +890,9 @@
         pushed - unit_one * jnp.mean(pushed * unit_one, axis=-1, keepdims=True)
     )
 
-    in_grad = in_grad[: 2 * full].reshape(2, full, width)
+    in_grad = in_grad.reshape(2, total, width)
     shared_in_grad = in_grad[:, :common].astype(WIDE).transpose(0, 2, 1)
-    expert_in_grad = in_grad[:, common:total].reshape(2, experts, hidden, width)
+    expert_in_grad = in_grad[:, common:].reshape(2, experts, hidden, width)
     expert_in_grad = expert_in_grad[:, :, :units].astype(WIDE).transpose(1, 0, 3, 2)
     down_grad = down_grad.astype(WIDE)
     return (

time: 1160 us -> 1130 us (0.974)
  blocking collectives: 179 us -> 120 us
  waiting for transfers between devices: 152 us -> 174 us
    all_to_all x1 -> x0, blocking collectives: 58.1 us -> none  [shards(): lax.all_to_all(attended_back, 'fsdp', split_axis=1, concat_axis=0, tiled=...]
    all_to_all x0 -> x1, waiting for transfers between devices: none -> 52.2 us  [shards(): lax.all_to_all(attended_back, 'fsdp', split_axis=1, concat_axis=0, tiled=...]
    psum x3, waiting for transfers between devices: 132 us -> 103 us  [reduce_rep(): return lax.psum(values, 'rep')]
    unnamed x89 -> x81, local copies, waits for them, and re-layouts: 40.1 us -> 35.8 us
  transfers between devices with their start and end apart: 15 -> 16, of which waited for: 4 -> 5; matrix products, arithmetic and copies ran while one was open for 35% -> 37% of each run, Pallas kernels for 7% -> 7%
where the time goes in v4:
time: 1130 us
  Pallas kernels  343 us (30%)
  matrix products  239 us (21%)
  waiting for transfers between devices  174 us (15%)
  local copies, waits for them, and re-layouts  140 us (12%)
  blocking collectives  120 us (11%)
  other arithmetic  84 us (7%)
  between operations  16.4 us (1%)
  starting transfers between devices  14.7 us (1%)
    dot_general x10, matrix products, dot(): lax.dot_general(left, right, ((dims[0], dims[1]), ((), ())), preferred_el...  239 us
    pallas_call x1, Pallas kernels, gather_all(): pl.pallas_call(functools.partial(gather_kernel, devices, reps), in_specs=...  134 us
    pallas_call x1, Pallas kernels, middle(): pl.pallas_call(functools.partial(middle_kernel, devices, experts), in_spe...  129 us
    all_to_all x1, blocking collectives, shards(): lax.all_to_all(weight_grad, 'fsdp', split_axis=0, concat_axis=2, tiled=Fa...  120 us
    psum x3, waiting for transfers between devices, reduce_rep(): return lax.psum(values, 'rep')  103 us
    all_to_all x1, waiting for transfers between devices, shards(): lax.all_to_all(attended_back, 'fsdp', split_axis=1, concat_axis=0, tiled=...  52.2 us
    pallas_call x1, Pallas kernels, attend_back(): pl.pallas_call(functools.partial(attend_back_kernel, size, held), in_spec...  41.5 us
    pallas_call x1, Pallas kernels, attend(): pl.pallas_call(functools.partial(attend_kernel, size, held), in_specs=[pl...  38.1 us
  transfers between devices with their start and end apart: 16, of which 5 were waited for; matrix products, arithmetic and copies ran while one was open for 37% of the time, Pallas kernels for 7%

profile of v4, /device:TPU:0, one launch (start us, length us, event | category | flops | bytes accessed | tf_op | source)
XLA Modules:
  0.0 1130.4 jit_solution(10483158523956359550)
XLA Ops:
  10.8 1.7 reshape.256.strip
  14.1 134.4 %shard_map.255 = (bf16[8,320,2048]{2,1,0:T(8,128)(2,1)}, bf16[8,4,64,768]{3,2,1,0:T(8,128)(2,1)}, bf16[8,4,64,2048]{3,2,1,0:T(8,128)(2,1)}, bf16[8,32,128]{2,1,0:T(8,128)(2,1)}) custom-call(bf16[320,2048]{1,0:T(8,128)(2,1)} %token_.1, bf16[8,64,768]{2,1,0:T(8,128)(2,1)} %reshape.256.strip, bf16[64,2048]{1,0:T(8,128)(2,1)} %constant_dynamic-slice_fusion.share, ...), custom_call_target="tpu_custom_call" | custom-call | flops 99999997952 | bytes 300000000 | tf_op jit(solution)/shard_map/pallas_call | solution.py:655
  149.7 6.1 multiply_reduce_fusion
  158.4 2.2 fusion.1
  161.6 6.2 fusion.21
  167.9 14.0 %multiply_add_fusion = f32[2560,768]{1,0:T(8,128)} fusion(bf16[2560,2048]{1,0:T(8,128)(2,1)} %bitcast.129, bf16[2048,768]{1,0:T(8,128)(2,1)} %bitcast.176, f32[768]{0:T(1024)S(1)} %reshape.277, f32[2560]{0:T(1024)S(1)} %rsqrt.32), kind=kOutput, calls=%fused_computation.9 | convolution fusion | flops 8056995840 | bytes 21509120 | tf_op jit(solution)/shard_map/dot_general | solution.py:19
  182.0 4.4 pad_maximum_fusion.3
  186.4 5.4 broadcast_in_dim.101
  191.8 2.5 bitcast_dynamic-update-slice_fusion.9
  197.1 38.1 %shard_map.256 = (bf16[8,320,256]{2,1,0:T(8,128)(2,1)}, bf16[8,320,256]{2,1,0:T(8,128)(2,1)}, bf16[8,320,256]{2,1,0:T(8,128)(2,1)}, bf16[8,320,256]{2,1,0:T(8,128)(2,1)}, f32[8,320,256]{2,1,0:T(8,128)}) custom-call(s32[2]{0:T(128)} %bitcast.164, f32[8,320,768]{2,1,0:T(8,128)} %bitcast.175, f32[8,320,128]{2,1,0:T(8,128)} %get-tuple-element.158.cosine, ...), custom_call_target="tpu_custom_call" | custom-call | flops 30000001024 | bytes 90000000 | tf_op jit(solution)/shard_map/pallas_call | solution.py:232
  235.1 5.0 all-to-all-start
  240.6 3.8 bitcast_dynamic-update-slice_fusion.1
  244.4 11.2 fusion.33
  255.6 6.2 constant_dynamic-update-slice_fusion.1
  262.5 4.2 bitcast_dynamic-update-slice_fusion
  266.7 3.4 constant_dynamic-update-slice_fusion
  270.8 3.1 bitcast_dynamic-update-slice_fusion.8
  273.9 2.5 bitcast_dynamic-update-slice_fusion.7
  277.4 4.1 pad_maximum_fusion.1.down_far
  282.0 1.7 collective-permute-start.5
  283.7 2.5 bitcast_dynamic-update-slice_fusion.6
  286.2 2.5 bitcast_dynamic-update-slice_fusion.5
  290.2 5.9 multiply_reduce_fusion.1
  296.2 18.9 %collective-permute-done.5 = bf16[320,2048]{1,0:T(8,128)(2,1)} collective-permute-done((bf16[320,2048]{1,0:T(8,128)(2,1)}, bf16[320,2048]{1,0:T(8,128)(2,1)}, u32[]{:S(2)}, u32[]{:S(2)}) %collective-permute-start.5) | collective-permute-done | bytes 1310752 | tf_op jit(solution)/shard_map/ppermute | solution.py:277
  316.4 2.5 bitcast_dynamic-update-slice_fusion.4
  318.9 2.5 bitcast_dynamic-update-slice_fusion.3
  322.6 128.8 %shard_map.257 = (bf16[8,320,2048]{2,1,0:T(8,128)(2,1)}, bf16[8,320,2176]{2,1,0:T(8,128)(2,1)}, bf16[8,320,4480]{2,1,0:T(8,128)(2,1)}) custom-call(bf16[320,2048]{1,0:T(8,128)(2,1)} %multiply_convert_fusion.hidden, bf16[8,320,2048]{2,1,0:T(8,128)(2,1)} %bitcast_dynamic-update-slice_fusion.2.cot_all, bf16[4480,2048]{1,0:T(8,128)(2,1)} %fusion.20.weights_far, ...), custom_call_target="tpu_custom_call" | custom-call | flops 109999996928 | bytes 330000000 | tf_op jit(solution)/shard_map/pallas_call | solution.py:443
  451.4 30.6 %convolution_bitcast_fusion = bf16[2176,2048]{1,0:T(8,128)(2,1)} fusion(bf16[8,320,2176]{2,1,0:T(8,128)(2,1)} %get-tuple-element.62, bf16[8,320,2048]{2,1,0:T(8,128)(2,1)} %bitcast_dynamic-update-slice_fusion.2.cot_all), kind=kOutput, calls=%fused_computation.4 | convolution fusion | flops 22817013760 | bytes 30539776 | tf_op jit(solution)/shard_map/dot_general | solution.py:19
  482.2 58.1 %fusion.35 = bf16[2560,2048]{1,0:T(8,128)(2,1)} fusion(bf16[2560,4480]{1,0:T(8,128)(2,1)} %bitcast.169, bf16[4480,2048]{1,0:T(8,128)(2,1)} %fusion.20.weights_far), kind=kOutput, calls=%fused_computation.100 | convolution fusion | flops 46976204800 | bytes 51773440 | tf_op jit(solution)/shard_map/dot_general | solution.py:19
  541.2 32.0 %fusion.31 = bf16[2560,2048]{1,0:T(8,128)(2,1)} fusion(bf16[2560,2176]{1,0:T(8,128)(2,1)} %bitcast.171, bf16[64,2048]{1,0:T(8,128)(2,1)S(1)} %copy-done.13, bf16[1408,2048]{1,0:T(8,128)(2,1)} %bitcast.141, bf16[704,2048]{1,0:T(8,128)(2,1)} %param.29), kind=kOutput, calls=%fused_computation.96 | convolution fusion | flops 22843752448 | bytes 30539776 | tf_op jit(solution)/shard_map/dot_general | solution.py:19
  573.3 55.9 %fusion.36 = bf16[4480,2048]{1,0:T(8,128)(2,1)} fusion(bf16[2560,4480]{1,0:T(8,128)(2,1)} %bitcast.170, bf16[2560,2048]{1,0:T(8,128)(2,1)} %bitcast.172), kind=kOutput, calls=%fused_computation.101 | convolution fusion | flops 46976204800 | bytes 51773440 | tf_op jit(solution)/shard_map/dot_general | solution.py:19
  629.2 7.8 fusion.32
  637.0 7.7 pad_maximum_fusion
  644.8 20.7 %all-reduce.6.cloned.1.call-done = bf16[2176,2048]{1,0:T(8,128)(2,1)} async-done(((bf16[2176,2048]{1,0:T(8,128)(2,1)}), bf16[2176,2048]{1,0:T(8,128)(2,1)}) %all-reduce.6.cloned.1.call-update) | async-done | bytes 8912912 | tf_op jit(solution)/shard_map/psum | solution.py:686
  665.6 3.0 fusion.5
  668.6 3.3 fusion.7
  673.4 8.7 fusion.13
  682.1 4.7 all-to-all-start.1
  688.2 52.2 %all-to-all-done.1 = bf16[320,8,256]{2,0,1:T(8,128)(2,1)S(1)} async-done(((bf16[320,8,256]{2,0,1:T(8,128)(2,1)}), bf16[320,8,256]{2,0,1:T(8,128)(2,1)S(1)}, u32[]{:S(2)}, u32[]{:S(2)}) %all-to-all-start.1) | async-done | bytes 1310752 | tf_op jit(solution)/shard_map/all_to_all | solution.py:843
  740.4 7.2 fusion.16
  747.6 4.0 pad_maximum_fusion.2
  751.8 13.8 %copy.62 = bf16[2048,2560]{1,0:T(8,128)(2,1)} copy(bf16[2048,2560]{0,1:T(8,128)(2,1)} %bitcast.130) | data formatting | bytes 20971520 | tf_op jit(solution)/shard_map/dot_general | solution.py:19
  765.6 1.5 broadcast_in_dim.117.scale_row
  767.1 41.5 %shard_map.258 = (bf16[8,320,768]{2,1,0:T(8,128)(2,1)}, bf16[8,320,768]{2,1,0:T(8,128)(2,1)}) custom-call(s32[2]{0:T(128)} %bitcast.165, bf16[8,320,256]{2,1,0:T(8,128)(2,1)} %get-tuple-element.69.query, bf16[8,320,256]{2,1,0:T(8,128)(2,1)} %get-tuple-element.70.keyed, bf16[8,320,256]{2,1,0:T(8,128)(2,1)} %get-tuple-element.71.value, ...), custom_call_target="tpu_custom_call" | custom-call | flops 1000000000 | bytes 3000000 | tf_op jit(solution)/shard_map/pallas_call | solution.py:249
  808.6 6.5 copy.63
  815.1 2.9 reduce_sum.79
  817.9 12.4 %fusion.37 = bf16[8,256,3,256]{3,1,2,0:T(8,128)(2,1)S(1)} fusion(bf16[8,256,2560,1]{2,1,3,0:T(8,128)(2,1)} %bitcast.140, bf16[3,256,2560,1]{2,1,0,3:T(8,128)(2,1)} %bitcast.149), kind=kOutput, calls=%fused_computation.102 | convolution fusion | flops 8053063680 | bytes 17563648 | tf_op jit(solution)/shard_map/dot_general | solution.py:19
  830.7 120.2 %all_to_all.44 = bf16[8,272,3,1,256]{4,1,2,3,0:T(8,128)(2,1)S(1)} all-to-all(bf16[8,272,3,1,256]{4,1,2,3,0:T(8,128)(2,1)S(1)} %maximum_bitcast_fusion), channel_id=1, replica_groups=mesh['rep'=4,'fsdp'=8] {'fsdp'}, dimensions={0} | all-to-all | bytes 6684672 | tf_op jit(solution)/shard_map/all_to_all | solution.py:866
  950.9 3.0 copy.65
  953.9 6.0 reshape_squeeze.11
  959.9 26.2 %all-reduce.8.cloned.1.call-done = bf16[4224,2048]{1,0:T(8,128)(2,1)} async-done(((bf16[4224,2048]{1,0:T(8,128)(2,1)}), bf16[4224,2048]{1,0:T(8,128)(2,1)}) %all-reduce.8.cloned.1.call-update) | async-done | bytes 17301520 | tf_op jit(solution)/shard_map/psum | solution.py:686
  986.3 13.6 %fusion.38 = bf16[2560,2048]{1,0:T(8,128)(2,1)} fusion(bf16[2560,768]{1,0:T(8,128)(2,1)} %bitcast.147, bf16[2048,768]{1,0:T(8,128)(2,1)} %bitcast.177), kind=kOutput, calls=%fused_computation.103 | convolution fusion | flops 8053063680 | bytes 17563648 | tf_op jit(solution)/shard_map/dot_general | solution.py:19
  1001.7 9.4 slice.116
  1011.1 3.3 slice.114
  1014.4 6.1 slice.115
  1020.6 3.1 convert_bitcast_fusion
  1023.7 9.4 copy.67
  1034.5 8.9 convert_bitcast_fusion.1
  1043.4 55.9 %all-reduce.10.cloned.1.call-done = (bf16[272,6144]{1,0:T(8,128)(2,1)}, bf16[256,2176]{0,1:T(8,128)(2,1)}) async-done(((bf16[272,6144]{1,0:T(8,128)(2,1)}, bf16[256,2176]{0,1:T(8,128)(2,1)}), (bf16[272,6144]{1,0:T(8,128)(2,1)}, bf16[256,2176]{0,1:T(8,128)(2,1)})) %all-reduce.10.cloned.1.call-update) | async-done | bytes 4456464 | tf_op jit(solution)/shard_map/psum | solution.py:686
  1099.3 2.7 slice_convert_fusion
  1102.0 2.9 copy.66
  1108.6 8.0 convert_multiply_fusion
  1116.6 1.9 fusion.9
  1118.6 4.3 fusion.11
  (165 shorter events, 30.5 us)
Async XLA Ops:
  8.0 4.5 copy-start
  8.0 5.2 copy-start.23
  8.0 5.4 copy-start.25
  8.0 5.4 copy-start.27
  8.1 5.4 copy-start.26
  148.5 7.4 copy-start.18
  148.5 7.5 copy-start.19
  148.5 7.8 copy-start.24
  148.5 9.8 copy-start.20
  148.5 46.7 %collective-permute-start = (bf16[320,2048]{1,0:T(8,128)(2,1)}, bf16[320,2048]{1,0:T(8,128)(2,1)}, u32[]{:S(2)}, u32[]{:S(2)}) collective-permute-start(bf16[320,2048]{1,0:T(8,128)(2,1)} %param.20), channel_id=1, source_target_pairs={{0,2},{1,3},{2,4},{3,5},{4,6},{5,7},{6,0},{7,1},{8,10},{9,11},{10,... | collective-permute-start | bytes 3932168 | tf_op jit(solution)/shard_map/ppermute | solution.py:277
  149.7 121.2 %collective-permute-start.1 = (bf16[320,2048]{1,0:T(8,128)(2,1)}, bf16[320,2048]{1,0:T(8,128)(2,1)}, u32[]{:S(2)}, u32[]{:S(2)}) collective-permute-start(bf16[320,2048]{1,0:T(8,128)(2,1)} %param.20), channel_id=1, source_target_pairs={{0,1},{1,0},{2,3},{3,2},{4,5},{5,4},{6,7},{7,6},{8,9},{9,8},{10,11... | collective-permute-start | bytes 3932168 | tf_op jit(solution)/shard_map/ppermute | solution.py:288
  156.2 0.6 copy-start.16
  158.3 156.7 %copy-start.14 = (f32[1,2,8,128]{3,1,2,0:T(2,128)}, f32[1,2,8,128]{3,1,2,0:T(2,128)S(1)}, u32[]{:S(2)}) copy-start(f32[1,2,8,128]{3,1,2,0:T(2,128)S(1)} %copy.72) | copy-start | bytes 24580
  195.2 88.4 %collective-permute-start.2 = (bf16[320,2048]{1,0:T(8,128)(2,1)}, bf16[320,2048]{1,0:T(8,128)(2,1)}, u32[]{:S(2)}, u32[]{:S(2)}) collective-permute-start(bf16[320,2048]{1,0:T(8,128)(2,1)} %collective-permute-done), channel_id=1, source_target_pairs={{0,1},{1,0},{2,3},{3,2},{4,5},{5,4},{6,7},{7,6},{8,9},{9,8},{10,11... | collective-permute-start | bytes 3932168 | tf_op jit(solution)/shard_map/ppermute | solution.py:288
  195.7 85.8 %collective-permute-start.3 = (bf16[320,2048]{1,0:T(8,128)(2,1)}, bf16[320,2048]{1,0:T(8,128)(2,1)}, u32[]{:S(2)}, u32[]{:S(2)}) collective-permute-start(bf16[320,2048]{1,0:T(8,128)(2,1)} %collective-permute-done), channel_id=1, source_target_pairs={{0,2},{1,3},{2,4},{3,5},{4,6},{5,7},{6,0},{7,1},{8,10},{9,11},{10,... | collective-permute-start | bytes 3932168 | tf_op jit(solution)/shard_map/ppermute | solution.py:277
  235.1 53.6 %all-to-all-start = ((bf16[8,320,256]{2,1,0:T(8,128)(2,1)}), bf16[8,320,256]{2,1,0:T(8,128)(2,1)}, u32[]{:S(2)}, u32[]{:S(2)}) async-start(bf16[8,320,256]{2,1,0:T(8,128)(2,1)} %get-tuple-element.55.attended), calls=%async_computation | async-start | bytes 2621440 | tf_op jit(solution)/shard_map/all_to_all | solution.py:793
  240.1 425.4 %all-reduce.6.cloned.1.call-start = ((), (), s32[]{:S(2)}) async-start(), calls=%async_computation.9 | async-start | bytes 17825792 | tf_op jit(solution)/shard_map/psum | solution.py:686
  261.7 4.9 copy-start.4
  266.6 10.7 slice-start.3
  266.7 10.7 slice-start.4
  270.1 7.2 copy-start.9
  277.4 4.1 copy-start.12
  281.4 8.8 copy-start.5
  281.4 35.0 %collective-permute-start.4 = (bf16[320,2048]{1,0:T(8,128)(2,1)}, bf16[320,2048]{1,0:T(8,128)(2,1)}, u32[]{:S(2)}, u32[]{:S(2)}) collective-permute-start(bf16[320,2048]{1,0:T(8,128)(2,1)} %collective-permute-done.3), channel_id=1, source_target_pairs={{0,1},{1,0},{2,3},{3,2},{4,5},{5,4},{6,7},{7,6},{8,9},{9,8},{10,11... | collective-permute-start | bytes 3932168 | tf_op jit(solution)/shard_map/ppermute | solution.py:288
  282.0 33.1 %collective-permute-start.5 = (bf16[320,2048]{1,0:T(8,128)(2,1)}, bf16[320,2048]{1,0:T(8,128)(2,1)}, u32[]{:S(2)}, u32[]{:S(2)}) collective-permute-start(bf16[320,2048]{1,0:T(8,128)(2,1)} %collective-permute-done.3), channel_id=1, source_target_pairs={{0,2},{1,3},{2,4},{3,5},{4,6},{5,7},{6,0},{7,1},{8,10},{9,11},{10,... | collective-permute-start | bytes 3932168 | tf_op jit(solution)/shard_map/ppermute | solution.py:277
  290.2 6.0 copy-start.11
  296.2 26.4 %copy-start.2 = (f32[320,2048]{1,0:T(8,128)}, f32[320,2048]{1,0:T(8,128)S(1)}, u32[]{:S(2)}) copy-start(f32[320,2048]{1,0:T(8,128)S(1)} %get-tuple-element.157) | copy-start | bytes 7864324
  296.2 26.4 %copy-start.21 = (f32[320]{0:T(512)}, f32[320]{0:T(512)S(1)}, u32[]{:S(2)}) copy-start(f32[320]{0:T(512)S(1)} %add_rsqrt_fusion.2) | copy-start | bytes 3844
  315.1 6.4 collective-permute-start.6
  482.1 183.4 %reduce-scatter.5.cloned.1.call-start = ((), (), s32[]{:S(2)}) async-start(), calls=%async_computation.7 | async-start | bytes 11796480 | tf_op jit(solution)/shard_map/reduce_scatter | solution.py:827
  540.2 0.9 copy-start.13
  540.3 419.6 %reduce-scatter.9.cloned.1.call-start = ((), (), s32[]{:S(2)}) async-start(), calls=%async_computation.11 | async-start | bytes 11796480 | tf_op jit(solution)/shard_map/reduce_scatter | solution.py:871
  573.2 412.8 %all-reduce.8.cloned.1.call-start = ((), (), s32[]{:S(2)}) async-start(), calls=%async_computation.10 | async-start | bytes 34603008 | tf_op jit(solution)/shard_map/psum | solution.py:686
  644.8 20.8 %copy-start.15 = (f32[1,2,8,128]{3,1,2,0:T(2,128)S(1)}, f32[1,2,8,128]{3,1,2,0:T(2,128)}, u32[]{:S(2)}) copy-start(f32[1,2,8,128]{3,1,2,0:T(2,128)} %copy-done.14) | copy-start | bytes 24580
  644.8 20.8 %copy-start.22 = (f32[320]{0:T(512)S(1)}, f32[320]{0:T(512)}, u32[]{:S(2)}) copy-start(f32[320]{0:T(512)} %copy-done.21) | copy-start | bytes 3844
  671.9 1.5 copy-start.7
  682.1 58.3 %all-to-all-start.1 = ((bf16[320,8,256]{2,0,1:T(8,128)(2,1)}), bf16[320,8,256]{2,0,1:T(8,128)(2,1)S(1)}, u32[]{:S(2)}, u32[]{:S(2)}) async-start(bf16[320,8,256]{2,0,1:T(8,128)(2,1)} %fusion.13), calls=%async_computation.2 | async-start | bytes 2621440 | tf_op jit(solution)/shard_map/all_to_all | solution.py:843
  686.8 299.3 %reduce-scatter.7.cloned.1.call-start = ((), (), s32[]{:S(2)}) async-start(), calls=%async_computation.8 | async-start | bytes 10027008 | tf_op jit(solution)/shard_map/reduce_scatter | solution.py:852
  740.4 7.2 copy-start.8
  751.7 347.6 %all-reduce.10.cloned.1.call-start = ((), (), s32[]{:S(2)}) async-start(), calls=%async_computation.13 | async-start | bytes 8912896 | tf_op jit(solution)/shard_map/psum | solution.py:686
  751.8 13.9 %copy-start.17 = (f32[8,320]{1,0:T(8,128)S(1)}, f32[8,320]{1,0:T(8,128)}, u32[]{:S(2)}) copy-start(f32[8,320]{1,0:T(8,128)} %copy-done.16) | copy-start | bytes 30724
  986.1 130.6 %reduce-scatter.11.cloned.1.call-start = ((), (), s32[]{:S(2)}) async-start(), calls=%async_computation.12 | async-start | bytes 11796480 | tf_op jit(solution)/shard_map/reduce_scatter | solution.py:876
  1000.0 0.7 copy-start.28
  1000.0 1.3 copy-start.6
  1000.0 11.1 slice-start
  1001.3 9.8 slice-start.1
  1001.7 9.4 slice-start.2
  1023.7 9.4 copy-start.3
  1023.7 9.4 copy-start.10
  1108.6 14.2 %copy-start.1 = (bf16[256,2048]{1,0:T(8,128)(2,1)S(1)}, bf16[256,2048]{1,0:T(8,128)(2,1)}, u32[]{:S(2)}) copy-start(bf16[256,2048]{1,0:T(8,128)(2,1)} %param.24) | copy-start | bytes 3145732
Sparse Core Ops, SparseCore 0:
  482.2 183.2 all-reduce.5
  669.4 316.6 all-reduce.7
  990.1 109.2 all-reduce.9
Sparse Core Ops, SparseCore 1:
  540.4 112.6 reduce-scatter.4
  655.8 128.7 reduce-scatter.8
  787.3 142.7 reduce-scatter.6
  1000.1 109.9 reduce-scatter.10

commit v5 on v4

--- a/solution.py
+++ b/solution.py
@@ -497,9 +497,16 @@
     open_kernel(around + across)
 
     owners = [lax.rem(mine + devices - 2 * s, devices) for s in range(steps)]
-    inputs = (token, share, small)
-    whole = (token_all, share_all.at[:, copy], small_all)
+    half = token.shape[0] // 2
+    inputs = (token.at[pl.ds(0, half)], share, small, token.at[pl.ds(half, half)])
     everything = []
+
+    def spot(j, owner):
+        if j == 1:
+            return share_all.at[owner, copy]
+        if j == 2:
+            return small_all.at[owner]
+        return token_all.at[owner, pl.ds(0 if j == 0 else half, half)]
 
     def begin(one):
         one.start()
@@ -513,35 +520,26 @@
         pltpu.make_async_copy(strip.at[mine], strip_all.at[mine, copy], local_done.at[3]),
     ]
     def ring_step(j, s):
-        source = inputs[j] if s == 0 else whole[j].at[owners[s]]
+        target = spot(j, owners[s])
+        source = inputs[j] if s == 0 else target
         if s + 1 < steps:
             begin(
                 remote(
-                    source,
-                    whole[j].at[owners[s]],
-                    ring_sent.at[j, s],
-                    ring_got.at[j, s],
-                    {"fsdp": right},
+                    source, target, ring_sent.at[j, s], ring_got.at[j, s], {"fsdp": right}
                 )
             )
-        begin(
+        begin(remote(source, target, twin_sent.at[j, s], twin_got.at[j, s], {"fsdp": twin}))
+
+    def ring_pass(j, s):
+        if 0 < s < steps:
             remote(
-                source,
-                whole[j].at[owners[s]],
-                twin_sent.at[j, s],
-                twin_got.at[j, s],
-                {"fsdp": twin},
-            )
-        )
-
-    def ring_wait(j, s):
-        remote(
-            inputs[j],
-            whole[j].at[owners[s + 1]],
-            ring_sent.at[j, s],
-            ring_got.at[j, s],
-            {"fsdp": right},
-        ).wait_recv()
+                inputs[j],
+                spot(j, owners[s]),
+                ring_sent.at[j, s - 1],
+                ring_got.at[j, s - 1],
+                {"fsdp": right},
+            ).wait_recv()
+            ring_step(j, s)
 
     shared = {}
 
@@ -561,6 +559,7 @@
     ring_step(1, 0)
     ring_step(2, 0)
     ring_step(0, 0)
+    ring_step(3, 0)
     deals = []
     for k in range(1, devices):
         peer = lax.rem(mine + k, devices)
@@ -580,12 +579,14 @@
         one.start()
     for s in range(1, steps):
         for j in (1, 2):
-            ring_wait(j, s - 1)
-            ring_step(j, s)
+            ring_pass(j, s)
         share_cross(s)
-    if steps > 1:
-        ring_wait(0, 0)
-        ring_step(0, 1)
+        if s == 1:
+            ring_pass(0, 1)
+        if s == 2:
+            ring_pass(3, 1)
+    if steps == 2:
+        ring_pass(3, 1)
     locals_[3].wait()
     for one in deals:
         one.wait_recv()
@@ -602,9 +603,8 @@
                 )
             )
         )
-    if steps > 2:
-        ring_wait(0, 1)
-        ring_step(0, 2)
+    ring_pass(0, 2)
+    ring_pass(3, 2)
     for s in range(steps):
         for k in range(1, reps):
             origin = lax.rem(copy + reps - k, reps)
@@ -619,15 +619,15 @@
                 )
             )
     for s in range(3, steps):
-        ring_wait(0, s - 1)
-        ring_step(0, s)
+        ring_pass(0, s)
+        ring_pass(3, s)
     for one in everything:
         one.wait_send()
-    for j in range(3):
+    for j in range(4):
         for s in range(steps):
             remote(
                 inputs[j],
-                whole[j].at[owners[s]],
+                spot(j, owners[s]),
                 twin_sent.at[j, s],
                 twin_got.at[j, s],
                 {"fsdp": twin},
@@ -663,10 +663,10 @@
             jax.ShapeDtypeStruct((devices,) + small.shape, LOW),
         ],
         scratch_shapes=[
-            dma((3, steps)),
-            dma((3, steps)),
-            dma((3, steps)),
-            dma((3, steps)),
+            dma((4, steps)),
+            dma((4, steps)),
+            dma((4, steps)),
+            dma((4, steps)),
             dma((devices - 1,)),
             dma((devices - 1,)),
             dma((reps - 1,)),

time: 1130 us -> 1160 us (1.027)
  starting transfers between devices: 14.7 us -> 48.5 us
    ppermute x3, starting transfers between devices: 2.9 us -> 36.6 us  [ring_blocks(): blocks.append(lax.ppermute(blocks[-1], 'fsdp', ring))]
  transfers between devices with their start and end apart: 16 -> 16, of which waited for: 5 -> 5; matrix products, arithmetic and copies ran while one was open for 37% -> 36% of each run, Pallas kernels for 7% -> 7%
where the time goes in v5:
time: 1160 us
  Pallas kernels  337 us (29%)
  matrix products  239 us (21%)
  waiting for transfers between devices  174 us (15%)
  local copies, waits for them, and re-layouts  140 us (12%)
  blocking collectives  120 us (10%)
  other arithmetic  84 us (7%)
  starting transfers between devices  48.5 us (4%)
  between operations  16.4 us (1%)
    dot_general x10, matrix products, dot(): lax.dot_general(left, right, ((dims[0], dims[1]), ((), ())), preferred_el...  239 us
    pallas_call x1, Pallas kernels, gather_all(): pl.pallas_call(functools.partial(gather_kernel, devices, reps), in_specs=...  129 us
    pallas_call x1, Pallas kernels, middle(): pl.pallas_call(functools.partial(middle_kernel, devices, experts), in_spe...  129 us
    all_to_all x1, blocking collectives, shards(): lax.all_to_all(weight_grad, 'fsdp', split_axis=0, concat_axis=2, tiled=Fa...  120 us
    psum x3, waiting for transfers between devices, reduce_rep(): return lax.psum(values, 'rep')  103 us
    all_to_all x1, waiting for transfers between devices, shards(): lax.all_to_all(attended_back, 'fsdp', split_axis=1, concat_axis=0, tiled=...  52.2 us
    pallas_call x1, Pallas kernels, attend_back(): pl.pallas_call(functools.partial(attend_back_kernel, size, held), in_spec...  41.5 us
    pallas_call x1, Pallas kernels, attend(): pl.pallas_call(functools.partial(attend_kernel, size, held), in_specs=[pl...  38.1 us
  transfers between devices with their start and end apart: 16, of which 5 were waited for; matrix products, arithmetic and copies ran while one was open for 36% of the time, Pallas kernels for 7%

profile of v5, /device:TPU:0, one launch (start us, length us, event | category | flops | bytes accessed | tf_op | source)
XLA Modules:
  0.0 1158.9 jit_solution(2708371719029076163)
XLA Ops:
  10.8 1.7 reshape.256.strip
  14.1 128.8 %shard_map.255 = (bf16[8,320,2048]{2,1,0:T(8,128)(2,1)}, bf16[8,4,64,768]{3,2,1,0:T(8,128)(2,1)}, bf16[8,4,64,2048]{3,2,1,0:T(8,128)(2,1)}, bf16[8,32,128]{2,1,0:T(8,128)(2,1)}) custom-call(bf16[320,2048]{1,0:T(8,128)(2,1)} %token_.1, bf16[8,64,768]{2,1,0:T(8,128)(2,1)} %reshape.256.strip, bf16[64,2048]{1,0:T(8,128)(2,1)} %constant_dynamic-slice_fusion.share, ...), custom_call_target="tpu_custom_call" | custom-call | flops 99999997952 | bytes 300000000 | tf_op jit(solution)/shard_map/pallas_call | solution.py:655
  143.0 34.9 %collective-permute-start = (bf16[320,2048]{1,0:T(8,128)(2,1)}, bf16[320,2048]{1,0:T(8,128)(2,1)}, u32[]{:S(2)}, u32[]{:S(2)}) collective-permute-start(bf16[320,2048]{1,0:T(8,128)(2,1)} %param.20), channel_id=1, source_target_pairs={{0,2},{1,3},{2,4},{3,5},{4,6},{5,7},{6,0},{7,1},{8,10},{9,11},{10,... | collective-permute-start | bytes 3932168 | tf_op jit(solution)/shard_map/ppermute | solution.py:277
  177.9 6.1 multiply_reduce_fusion
  186.6 2.2 fusion.1
  189.8 6.2 fusion.21
  196.1 14.0 %multiply_add_fusion = f32[2560,768]{1,0:T(8,128)} fusion(bf16[2560,2048]{1,0:T(8,128)(2,1)} %bitcast.129, bf16[2048,768]{1,0:T(8,128)(2,1)} %bitcast.176, f32[768]{0:T(1024)S(1)} %reshape.277, f32[2560]{0:T(1024)S(1)} %rsqrt.32), kind=kOutput, calls=%fused_computation.9 | convolution fusion | flops 8056995840 | bytes 21509120 | tf_op jit(solution)/shard_map/dot_general | solution.py:19
  210.2 4.4 pad_maximum_fusion.3
  214.6 5.4 broadcast_in_dim.101
  220.0 2.5 bitcast_dynamic-update-slice_fusion.9
  225.3 38.1 %shard_map.256 = (bf16[8,320,256]{2,1,0:T(8,128)(2,1)}, bf16[8,320,256]{2,1,0:T(8,128)(2,1)}, bf16[8,320,256]{2,1,0:T(8,128)(2,1)}, bf16[8,320,256]{2,1,0:T(8,128)(2,1)}, f32[8,320,256]{2,1,0:T(8,128)}) custom-call(s32[2]{0:T(128)} %bitcast.164, f32[8,320,768]{2,1,0:T(8,128)} %bitcast.175, f32[8,320,128]{2,1,0:T(8,128)} %get-tuple-element.158.cosine, ...), custom_call_target="tpu_custom_call" | custom-call | flops 30000001024 | bytes 90000000 | tf_op jit(solution)/shard_map/pallas_call | solution.py:232
  263.3 5.0 all-to-all-start
  268.8 3.8 bitcast_dynamic-update-slice_fusion.1
  272.6 11.2 fusion.33
  283.8 6.2 constant_dynamic-update-slice_fusion.1
  290.7 4.2 bitcast_dynamic-update-slice_fusion
  294.9 3.4 constant_dynamic-update-slice_fusion
  299.0 3.1 bitcast_dynamic-update-slice_fusion.8
  302.1 2.5 bitcast_dynamic-update-slice_fusion.7
  305.6 4.1 pad_maximum_fusion.1.down_far
  310.2 1.7 collective-permute-start.5
  311.9 2.5 bitcast_dynamic-update-slice_fusion.6
  314.4 2.5 bitcast_dynamic-update-slice_fusion.5
  318.4 5.9 multiply_reduce_fusion.1
  324.4 18.9 %collective-permute-done.5 = bf16[320,2048]{1,0:T(8,128)(2,1)} collective-permute-done((bf16[320,2048]{1,0:T(8,128)(2,1)}, bf16[320,2048]{1,0:T(8,128)(2,1)}, u32[]{:S(2)}, u32[]{:S(2)}) %collective-permute-start.5) | collective-permute-done | bytes 1310752 | tf_op jit(solution)/shard_map/ppermute | solution.py:277
  344.6 2.5 bitcast_dynamic-update-slice_fusion.4
  347.1 2.5 bitcast_dynamic-update-slice_fusion.3
  350.8 128.8 %shard_map.257 = (bf16[8,320,2048]{2,1,0:T(8,128)(2,1)}, bf16[8,320,2176]{2,1,0:T(8,128)(2,1)}, bf16[8,320,4480]{2,1,0:T(8,128)(2,1)}) custom-call(bf16[320,2048]{1,0:T(8,128)(2,1)} %multiply_convert_fusion.hidden, bf16[8,320,2048]{2,1,0:T(8,128)(2,1)} %bitcast_dynamic-update-slice_fusion.2.cot_all, bf16[4480,2048]{1,0:T(8,128)(2,1)} %fusion.20.weights_far, ...), custom_call_target="tpu_custom_call" | custom-call | flops 109999996928 | bytes 330000000 | tf_op jit(solution)/shard_map/pallas_call | solution.py:443
  479.6 30.6 %convolution_bitcast_fusion = bf16[2176,2048]{1,0:T(8,128)(2,1)} fusion(bf16[8,320,2176]{2,1,0:T(8,128)(2,1)} %get-tuple-element.62, bf16[8,320,2048]{2,1,0:T(8,128)(2,1)} %bitcast_dynamic-update-slice_fusion.2.cot_all), kind=kOutput, calls=%fused_computation.4 | convolution fusion | flops 22817013760 | bytes 30539776 | tf_op jit(solution)/shard_map/dot_general | solution.py:19
  510.4 58.1 %fusion.35 = bf16[2560,2048]{1,0:T(8,128)(2,1)} fusion(bf16[2560,4480]{1,0:T(8,128)(2,1)} %bitcast.169, bf16[4480,2048]{1,0:T(8,128)(2,1)} %fusion.20.weights_far), kind=kOutput, calls=%fused_computation.100 | convolution fusion | flops 46976204800 | bytes 51773440 | tf_op jit(solution)/shard_map/dot_general | solution.py:19
  569.4 32.0 %fusion.31 = bf16[2560,2048]{1,0:T(8,128)(2,1)} fusion(bf16[2560,2176]{1,0:T(8,128)(2,1)} %bitcast.171, bf16[64,2048]{1,0:T(8,128)(2,1)S(1)} %copy-done.13, bf16[1408,2048]{1,0:T(8,128)(2,1)} %bitcast.141, bf16[704,2048]{1,0:T(8,128)(2,1)} %param.29), kind=kOutput, calls=%fused_computation.96 | convolution fusion | flops 22843752448 | bytes 30539776 | tf_op jit(solution)/shard_map/dot_general | solution.py:19
  601.5 55.9 %fusion.36 = bf16[4480,2048]{1,0:T(8,128)(2,1)} fusion(bf16[2560,4480]{1,0:T(8,128)(2,1)} %bitcast.170, bf16[2560,2048]{1,0:T(8,128)(2,1)} %bitcast.172), kind=kOutput, calls=%fused_computation.101 | convolution fusion | flops 46976204800 | bytes 51773440 | tf_op jit(solution)/shard_map/dot_general | solution.py:19
  657.5 7.7 fusion.32
  665.2 7.7 pad_maximum_fusion
  672.9 21.0 %all-reduce.6.cloned.1.call-done = bf16[2176,2048]{1,0:T(8,128)(2,1)} async-done(((bf16[2176,2048]{1,0:T(8,128)(2,1)}), bf16[2176,2048]{1,0:T(8,128)(2,1)}) %all-reduce.6.cloned.1.call-update) | async-done | bytes 8912912 | tf_op jit(solution)/shard_map/psum | solution.py:686
  694.0 3.0 fusion.5
  697.0 3.3 fusion.7
  701.9 8.7 fusion.13
  710.5 4.7 all-to-all-start.1
  716.6 52.2 %all-to-all-done.1 = bf16[320,8,256]{2,0,1:T(8,128)(2,1)S(1)} async-done(((bf16[320,8,256]{2,0,1:T(8,128)(2,1)}), bf16[320,8,256]{2,0,1:T(8,128)(2,1)S(1)}, u32[]{:S(2)}, u32[]{:S(2)}) %all-to-all-start.1) | async-done | bytes 1310752 | tf_op jit(solution)/shard_map/all_to_all | solution.py:843
  768.9 7.2 fusion.16
  776.1 4.0 pad_maximum_fusion.2
  780.2 13.8 %copy.62 = bf16[2048,2560]{1,0:T(8,128)(2,1)} copy(bf16[2048,2560]{0,1:T(8,128)(2,1)} %bitcast.130) | data formatting | bytes 20971520 | tf_op jit(solution)/shard_map/dot_general | solution.py:19
  795.6 41.5 %shard_map.258 = (bf16[8,320,768]{2,1,0:T(8,128)(2,1)}, bf16[8,320,768]{2,1,0:T(8,128)(2,1)}) custom-call(s32[2]{0:T(128)} %bitcast.165, bf16[8,320,256]{2,1,0:T(8,128)(2,1)} %get-tuple-element.69.query, bf16[8,320,256]{2,1,0:T(8,128)(2,1)} %get-tuple-element.70.keyed, bf16[8,320,256]{2,1,0:T(8,128)(2,1)} %get-tuple-element.71.value, ...), custom_call_target="tpu_custom_call" | custom-call | flops 1000000000 | bytes 3000000 | tf_op jit(solution)/shard_map/pallas_call | solution.py:249
  837.0 6.5 copy.63
  843.5 2.9 reduce_sum.79
  846.4 12.4 %fusion.37 = bf16[8,256,3,256]{3,1,2,0:T(8,128)(2,1)S(1)} fusion(bf16[8,256,2560,1]{2,1,3,0:T(8,128)(2,1)} %bitcast.140, bf16[3,256,2560,1]{2,1,0,3:T(8,128)(2,1)} %bitcast.149), kind=kOutput, calls=%fused_computation.102 | convolution fusion | flops 8053063680 | bytes 17563648 | tf_op jit(solution)/shard_map/dot_general | solution.py:19
  859.1 120.3 %all_to_all.44 = bf16[8,272,3,1,256]{4,1,2,3,0:T(8,128)(2,1)S(1)} all-to-all(bf16[8,272,3,1,256]{4,1,2,3,0:T(8,128)(2,1)S(1)} %maximum_bitcast_fusion), channel_id=1, replica_groups=mesh['rep'=4,'fsdp'=8] {'fsdp'}, dimensions={0} | all-to-all | bytes 6684672 | tf_op jit(solution)/shard_map/all_to_all | solution.py:866
  979.4 3.0 copy.65
  982.3 6.0 reshape_squeeze.11
  988.3 26.2 %all-reduce.8.cloned.1.call-done = bf16[4224,2048]{1,0:T(8,128)(2,1)} async-done(((bf16[4224,2048]{1,0:T(8,128)(2,1)}), bf16[4224,2048]{1,0:T(8,128)(2,1)}) %all-reduce.8.cloned.1.call-update) | async-done | bytes 17301520 | tf_op jit(solution)/shard_map/psum | solution.py:686
  1014.8 13.6 %fusion.38 = bf16[2560,2048]{1,0:T(8,128)(2,1)} fusion(bf16[2560,768]{1,0:T(8,128)(2,1)} %bitcast.147, bf16[2048,768]{1,0:T(8,128)(2,1)} %bitcast.177), kind=kOutput, calls=%fused_computation.103 | convolution fusion | flops 8053063680 | bytes 17563648 | tf_op jit(solution)/shard_map/dot_general | solution.py:19
  1030.1 9.4 slice.116
  1039.6 3.3 slice.114
  1042.9 6.1 slice.115
  1049.0 3.1 convert_bitcast_fusion
  1052.2 9.4 copy.67
  1063.0 8.9 convert_bitcast_fusion.1
  1071.9 55.9 %all-reduce.10.cloned.1.call-done = (bf16[272,6144]{1,0:T(8,128)(2,1)}, bf16[256,2176]{0,1:T(8,128)(2,1)}) async-done(((bf16[272,6144]{1,0:T(8,128)(2,1)}, bf16[256,2176]{0,1:T(8,128)(2,1)}), (bf16[272,6144]{1,0:T(8,128)(2,1)}, bf16[256,2176]{0,1:T(8,128)(2,1)})) %all-reduce.10.cloned.1.call-update) | async-done | bytes 4456464 | tf_op jit(solution)/shard_map/psum | solution.py:686
  1127.8 2.7 slice_convert_fusion
  1130.5 2.9 copy.66
  1137.1 8.0 convert_multiply_fusion
  1145.1 1.9 fusion.9
  1147.0 4.3 fusion.11
  (165 shorter events, 30.9 us)
Async XLA Ops:
  8.0 4.5 copy-start
  8.0 5.2 copy-start.23
  8.0 5.4 copy-start.25
  8.0 5.4 copy-start.27
  8.1 5.4 copy-start.26
  142.9 41.1 %copy-start.18 = (s32[2560]{0:T(1024)S(1)}, s32[2560]{0:T(1024)}, u32[]{:S(2)}) copy-start(s32[2560]{0:T(1024)} %param.18) | copy-start | bytes 30724
  142.9 41.3 %copy-start.19 = (bf16[8,32,128]{2,1,0:T(8,128)(2,1)S(1)}, bf16[8,32,128]{2,1,0:T(8,128)(2,1)}, u32[]{:S(2)}) copy-start(bf16[8,32,128]{2,1,0:T(8,128)(2,1)} %get-tuple-element.52) | copy-start | bytes 196612
  142.9 41.6 %copy-start.24 = (s32[1,2]{1,0:T(1,128)S(1)}, s32[1,2]{1,0:T(1,128)}, u32[]{:S(2)}) copy-start(s32[1,2]{1,0:T(1,128)} %param.17) | copy-start | bytes 28
  143.0 43.6 %copy-start.20 = (s32[2560,4]{0,1:T(4,128)S(1)}, s32[2560,4]{0,1:T(4,128)}, u32[]{:S(2)}) copy-start(s32[2560,4]{0,1:T(4,128)} %param.19) | copy-start | bytes 122884
  143.0 80.5 %collective-permute-start = (bf16[320,2048]{1,0:T(8,128)(2,1)}, bf16[320,2048]{1,0:T(8,128)(2,1)}, u32[]{:S(2)}, u32[]{:S(2)}) collective-permute-start(bf16[320,2048]{1,0:T(8,128)(2,1)} %param.20), channel_id=1, source_target_pairs={{0,2},{1,3},{2,4},{3,5},{4,6},{5,7},{6,0},{7,1},{8,10},{9,11},{10,... | collective-permute-start | bytes 3932168 | tf_op jit(solution)/shard_map/ppermute | solution.py:277
  177.9 121.2 %collective-permute-start.1 = (bf16[320,2048]{1,0:T(8,128)(2,1)}, bf16[320,2048]{1,0:T(8,128)(2,1)}, u32[]{:S(2)}, u32[]{:S(2)}) collective-permute-start(bf16[320,2048]{1,0:T(8,128)(2,1)} %param.20), channel_id=1, source_target_pairs={{0,1},{1,0},{2,3},{3,2},{4,5},{5,4},{6,7},{7,6},{8,9},{9,8},{10,11... | collective-permute-start | bytes 3932168 | tf_op jit(solution)/shard_map/ppermute | solution.py:288
  184.4 0.6 copy-start.16
  186.5 156.7 %copy-start.14 = (f32[1,2,8,128]{3,1,2,0:T(2,128)}, f32[1,2,8,128]{3,1,2,0:T(2,128)S(1)}, u32[]{:S(2)}) copy-start(f32[1,2,8,128]{3,1,2,0:T(2,128)S(1)} %copy.72) | copy-start | bytes 24580
  223.4 88.4 %collective-permute-start.2 = (bf16[320,2048]{1,0:T(8,128)(2,1)}, bf16[320,2048]{1,0:T(8,128)(2,1)}, u32[]{:S(2)}, u32[]{:S(2)}) collective-permute-start(bf16[320,2048]{1,0:T(8,128)(2,1)} %collective-permute-done), channel_id=1, source_target_pairs={{0,1},{1,0},{2,3},{3,2},{4,5},{5,4},{6,7},{7,6},{8,9},{9,8},{10,11... | collective-permute-start | bytes 3932168 | tf_op jit(solution)/shard_map/ppermute | solution.py:288
  223.9 85.8 %collective-permute-start.3 = (bf16[320,2048]{1,0:T(8,128)(2,1)}, bf16[320,2048]{1,0:T(8,128)(2,1)}, u32[]{:S(2)}, u32[]{:S(2)}) collective-permute-start(bf16[320,2048]{1,0:T(8,128)(2,1)} %collective-permute-done), channel_id=1, source_target_pairs={{0,2},{1,3},{2,4},{3,5},{4,6},{5,7},{6,0},{7,1},{8,10},{9,11},{10,... | collective-permute-start | bytes 3932168 | tf_op jit(solution)/shard_map/ppermute | solution.py:277
  263.3 53.6 %all-to-all-start = ((bf16[8,320,256]{2,1,0:T(8,128)(2,1)}), bf16[8,320,256]{2,1,0:T(8,128)(2,1)}, u32[]{:S(2)}, u32[]{:S(2)}) async-start(bf16[8,320,256]{2,1,0:T(8,128)(2,1)} %get-tuple-element.55.attended), calls=%async_computation | async-start | bytes 2621440 | tf_op jit(solution)/shard_map/all_to_all | solution.py:793
  268.4 425.6 %all-reduce.6.cloned.1.call-start = ((), (), s32[]{:S(2)}) async-start(), calls=%async_computation.9 | async-start | bytes 17825792 | tf_op jit(solution)/shard_map/psum | solution.py:686
  290.0 4.9 copy-start.4
  294.9 10.7 slice-start.3
  294.9 10.7 slice-start.4
  298.3 7.2 copy-start.9
  305.6 4.1 copy-start.12
  309.6 8.8 copy-start.5
  309.7 35.0 %collective-permute-start.4 = (bf16[320,2048]{1,0:T(8,128)(2,1)}, bf16[320,2048]{1,0:T(8,128)(2,1)}, u32[]{:S(2)}, u32[]{:S(2)}) collective-permute-start(bf16[320,2048]{1,0:T(8,128)(2,1)} %collective-permute-done.3), channel_id=1, source_target_pairs={{0,1},{1,0},{2,3},{3,2},{4,5},{5,4},{6,7},{7,6},{8,9},{9,8},{10,11... | collective-permute-start | bytes 3932168 | tf_op jit(solution)/shard_map/ppermute | solution.py:288
  310.2 33.1 %collective-permute-start.5 = (bf16[320,2048]{1,0:T(8,128)(2,1)}, bf16[320,2048]{1,0:T(8,128)(2,1)}, u32[]{:S(2)}, u32[]{:S(2)}) collective-permute-start(bf16[320,2048]{1,0:T(8,128)(2,1)} %collective-permute-done.3), channel_id=1, source_target_pairs={{0,2},{1,3},{2,4},{3,5},{4,6},{5,7},{6,0},{7,1},{8,10},{9,11},{10,... | collective-permute-start | bytes 3932168 | tf_op jit(solution)/shard_map/ppermute | solution.py:277
  318.4 6.0 copy-start.11
  324.4 26.4 %copy-start.2 = (f32[320,2048]{1,0:T(8,128)}, f32[320,2048]{1,0:T(8,128)S(1)}, u32[]{:S(2)}) copy-start(f32[320,2048]{1,0:T(8,128)S(1)} %get-tuple-element.157) | copy-start | bytes 7864324
  324.4 26.4 %copy-start.21 = (f32[320]{0:T(512)}, f32[320]{0:T(512)S(1)}, u32[]{:S(2)}) copy-start(f32[320]{0:T(512)S(1)} %add_rsqrt_fusion.2) | copy-start | bytes 3844
  343.3 6.4 collective-permute-start.6
  510.3 183.7 %reduce-scatter.5.cloned.1.call-start = ((), (), s32[]{:S(2)}) async-start(), calls=%async_computation.7 | async-start | bytes 11796480 | tf_op jit(solution)/shard_map/reduce_scatter | solution.py:827
  568.5 0.9 copy-start.13
  568.5 419.9 %reduce-scatter.9.cloned.1.call-start = ((), (), s32[]{:S(2)}) async-start(), calls=%async_computation.11 | async-start | bytes 11796480 | tf_op jit(solution)/shard_map/reduce_scatter | solution.py:871
  601.5 413.0 %all-reduce.8.cloned.1.call-start = ((), (), s32[]{:S(2)}) async-start(), calls=%async_computation.10 | async-start | bytes 34603008 | tf_op jit(solution)/shard_map/psum | solution.py:686
  672.9 21.1 %copy-start.15 = (f32[1,2,8,128]{3,1,2,0:T(2,128)S(1)}, f32[1,2,8,128]{3,1,2,0:T(2,128)}, u32[]{:S(2)}) copy-start(f32[1,2,8,128]{3,1,2,0:T(2,128)} %copy-done.14) | copy-start | bytes 24580
  672.9 21.1 %copy-start.22 = (f32[320]{0:T(512)S(1)}, f32[320]{0:T(512)}, u32[]{:S(2)}) copy-start(f32[320]{0:T(512)} %copy-done.21) | copy-start | bytes 3844
  700.4 1.5 copy-start.7
  710.5 58.3 %all-to-all-start.1 = ((bf16[320,8,256]{2,0,1:T(8,128)(2,1)}), bf16[320,8,256]{2,0,1:T(8,128)(2,1)S(1)}, u32[]{:S(2)}, u32[]{:S(2)}) async-start(bf16[320,8,256]{2,0,1:T(8,128)(2,1)} %fusion.13), calls=%async_computation.2 | async-start | bytes 2621440 | tf_op jit(solution)/shard_map/all_to_all | solution.py:843
  715.2 299.3 %reduce-scatter.7.cloned.1.call-start = ((), (), s32[]{:S(2)}) async-start(), calls=%async_computation.8 | async-start | bytes 10027008 | tf_op jit(solution)/shard_map/reduce_scatter | solution.py:852
  768.8 7.2 copy-start.8
  780.1 347.6 %all-reduce.10.cloned.1.call-start = ((), (), s32[]{:S(2)}) async-start(), calls=%async_computation.13 | async-start | bytes 8912896 | tf_op jit(solution)/shard_map/psum | solution.py:686
  780.2 13.9 %copy-start.17 = (f32[8,320]{1,0:T(8,128)S(1)}, f32[8,320]{1,0:T(8,128)}, u32[]{:S(2)}) copy-start(f32[8,320]{1,0:T(8,128)} %copy-done.16) | copy-start | bytes 30724
  1014.5 130.6 %reduce-scatter.11.cloned.1.call-start = ((), (), s32[]{:S(2)}) async-start(), calls=%async_computation.12 | async-start | bytes 11796480 | tf_op jit(solution)/shard_map/reduce_scatter | solution.py:876
  1028.4 0.7 copy-start.28
  1028.4 1.3 copy-start.6
  1028.4 11.1 slice-start
  1029.8 9.8 slice-start.1
  1030.1 9.4 slice-start.2
  1052.2 9.4 copy-start.3
  1052.2 9.4 copy-start.10
  1137.1 14.2 %copy-start.1 = (bf16[256,2048]{1,0:T(8,128)(2,1)S(1)}, bf16[256,2048]{1,0:T(8,128)(2,1)}, u32[]{:S(2)}) copy-start(bf16[256,2048]{1,0:T(8,128)(2,1)} %param.24) | copy-start | bytes 3145732
Sparse Core Ops, SparseCore 0:
  510.4 183.4 all-reduce.5
  697.8 316.6 all-reduce.7
  1018.5 109.2 all-reduce.9
Sparse Core Ops, SparseCore 1:
  568.6 112.8 reduce-scatter.4
  684.2 128.7 reduce-scatter.8
  815.7 142.8 reduce-scatter.6
  1028.5 109.9 reduce-scatter.10
